TPU v7x, 512 devices: a whole 4x8x8 slice. The times are simulated.
512 devices in a mesh: rep: 16 (over z, core), tp: 32 (over y, x).
Axes of the slice: x: 4, y: 8, z: 8, core: 2. Of those that a mesh axis runs over, the one named last changes fastest.
Arguments:
- queries: bfloat16 [2048, 4096], P(('rep', 'tp')), parts along dimension 0, may hold values from -18 to 18
- key_cache: bfloat16 [2048, 256, 512], P(('rep', 'tp')), parts along dimension 0, may hold values from -6 to 6
- value_cache: bfloat16 [2048, 256, 512], P(('rep', 'tp')), parts along dimension 0, may hold values from -24 to 24
- lengths: int32 [2048], P(('rep', 'tp')), parts along dimension 0, may hold values from 32 to 256, as said below
- request_adapter: int32 [2048], P('rep'), parts along dimension 0, may hold values from 0 to 199, as said below
- block_adapter: int32 [256], P('rep'), parts along dimension 0, may hold values from 0 to 199, as said below
- output_weight: bfloat16 [4096, 8192], P('tp'), may hold values from -0.1875 to 0.1875
- down_factors: bfloat16 [256, 4096, 64], P('rep', 'tp'), parts along dimension 0, may hold values from -0.09375 to 0.09375
- up_factors: bfloat16 [256, 64, 8192], P('rep', None, 'tp'), parts along dimension 0, may hold values from -0.75 to 0.75
Outputs:
- layer_out: bfloat16 [2048, 8192], P('rep', 'tp'), parts along dimension 0
There are 16 independent parts, one for each index of `rep`. A program takes and returns all parts, laid end to end along the dimension named above; an argument that names none is the same for every part. Nothing has to cross between parts.
Inputs may be any that keep to these rules, and one draw needn't show every extreme that they name: `lengths`: every request has live positions; some request's cache is live at all 256 positions. `block_adapter`: the entries are distinct adapters. `request_adapter`: every request's adapter appears in block_adapter; block b takes the requests whose adapter is block_adapter[b], at most 16 of them, and some block takes exactly 16.
All inputs are finite; a program needn't handle non-finite values.
Results may differ from a plain program's by a relative error of at most 0.006.
Values may be sent and summed in bfloat16 or wider, within the bound.
No kernel may reach another device: no remote copies, remote signals or barrier semaphores. Data moves between devices by JAX's collectives and lax.ppermute only.
A program may use at most 64 MiB of HBM per device.

v0:
```python
import math

import jax
import jax.numpy as jnp
from jax import lax
from jax.sharding import PartitionSpec as P

HEAD_SIZE = 128
QUERY_HEADS = 32
KVH = 4
BLK = 16
CTX = 256


def attend(queries, key_cache, value_cache, lengths):
    row_count = queries.shape[0]
    group_size = QUERY_HEADS // KVH
    query_split = queries.reshape(row_count, KVH, group_size, HEAD_SIZE)
    key_split = key_cache.reshape(row_count, CTX, KVH, HEAD_SIZE)
    value_split = value_cache.reshape(row_count, CTX, KVH, HEAD_SIZE)
    scores = jnp.einsum(
        "rkgd,rpkd->rkgp", query_split, key_split, preferred_element_type=jnp.float32
    ) / math.sqrt(HEAD_SIZE)
    live_keys = (jnp.arange(CTX, dtype=jnp.int32)[None, :] < lengths[:, None])[:, None, None, :]
    scores = jnp.where(live_keys, scores, -1e30)
    row_max = jnp.max(scores, axis=-1, keepdims=True)
    raw_weights = jnp.where(live_keys, jnp.exp(scores - row_max), 0.0)
    weights = (raw_weights / jnp.sum(raw_weights, axis=-1, keepdims=True)).astype(jnp.bfloat16)
    attended = jnp.einsum(
        "rkgp,rpkd->rkgd", weights, value_split, preferred_element_type=jnp.float32
    )
    return attended.reshape(row_count, QUERY_HEADS * HEAD_SIZE).astype(jnp.bfloat16)


def per_block(rows_in, factors, slot_lookup, slot_inverse):
    block_result = factors.shape[0]
    slotted = jnp.dot(slot_lookup, rows_in, preferred_element_type=jnp.float32).astype(jnp.bfloat16)
    slotted = slotted.reshape(block_result, BLK, rows_in.shape[1])
    products = jnp.einsum("bsc,bck->bsk", slotted, factors, preferred_element_type=jnp.float32)
    flat_products = products.reshape(block_result * BLK, factors.shape[2])
    return jnp.dot(slot_inverse, flat_products, precision=lax.Precision.HIGHEST)


def per_device(
    queries,
    key_cache,
    value_cache,
    lengths,
    request_adapter,
    block_adapter,
    output_weight,
    down_factors,
    up_factors,
):
    own_heads = attend(queries, key_cache, value_cache, lengths)
    column_span = lax.all_to_all(own_heads, "tp", split_axis=1, concat_axis=0, tiled=True)
    row_count = column_span.shape[0]
    block_result = down_factors.shape[0]
    slot_total = block_result * BLK
    matches = request_adapter[:, None] == block_adapter[None, :]
    block_of = jnp.sum(
        jnp.where(matches, jnp.arange(block_result, dtype=jnp.int32)[None, :], 0), axis=1
    )
    positions = jnp.arange(row_count, dtype=jnp.int32)
    earlier = (request_adapter[:, None] == request_adapter[None, :]) & (
        positions[None, :] < positions[:, None]
    )
    slot_of = block_of * BLK + jnp.sum(earlier.astype(jnp.int32), axis=1)
    slot_hits = jnp.arange(slot_total, dtype=jnp.int32)[:, None] == slot_of[None, :]
    slot_lookup = slot_hits.astype(jnp.bfloat16)
    slot_inverse = slot_hits.T.astype(jnp.float32)
    partial_downward = per_block(column_span, down_factors, slot_lookup, slot_inverse)
    shrink_total = lax.psum(partial_downward, "tp")
    local_base = lax.psum_scatter(
        lax.dot_general(
            output_weight, column_span, (((0,), (1,)), ((), ())), preferred_element_type=jnp.float32
        ),
        "tp",
        scatter_dimension=0,
        tiled=True,
    ).T
    reduced_activations = shrink_total.astype(jnp.bfloat16)
    local_adapter = per_block(reduced_activations, up_factors, slot_lookup, slot_inverse)
    return (local_base + local_adapter).astype(jnp.bfloat16)


def solution(mesh):
    in_specs = (
        P(("rep", "tp"), None),
        P(("rep", "tp"), None, None),
        P(("rep", "tp"), None, None),
        P(("rep", "tp")),
        P("rep"),
        P("rep"),
        P("tp", None),
        P("rep", "tp", None),
        P("rep", None, "tp"),
    )
    out_specs = P("rep", "tp")
    return jax.shard_map(
        per_device, mesh=mesh, in_specs=in_specs, out_specs=out_specs, check_vma=False
    )
```

profile of v0, /device:TPU:1, one launch (start us, length us, event | category | flops | bytes accessed | tf_op | source)
XLA Modules:
  0.0 262.2 jit_solution(4616087115004960908)
XLA Ops:
  6.5 0.0 copy-start
  6.5 0.0 reduce-scatter.2.cloned.1.call-start
  6.5 0.9 iota_compare_fusion.6
  7.4 1.8 fusion.21
  9.2 1.5 fusion.6
  10.8 19.0 %all_to_all.16 = bf16[4,32,128]{2,0,1:T(4,128)(2,1)S(1)} all-to-all(bf16[4,32,128]{2,0,1:T(4,128)(2,1)S(1)} %copy.19), channel_id=1, replica_groups=mesh['rep'=16,'tp'=32] {'tp'}, dimensions={1} | all-to-all | bytes 65536 | tf_op jit(solution)/shard_map/all_to_all | solution.py:56
  29.8 0.0 copy-done
  29.8 2.6 %convolution_bitcast_fusion = f32[8192,128]{0,1:T(8,128)} fusion(bf16[128,128]{1,0:T(8,128)(2,1)S(1)} %bitcast.49, bf16[128,8192]{1,0:T(8,128)(2,1)S(1)} %copy-done), kind=kOutput, calls=%fused_computation.1 | convolution fusion | flops 268435456 | bytes 6324224 | tf_op jit(solution)/shard_map/dot_general | solution.py:75
  32.4 0.0 copy-start.3
  32.4 0.0 copy-start.4
  32.4 0.0 copy-start.2
  32.4 0.0 copy-start.1
  32.4 0.0 reduce-scatter.2.cloned.1.call-update
  32.4 0.6 copy-done.3
  33.1 0.0 copy-done.4
  33.1 0.1 select_reduce_fusion
  33.2 0.2 convert_reduce_fusion
  33.3 0.2 convolution_convert_fusion
  33.5 0.0 copy-done.2
  33.5 0.2 fusion.26
  33.8 0.3 fusion.11
  34.0 111.8 %psum.7 = bf16[128,64]{0,1:T(8,128)(2,1)S(1)} all-reduce(f32[128,64]{0,1:T(8,128)S(1)} %fusion.11), channel_id=1, replica_groups=mesh['rep'=16,'tp'=32] {'tp'}, use_global_device_ids=true, to_apply=%region_5.6 | all-reduce | flops 8192 | bytes 49152 | tf_op jit(solution)/shard_map/psum | solution.py:73
  145.8 0.1 convolution_convert_fusion.1
  146.0 0.1 copy.20
  146.1 0.0 copy-done.1
  146.1 0.2 fusion.27
  146.3 107.2 %reduce-scatter.2.cloned.1.call-done = f32[256,128]{0,1:T(8,128)} async-done(((f32[8192,128]{0,1:T(8,128)}), f32[256,128]{0,1:T(8,128)}) %reduce-scatter.2.cloned.1.call-update) | async-done | bytes 131088 | tf_op jit(solution)/shard_map/reduce_scatter | solution.py:74
  253.6 1.8 fusion.5
  (2 shorter events, 0.0 us)
Async XLA Ops:
  6.5 23.2 %copy-start = (bf16[128,8192]{1,0:T(8,128)(2,1)S(1)}, bf16[128,8192]{1,0:T(8,128)(2,1)}, u32[]{:S(2)}) copy-start(bf16[128,8192]{1,0:T(8,128)(2,1)} %param.15) | copy-start | bytes 6291460
  6.5 247.0 %reduce-scatter.2.cloned.1.call-start = ((), (), s32[]{:S(2)}) async-start(), calls=%async_computation.2 | async-start | bytes 4325376 | tf_op jit(solution)/shard_map/reduce_scatter | solution.py:74
  32.4 0.7 copy-start.3
  32.4 0.7 copy-start.4
  32.4 1.1 copy-start.2
  32.4 113.7 %copy-start.1 = (bf16[16,64,256]{2,1,0:T(8,128)(2,1)S(1)}, bf16[16,64,256]{2,1,0:T(8,128)(2,1)}, u32[]{:S(2)}) copy-start(bf16[16,64,256]{2,1,0:T(8,128)(2,1)} %param.17) | copy-start | bytes 1572868
Sparse Core Ops, SparseCore 0:
  32.6 220.9 reduce-scatter.1
where the time goes:
time: 266 us; the launch traced here: 262 us
  blocking collectives  131 us (49%)
  waiting for transfers between devices  107 us (40%)
  between operations  13.4 us (5%)
  matrix products  8.79 us (3%)
    psum x1, blocking collectives, per_device(): shrink_total = lax.psum(partial_downward, 'tp')  112 us
    reduce_scatter x1, waiting for transfers between devices, per_device(): lax.psum_scatter(lax.dot_general(output_weight, column_span, (((0,), (1,)...  107 us
    all_to_all x1, blocking collectives, per_device(): lax.all_to_all(own_heads, 'tp', split_axis=1, concat_axis=0, tiled=True)  19 us
  transfers between devices with their start and end apart: 1, of which 1 were waited for; matrix products, arithmetic and copies ran while one was open for 1% of the time, Pallas kernels for 0%

commit v1 on v0

v1 whole, which is shorter than its diff:
```python
import functools
import math

import jax
import jax.numpy as jnp
from jax import lax
from jax.experimental import pallas as pl
from jax.experimental.pallas import tpu as pltpu
from jax.sharding import PartitionSpec as P

HEAD_SIZE = 128
QUERY_HEADS = 32
KVH = 4
CTX = 256
BF16, F32 = jnp.bfloat16, jnp.float32
VMEM_LIMIT = 32 * 1024 * 1024


def attend_kernel(len_ref, q_ref, k_hbm, v_hbm, out_ref, k_buf, v_buf, k_sem, v_sem):
    rows = q_ref.shape[0]
    group = QUERY_HEADS // KVH
    k_copies = [pltpu.make_async_copy(k_hbm.at[r], k_buf.at[r], k_sem.at[r]) for r in range(rows)]
    v_copies = [pltpu.make_async_copy(v_hbm.at[r], v_buf.at[r], v_sem.at[r]) for r in range(rows)]
    for r in range(rows):
        k_copies[r].start()
        v_copies[r].start()
    head_row = lax.broadcasted_iota(jnp.int32, (QUERY_HEADS, HEAD_SIZE), 0) // group
    position = lax.broadcasted_iota(jnp.int32, (QUERY_HEADS, CTX), 1)
    for r in range(rows):
        q = q_ref[r]
        spread = jnp.concatenate(
            [jnp.where(head_row == k, q, jnp.zeros_like(q)) for k in range(KVH)], axis=1
        )
        k_copies[r].wait()
        scores = lax.dot_general(
            spread, k_buf[r], (((1,), (1,)), ((), ())), preferred_element_type=F32
        ) * (1.0 / math.sqrt(HEAD_SIZE))
        live = position < len_ref[r]
        scores = jnp.where(live, scores, -1e30)
        raw = jnp.where(live, jnp.exp(scores - jnp.max(scores, axis=1, keepdims=True)), 0.0)
        probs = (raw / jnp.sum(raw, axis=1, keepdims=True)).astype(BF16)
        v_copies[r].wait()
        wide = jnp.dot(probs, v_buf[r], preferred_element_type=F32)
        out_ref[r] = jnp.concatenate(
            [
                wide[k * group : (k + 1) * group, k * HEAD_SIZE : (k + 1) * HEAD_SIZE]
                for k in range(KVH)
            ],
            axis=0,
        ).astype(BF16)


def attend(queries, key_cache, value_cache, lengths):
    rows = queries.shape[0]
    return pl.pallas_call(
        attend_kernel,
        out_shape=jax.ShapeDtypeStruct((rows, QUERY_HEADS, HEAD_SIZE), BF16),
        in_specs=[
            pl.BlockSpec(memory_space=pltpu.SMEM),
            pl.BlockSpec(memory_space=pltpu.VMEM),
            pl.BlockSpec(memory_space=pl.ANY),
            pl.BlockSpec(memory_space=pl.ANY),
        ],
        out_specs=pl.BlockSpec(memory_space=pltpu.VMEM),
        scratch_shapes=[
            pltpu.VMEM((rows, CTX, KVH * HEAD_SIZE), BF16),
            pltpu.VMEM((rows, CTX, KVH * HEAD_SIZE), BF16),
            pltpu.SemaphoreType.DMA((rows,)),
            pltpu.SemaphoreType.DMA((rows,)),
        ],
        compiler_params=pltpu.CompilerParams(vmem_limit_bytes=VMEM_LIMIT),
        name="attend",
    )(lengths, queries.reshape(rows, QUERY_HEADS, HEAD_SIZE), key_cache, value_cache)


def project_kernel(block_ref, adapter_ref, heads_ref, weight_ref, down_ref, out_ref):
    devices, _, width = out_ref.shape
    rows = heads_ref.shape[0]
    heads = heads_ref[...]
    adapter = adapter_ref[...]
    for d in range(devices):
        out_ref[d, :rows, :] = jnp.dot(
            heads, weight_ref[:, d * width : (d + 1) * width], preferred_element_type=F32
        ).astype(BF16)
    shrink = jnp.zeros((rows, down_ref.shape[2]), F32)
    for b in range(down_ref.shape[0]):
        mine = jnp.where(adapter == block_ref[b], heads, jnp.zeros_like(heads))
        shrink += jnp.dot(mine, down_ref[b], preferred_element_type=F32)
    quarter = rows * shrink.shape[1] // width
    packed = jnp.concatenate(
        [shrink[i * quarter : (i + 1) * quarter] for i in range(rows // quarter)], axis=1
    ).astype(BF16)
    for d in range(devices):
        out_ref[d, rows:, :] = packed


def project(heads, weight, down, adapter_col, block_adapter, devices):
    rows = heads.shape[0]
    width = weight.shape[1] // devices
    extra = rows * down.shape[2] // width
    vmem = pl.BlockSpec(memory_space=pltpu.VMEM)
    return pl.pallas_call(
        project_kernel,
        out_shape=jax.ShapeDtypeStruct((devices, rows + extra, width), BF16),
        in_specs=[pl.BlockSpec(memory_space=pltpu.SMEM)] + [vmem] * 4,
        out_specs=vmem,
        compiler_params=pltpu.CompilerParams(vmem_limit_bytes=VMEM_LIMIT),
        name="project",
    )(block_adapter, adapter_col, heads, weight, down)


def finish_kernel(block_ref, adapter_ref, parts_ref, up_ref, out_ref):
    count = parts_ref.shape[0]
    rows, width = out_ref.shape
    blocks, rank, _ = up_ref.shape
    packed = parts_ref[0, rows:, :].astype(F32)
    for s in range(1, count):
        packed += parts_ref[s, rows:, :].astype(F32)
    low_rank = jnp.concatenate(
        [packed[:, i * rank : (i + 1) * rank] for i in range(width // rank)], axis=0
    ).astype(BF16)
    adapter = adapter_ref[...]
    spread = jnp.concatenate(
        [
            jnp.where(adapter == block_ref[b], low_rank, jnp.zeros_like(low_rank))
            for b in range(blocks)
        ],
        axis=1,
    )
    lora = jnp.dot(
        spread, up_ref[...].reshape(blocks * rank, width), preferred_element_type=F32
    )
    step = 32
    for i in range(0, rows, step):
        total = parts_ref[0, i : i + step, :].astype(F32)
        for s in range(1, count):
            total += parts_ref[s, i : i + step, :].astype(F32)
        out_ref[i : i + step, :] = (total + lora[i : i + step]).astype(BF16)


def finish(parts, up, adapter_col, block_adapter, rows):
    width = parts.shape[2]
    vmem = pl.BlockSpec(memory_space=pltpu.VMEM)
    return pl.pallas_call(
        finish_kernel,
        out_shape=jax.ShapeDtypeStruct((rows, width), BF16),
        in_specs=[pl.BlockSpec(memory_space=pltpu.SMEM)] + [vmem] * 3,
        out_specs=vmem,
        compiler_params=pltpu.CompilerParams(vmem_limit_bytes=VMEM_LIMIT),
        name="finish",
    )(block_adapter, adapter_col, parts, up)


def per_device(
    devices,
    queries,
    key_cache,
    value_cache,
    lengths,
    request_adapter,
    block_adapter,
    output_weight,
    down_factors,
    up_factors,
):
    adapter_col = request_adapter[:, None]
    rows = request_adapter.shape[0]
    own = attend(queries, key_cache, value_cache, lengths)
    heads = lax.all_to_all(own, "tp", split_axis=1, concat_axis=0, tiled=True)
    heads = heads.reshape(rows, HEAD_SIZE)
    parts = project(heads, output_weight, down_factors, adapter_col, block_adapter, devices)
    parts = lax.all_to_all(parts, "tp", split_axis=0, concat_axis=0, tiled=True)
    return finish(parts, up_factors, adapter_col, block_adapter, rows)


def solution(mesh):
    in_specs = (
        P(("rep", "tp"), None),
        P(("rep", "tp"), None, None),
        P(("rep", "tp"), None, None),
        P(("rep", "tp")),
        P("rep"),
        P("rep"),
        P("tp", None),
        P("rep", "tp", None),
        P("rep", None, "tp"),
    )
    return jax.shard_map(
        functools.partial(per_device, mesh.shape["tp"]),
        mesh=mesh,
        in_specs=in_specs,
        out_specs=P("rep", "tp"),
        check_vma=False,
    )
```

time: 266 us -> 96.2 us (0.36)
  the two profiles are of different devices: /device:TPU:1 before, /device:TPU:128 now
where the time goes in v1:
time: 96.2 us; the launch traced here: 95.9 us
  blocking collectives  64.7 us (67%)
  starting transfers between devices  9.95 us (10%)
  waiting for transfers between devices  7.85 us (8%)
  Pallas kernels  6.7 us (7%)
  local copies, waits for them, and re-layouts  6.65 us (7%)
    all_to_all x1, blocking collectives, per_device(): parts = lax.all_to_all(parts, 'tp', split_axis=0, concat_axis=0, tiled=True)  64.7 us
    all_to_all x1, starting transfers between devices, per_device(): heads = lax.all_to_all(own, 'tp', split_axis=1, concat_axis=0, tiled=True)  9.95 us
    all_to_all x1, waiting for transfers between devices, per_device(): heads = lax.all_to_all(own, 'tp', split_axis=1, concat_axis=0, tiled=True)  7.85 us
    unnamed x14, local copies, waits for them, and re-layouts  5.25 us
    pallas_call x1, Pallas kernels, attend(): pl.pallas_call(attend_kernel, out_shape=jax.ShapeDtypeStruct((rows, QUERY...  3.23 us
    pallas_call x1, Pallas kernels, finish(): pl.pallas_call(finish_kernel, out_shape=jax.ShapeDtypeStruct((rows, width...  1.96 us
  transfers between devices with their start and end apart: 1, of which 1 were waited for; matrix products, arithmetic and copies ran while one was open for 2% of the time, Pallas kernels for 0%

profile of v1, /device:TPU:128, one launch (start us, length us, event | category | flops | bytes accessed | tf_op | source)
XLA Modules:
  0.0 95.9 jit_solution(4856673281679515676)
XLA Ops:
  0.0 0.0 copy-start
  0.0 0.9 copy.20
  0.9 0.0 copy-start.1
  0.9 1.2 %copy-done.1 = bf16[4,256,512]{2,1,0:T(8,128)(2,1)S(1)} copy-done((bf16[4,256,512]{2,1,0:T(8,128)(2,1)S(1)}, bf16[4,256,512]{2,1,0:T(8,128)(2,1)}, u32[]{:S(2)}) %copy-start.1) | copy-done | bytes 1048600
  2.1 0.0 copy-start.2
  2.1 1.2 %copy-done.2 = bf16[4,256,512]{2,1,0:T(8,128)(2,1)S(1)} copy-done((bf16[4,256,512]{2,1,0:T(8,128)(2,1)S(1)}, bf16[4,256,512]{2,1,0:T(8,128)(2,1)}, u32[]{:S(2)}) %copy-start.2) | copy-done | bytes 1048600
  3.4 0.0 copy-start.5
  3.4 0.7 copy-done.5
  4.0 0.0 copy-start.4
  4.0 3.2 %attend.1 = bf16[4,32,128]{2,1,0:T(8,128)(2,1)S(1)} custom-call(s32[4]{0:T(128)S(1)} %copy-done.5, bf16[4,32,128]{2,1,0:T(8,128)(2,1)S(1)} %bitcast.11, bf16[4,256,512]{2,1,0:T(8,128)(2,1)S(1)} %copy-done.1, bf16[4,256,512]{2,1,0:T(8,128)(2,1)S(1)} %copy-done.2), custom_call_target="tpu_custom_call" | custom-call | tf_op jit(solution)/shard_map/attend/pallas_call | solution.py:55
  7.3 0.6 copy.14
  7.9 9.9 %all-to-all-start = ((bf16[4,32,128]{2,0,1:T(4,128)(2,1)}), bf16[4,32,128]{2,0,1:T(4,128)(2,1)S(1)}, u32[]{:S(2)}, u32[]{:S(2)}) async-start(bf16[4,32,128]{2,0,1:T(4,128)(2,1)} %copy.14), calls=%async_computation | async-start | bytes 65536 | tf_op jit(solution)/shard_map/all_to_all | solution.py:169
  17.9 0.8 copy.17.adapter_ref
  18.6 1.2 %copy.16.down_ref = bf16[16,128,64]{2,1,0:T(8,128)(2,1)S(1)} copy(bf16[16,128,64]{1,2,0:T(8,128)(2,1)} %param.16) | data formatting | bytes 524288 | tf_op args[7]
  19.8 7.9 %all-to-all-done = bf16[4,32,128]{2,0,1:T(4,128)(2,1)S(1)} async-done(((bf16[4,32,128]{2,0,1:T(4,128)(2,1)}), bf16[4,32,128]{2,0,1:T(4,128)(2,1)S(1)}, u32[]{:S(2)}, u32[]{:S(2)}) %all-to-all-start) | async-done | bytes 32800 | tf_op jit(solution)/shard_map/all_to_all | solution.py:169
  27.7 0.0 copy-done
  27.7 0.0 copy-done.4
  27.7 1.5 %project.1 = bf16[32,160,256]{2,1,0:T(8,128)(2,1)S(1)} custom-call(s32[16]{0:T(128)S(1)} %copy-done.4, s32[128,1]{1,0:T(8,128)S(1)} %copy.17.adapter_ref, bf16[128,128]{1,0:T(8,128)(2,1)S(1)} %bitcast.10, bf16[128,8192]{1,0:T(8,128)(2,1)S(1)} %copy-done, bf16[16,128,64]{2,1,0:T(8,128)(2,1)S(1)} %copy.16.down_ref), custom_call_target="tpu_custom_call" | custom-call | tf_op jit(solution)/shard_map/project/pallas_call | solution.py:102
  29.2 0.0 copy-start.3
  29.2 64.7 %all_to_all.20.parts_ref = bf16[32,160,256]{2,1,0:T(8,128)(2,1)S(1)} all-to-all(bf16[32,160,256]{2,1,0:T(8,128)(2,1)S(1)} %project.1), channel_id=1, replica_groups=mesh['rep'=16,'tp'=32] {'tp'}, dimensions={0} | all-to-all | bytes 5242880 | tf_op jit(solution)/shard_map/all_to_all | solution.py:172
  93.9 0.0 copy-done.3
  93.9 2.0 %finish.1 = bf16[128,256]{1,0:T(8,128)(2,1)} custom-call(s32[16]{0:T(128)S(1)} %copy-done.4, s32[128,1]{1,0:T(8,128)S(1)} %copy.17.adapter_ref, bf16[32,160,256]{2,1,0:T(8,128)(2,1)S(1)} %all_to_all.20.parts_ref, bf16[16,64,256]{2,1,0:T(8,128)(2,1)S(1)} %copy-done.3), custom_call_target="tpu_custom_call" | custom-call | tf_op jit(solution)/shard_map/finish/pallas_call | solution.py:144
Async XLA Ops:
  0.0 27.7 %copy-start = (bf16[128,8192]{1,0:T(8,128)(2,1)S(1)}, bf16[128,8192]{1,0:T(8,128)(2,1)}, u32[]{:S(2)}) copy-start(bf16[128,8192]{1,0:T(8,128)(2,1)} %weight_ref.1) | copy-start | bytes 6291460
  0.9 1.2 %copy-start.1 = (bf16[4,256,512]{2,1,0:T(8,128)(2,1)S(1)}, bf16[4,256,512]{2,1,0:T(8,128)(2,1)}, u32[]{:S(2)}) copy-start(bf16[4,256,512]{2,1,0:T(8,128)(2,1)} %k_hbm.1) | copy-start | bytes 3145732
  2.1 1.2 %copy-start.2 = (bf16[4,256,512]{2,1,0:T(8,128)(2,1)S(1)}, bf16[4,256,512]{2,1,0:T(8,128)(2,1)}, u32[]{:S(2)}) copy-start(bf16[4,256,512]{2,1,0:T(8,128)(2,1)} %v_hbm.1) | copy-start | bytes 3145732
  3.4 0.7 copy-start.5
  4.0 23.7 %copy-start.4 = (s32[16]{0:T(128)S(1)}, s32[16]{0:T(128)}, u32[]{:S(2)}) copy-start(s32[16]{0:T(128)} %block_ref.3) | copy-start | bytes 196
  7.9 19.8 %all-to-all-start = ((bf16[4,32,128]{2,0,1:T(4,128)(2,1)}), bf16[4,32,128]{2,0,1:T(4,128)(2,1)S(1)}, u32[]{:S(2)}, u32[]{:S(2)}) async-start(bf16[4,32,128]{2,0,1:T(4,128)(2,1)} %copy.14), calls=%async_computation | async-start | bytes 65536 | tf_op jit(solution)/shard_map/all_to_all | solution.py:169
  29.2 64.7 %copy-start.3 = (bf16[16,64,256]{2,1,0:T(8,128)(2,1)S(1)}, bf16[16,64,256]{2,1,0:T(8,128)(2,1)}, u32[]{:S(2)}) copy-start(bf16[16,64,256]{2,1,0:T(8,128)(2,1)} %up_ref.1) | copy-start | bytes 1572868

commit v2 on v1

v2 whole, which is shorter than its diff:
```python
import functools
import math

import jax
import jax.numpy as jnp
from jax import lax
from jax.experimental import pallas as pl
from jax.experimental.pallas import tpu as pltpu
from jax.sharding import PartitionSpec as P

HEAD_SIZE = 128
QUERY_HEADS = 32
KVH = 4
CTX = 256
QUAD = 4
LINE = 256
BF16, F32 = jnp.bfloat16, jnp.float32
VMEM = pl.BlockSpec(memory_space=pltpu.VMEM)
SMEM = pl.BlockSpec(memory_space=pltpu.SMEM)
HBM = pl.BlockSpec(memory_space=pl.ANY)
PARAMS = pltpu.CompilerParams(vmem_limit_bytes=32 * 1024 * 1024)


def regroup_kernel(quad_ref, weight_hbm, *refs):
    outs, sem = refs[:QUAD], refs[QUAD]
    lines = outs[0].shape[1] // LINE
    copies = []
    for ahead, out_ref in enumerate(outs):
        x = lax.rem(quad_ref[0] + ahead, QUAD)
        for y in range(lines):
            start = pl.multiple_of((y * QUAD + x) * LINE, LINE)
            copies.append(
                pltpu.make_async_copy(
                    weight_hbm.at[:, pl.ds(start, LINE)],
                    out_ref.at[:, pl.ds(y * LINE, LINE)],
                    sem.at[ahead, y],
                )
            )
    for copy in copies:
        copy.start()
    for copy in copies:
        copy.wait()


def regroup(quad, weight):
    depth, columns = weight.shape
    piece = jax.ShapeDtypeStruct((depth, columns // QUAD), BF16)
    return pl.pallas_call(
        regroup_kernel,
        out_shape=(piece,) * QUAD,
        in_specs=[SMEM, HBM],
        out_specs=(VMEM,) * QUAD,
        scratch_shapes=[pltpu.SemaphoreType.DMA((QUAD, columns // QUAD // LINE))],
        compiler_params=PARAMS,
        name="regroup",
    )(quad, weight)


def attend_kernel(len_ref, q_ref, k_ref, v_ref, out_ref):
    rows = q_ref.shape[0]
    group = QUERY_HEADS // KVH
    head_row = lax.broadcasted_iota(jnp.int32, (QUERY_HEADS, HEAD_SIZE), 0) // group
    position = lax.broadcasted_iota(jnp.int32, (QUERY_HEADS, CTX), 1)
    attended = []
    for r in range(rows):
        q = q_ref[r]
        spread = jnp.concatenate(
            [jnp.where(head_row == k, q, jnp.zeros_like(q)) for k in range(KVH)], axis=1
        )
        scores = lax.dot_general(
            spread, k_ref[r], (((1,), (1,)), ((), ())), preferred_element_type=F32
        ) * (1.0 / math.sqrt(HEAD_SIZE))
        live = position < len_ref[r]
        scores = jnp.where(live, scores, -1e30)
        raw = jnp.where(live, jnp.exp(scores - jnp.max(scores, axis=1, keepdims=True)), 0.0)
        probs = (raw / jnp.sum(raw, axis=1, keepdims=True)).astype(BF16)
        wide = jnp.dot(probs, v_ref[r], preferred_element_type=F32)
        attended.append(
            jnp.concatenate(
                [
                    wide[k * group : (k + 1) * group, k * HEAD_SIZE : (k + 1) * HEAD_SIZE]
                    for k in range(KVH)
                ],
                axis=0,
            )
        )
    stacked = jnp.stack(attended, axis=1)
    for y in range(QUERY_HEADS // QUAD):
        piece = stacked[y * QUAD : (y + 1) * QUAD].reshape(QUAD * rows, HEAD_SIZE).astype(BF16)
        for x in range(QUAD):
            out_ref[y * QUAD + x] = piece


def attend(queries, key_cache, value_cache, lengths):
    rows = queries.shape[0]
    return pl.pallas_call(
        attend_kernel,
        out_shape=jax.ShapeDtypeStruct((QUERY_HEADS, QUAD * rows, HEAD_SIZE), BF16),
        in_specs=[SMEM, VMEM, VMEM, VMEM],
        out_specs=VMEM,
        compiler_params=PARAMS,
        name="attend",
    )(lengths, queries.reshape(rows, QUERY_HEADS, HEAD_SIZE), key_cache, value_cache)


def pick_rows(spans, index):
    count, size = spans.shape
    rows = count // QUAD
    row = lax.broadcasted_iota(jnp.int32, (rows, count), 0)
    column = lax.broadcasted_iota(jnp.int32, (rows, count), 1)
    wanted = (row // 4) * 16 + index * 4 + row % 4
    choice = jnp.where(column == wanted, 1.0, 0.0).astype(BF16)
    return jnp.dot(choice, spans, preferred_element_type=F32).astype(BF16)


def shrink_kernel(quad_ref, block_ref, adapter_ref, spans_ref, down_ref, out_ref):
    devices, half, _ = out_ref.shape
    heads = pick_rows(spans_ref[...], quad_ref[0])
    adapter = adapter_ref[...]
    rank = down_ref.shape[1]
    shrink = jnp.zeros((heads.shape[0], rank), F32)
    for b in range(down_ref.shape[0]):
        mine = jnp.where(adapter == block_ref[b], heads, jnp.zeros_like(heads))
        shrink += lax.dot_general(
            mine, down_ref[b], (((1,), (1,)), ((), ())), preferred_element_type=F32
        )
    for y in range(devices // QUAD):
        base = y * 2 * half
        pair = jnp.concatenate(
            [shrink[base : base + half], shrink[base + half : base + 2 * half]], axis=1
        ).astype(BF16)
        for x in range(QUAD):
            out_ref[y * QUAD + x] = pair


def shrink_parts(quad, spans, down, adapter_col, block_adapter):
    devices = spans.shape[0] // (QUAD * 4)
    rows = spans.shape[0] // QUAD
    half = rows // (devices // QUAD) // 2
    return pl.pallas_call(
        shrink_kernel,
        out_shape=jax.ShapeDtypeStruct((devices, half, 2 * down.shape[2]), BF16),
        in_specs=[SMEM, SMEM, VMEM, VMEM, VMEM],
        out_specs=VMEM,
        compiler_params=PARAMS,
        name="shrink",
    )(quad, block_adapter, adapter_col, spans, jnp.swapaxes(down, 1, 2))


def project_kernel(quad_ref, spans_ref, *refs):
    weight_refs, shrink_ref, out_ref = refs[:QUAD], refs[QUAD], refs[QUAD + 1]
    dests, _, width = out_ref.shape
    rows = spans_ref.shape[0] // QUAD
    spans = spans_ref[...]
    heads = jnp.concatenate(
        [pick_rows(spans, lax.rem(quad_ref[0] + QUAD - ahead, QUAD)) for ahead in range(QUAD)],
        axis=1,
    )
    for d in range(dests):
        columns = jnp.concatenate(
            [ref[:, d * width : (d + 1) * width] for ref in weight_refs], axis=0
        )
        out_ref[d, :rows, :] = jnp.dot(heads, columns, preferred_element_type=F32).astype(BF16)
    low_rank = shrink_ref[0].astype(F32)
    for s in range(1, shrink_ref.shape[0]):
        low_rank += shrink_ref[s].astype(F32)
    wide = jnp.concatenate([low_rank, jnp.zeros_like(low_rank)], axis=1)
    block = jnp.concatenate([wide, jnp.zeros_like(wide)], axis=0).astype(BF16)
    for d in range(dests):
        out_ref[d, rows:, :] = block


def project(quad, spans, weights, shrinks):
    rows = spans.shape[0] // QUAD
    dests = weights[0].shape[1] // LINE
    return pl.pallas_call(
        project_kernel,
        out_shape=jax.ShapeDtypeStruct((dests, rows + 2 * shrinks.shape[1], LINE), BF16),
        in_specs=[SMEM] + [VMEM] * (QUAD + 2),
        out_specs=VMEM,
        compiler_params=PARAMS,
        name="project",
    )(quad, spans, *weights, shrinks)


def finish_kernel(block_ref, adapter_ref, parts_ref, up_ref, out_ref):
    count = parts_ref.shape[0]
    rows, width = out_ref.shape
    blocks, rank, _ = up_ref.shape
    lanes = 2 * rank
    half = rows // count // 2
    left = lax.broadcasted_iota(jnp.int32, (half, lanes), 1) < rank
    pieces = []
    for s in range(count):
        pair = parts_ref[s, rows : rows + 2 * half, :lanes].astype(F32)[:half]
        turned = jnp.concatenate([pair[:, rank:], pair[:, :rank]], axis=1)
        pieces += [jnp.where(left, pair, turned), jnp.where(left, turned, pair)]
    low_rank = jnp.concatenate(pieces, axis=0)
    adapter = adapter_ref[...]
    wide_left = lax.broadcasted_iota(jnp.int32, (rows, lanes), 1) < rank
    spread = []
    for b in range(0, blocks, 2):
        match = jnp.where(wide_left, block_ref[b], block_ref[b + 1]) == adapter
        spread.append(jnp.where(match, low_rank, 0.0).astype(BF16))
    lora = jnp.dot(
        jnp.concatenate(spread, axis=1),
        up_ref[...].reshape(blocks * rank, width),
        preferred_element_type=F32,
    )
    total = parts_ref[0, :rows, :].astype(F32)
    for s in range(1, count):
        total += parts_ref[s, :rows, :].astype(F32)
    out_ref[...] = (total + lora).astype(BF16)


def finish(parts, up, adapter_col, block_adapter, rows):
    return pl.pallas_call(
        finish_kernel,
        out_shape=jax.ShapeDtypeStruct((rows, parts.shape[2]), BF16),
        in_specs=[SMEM, VMEM, VMEM, VMEM],
        out_specs=VMEM,
        compiler_params=PARAMS,
        name="finish",
    )(block_adapter, adapter_col, parts, up)


def per_device(
    devices,
    queries,
    key_cache,
    value_cache,
    lengths,
    request_adapter,
    block_adapter,
    output_weight,
    down_factors,
    up_factors,
):
    lines = devices // QUAD
    along_y = [[y * QUAD + x for y in range(lines)] for x in range(QUAD)]
    exchange = functools.partial(
        lax.all_to_all, axis_name="tp", split_axis=0, concat_axis=0, tiled=True
    )
    rows = request_adapter.shape[0]
    adapter_col = request_adapter[:, None]
    quad = (lax.axis_index("tp") & (QUAD - 1)).astype(jnp.int32)[None]

    weights = list(regroup(quad, output_weight))
    for ahead in range(1, QUAD):
        turn = [
            (y * QUAD + x, y * QUAD + (x + ahead) % QUAD) for y in range(lines) for x in range(QUAD)
        ]
        weights[ahead] = lax.ppermute(weights[ahead], "tp", turn)
    spans = exchange(attend(queries, key_cache, value_cache, lengths))
    spans = spans.reshape(QUAD * rows, HEAD_SIZE)
    shrinks = exchange(shrink_parts(quad, spans, down_factors, adapter_col, block_adapter))
    parts = exchange(project(quad, spans, weights, shrinks), axis_index_groups=along_y)
    return finish(parts, up_factors, adapter_col, block_adapter, rows)


def solution(mesh):
    in_specs = (
        P(("rep", "tp"), None),
        P(("rep", "tp"), None, None),
        P(("rep", "tp"), None, None),
        P(("rep", "tp")),
        P("rep"),
        P("rep"),
        P("tp", None),
        P("rep", "tp", None),
        P("rep", None, "tp"),
    )
    return jax.shard_map(
        functools.partial(per_device, mesh.shape["tp"]),
        mesh=mesh,
        in_specs=in_specs,
        out_specs=P("rep", "tp"),
        check_vma=False,
    )
```

time: 96.2 us -> 78.9 us (0.82)
  the two profiles are of different devices: /device:TPU:128 before, /device:TPU:320 now
where the time goes in v2:
time: 78.9 us; the launch traced here: 78.5 us
  blocking collectives  38.4 us (49%)
  starting transfers between devices  18.9 us (24%)
  waiting for transfers between devices  10.5 us (13%)
  Pallas kernels  8.06 us (10%)
  local copies, waits for them, and re-layouts  2.51 us (3%)
    all_to_all x1, blocking collectives, per_device(): exchange(project(quad, spans, weights, shrinks), axis_index_groups=along_y)  19.9 us
    all_to_all x1, blocking collectives, per_device(): exchange(shrink_parts(quad, spans, down_factors, adapter_col, block_adapt...  18.5 us
    ppermute x3, starting transfers between devices, per_device(): weights[ahead] = lax.ppermute(weights[ahead], 'tp', turn)  11.4 us
    all_to_all x1, waiting for transfers between devices, per_device(): spans = exchange(attend(queries, key_cache, value_cache, lengths))  10.5 us
    all_to_all x1, starting transfers between devices, per_device(): spans = exchange(attend(queries, key_cache, value_cache, lengths))  7.52 us
    pallas_call x1, Pallas kernels, attend(): pl.pallas_call(attend_kernel, out_shape=jax.ShapeDtypeStruct((QUERY_HEADS...  3.15 us
    unnamed x17, local copies, waits for them, and re-layouts  2.4 us
    pallas_call x1, Pallas kernels, regroup(): pl.pallas_call(regroup_kernel, out_shape=(piece,) * QUAD, in_specs=[SMEM,...  1.69 us
  transfers between devices with their start and end apart: 4, of which 1 were waited for; matrix products, arithmetic and copies ran while one was open for 1% of the time, Pallas kernels for 5%

profile of v2, /device:TPU:320, one launch (start us, length us, event | category | flops | bytes accessed | tf_op | source)
XLA Modules:
  0.0 78.5 jit_solution(17650870318118438239)
XLA Ops:
  0.0 0.0 copy-start.6
  0.0 0.0 copy-start
  0.0 1.6 %copy-done = bf16[128,8192]{1,0:T(8,128)(2,1)S(1)} copy-done((bf16[128,8192]{1,0:T(8,128)(2,1)S(1)}, bf16[128,8192]{1,0:T(8,128)(2,1)}, u32[]{:S(2)}) %copy-start) | copy-done | bytes 2097176
  1.6 0.0 copy-start.2
  1.6 0.0 copy-start.7
  1.6 0.0 copy-start.4
  1.6 0.0 copy-start.5
  1.6 1.7 %regroup.1 = (bf16[128,2048]{1,0:T(8,128)(2,1)S(1)}, bf16[128,2048]{1,0:T(8,128)(2,1)}, bf16[128,2048]{1,0:T(8,128)(2,1)}, bf16[128,2048]{1,0:T(8,128)(2,1)S(1)}) custom-call(s32[1]{0:T(128)} %bitcast.1.quad_ref, bf16[128,8192]{1,0:T(8,128)(2,1)S(1)} %copy-done), custom_call_target="tpu_custom_call" | custom-call | tf_op jit(solution)/shard_map/regroup/pallas_call | solution.py:48
  3.3 3.4 %collective-permute-start = (bf16[128,2048]{1,0:T(8,128)(2,1)}, bf16[128,2048]{1,0:T(8,128)(2,1)S(1)}, u32[]{:S(2)}, u32[]{:S(2)}) collective-permute-start(bf16[128,2048]{1,0:T(8,128)(2,1)} %get-tuple-element.10), channel_id=1, source_target_pairs={{0,1},{1,2},{2,3},{3,0},{4,5},{5,6},{6,7},{7,4},{8,9},{9,10},{10,1... | collective-permute-start | bytes 1572872 | tf_op jit(solution)/shard_map/ppermute | solution.py:253
  6.7 4.6 %collective-permute-start.1 = (bf16[128,2048]{1,0:T(8,128)(2,1)}, bf16[128,2048]{1,0:T(8,128)(2,1)S(1)}, u32[]{:S(2)}, u32[]{:S(2)}) collective-permute-start(bf16[128,2048]{1,0:T(8,128)(2,1)} %get-tuple-element.11), channel_id=1, source_target_pairs={{0,2},{1,3},{2,0},{3,1},{4,6},{5,7},{6,4},{7,5},{8,10},{9,11},{10,... | collective-permute-start | bytes 1572872 | tf_op jit(solution)/shard_map/ppermute | solution.py:253
  11.4 3.3 %collective-permute-start.2 = (bf16[128,2048]{1,0:T(8,128)(2,1)S(1)}, bf16[128,2048]{1,0:T(8,128)(2,1)S(1)}, u32[]{:S(2)}, u32[]{:S(2)}) collective-permute-start(bf16[128,2048]{1,0:T(8,128)(2,1)S(1)} %get-tuple-element.12), channel_id=1, source_target_pairs={{0,3},{1,0},{2,1},{3,2},{4,7},{5,4},{6,5},{7,6},{8,11},{9,8},{10,9... | collective-permute-start | bytes 1572872 | tf_op jit(solution)/shard_map/ppermute | solution.py:253
  14.7 0.8 copy.14
  15.5 0.0 copy-done.6
  15.5 0.0 copy-done.1
  15.5 0.0 copy-done.2
  15.5 3.1 %attend.1 = bf16[32,16,128]{2,1,0:T(8,128)(2,1)} custom-call(s32[4]{0:T(128)S(1)} %copy-done.6, bf16[4,32,128]{2,1,0:T(8,128)(2,1)S(1)} %bitcast.11, bf16[4,256,512]{2,1,0:T(8,128)(2,1)S(1)} %copy-done.1, bf16[4,256,512]{2,1,0:T(8,128)(2,1)S(1)} %copy-done.2), custom_call_target="tpu_custom_call" | custom-call | tf_op jit(solution)/shard_map/attend/pallas_call | solution.py:96
  18.7 7.5 %all-to-all-start = ((bf16[32,16,128]{2,1,0:T(8,128)(2,1)}), bf16[32,16,128]{2,1,0:T(8,128)(2,1)S(1)}, u32[]{:S(2)}, u32[]{:S(2)}) async-start(bf16[32,16,128]{2,1,0:T(8,128)(2,1)} %attend.1), calls=%async_computation | async-start | bytes 262144 | tf_op jit(solution)/shard_map/all_to_all | solution.py:254
  26.2 0.0 copy-done.7
  26.2 0.1 copy.11.adapter_ref
  26.3 10.5 %all-to-all-done = bf16[32,16,128]{2,1,0:T(8,128)(2,1)S(1)} async-done(((bf16[32,16,128]{2,1,0:T(8,128)(2,1)}), bf16[32,16,128]{2,1,0:T(8,128)(2,1)S(1)}, u32[]{:S(2)}, u32[]{:S(2)}) %all-to-all-start) | async-done | bytes 131104 | tf_op jit(solution)/shard_map/all_to_all | solution.py:254
  36.8 0.0 copy-done.4
  36.8 0.0 copy-done.5
  36.8 1.1 %shrink.1 = bf16[32,8,128]{2,1,0:T(8,128)(2,1)S(1)} custom-call(s32[1]{0:T(128)} %bitcast.1.quad_ref, s32[16]{0:T(128)S(1)} %copy-done.5, s32[128,1]{1,0:T(8,128)S(1)} %copy.11.adapter_ref, bf16[512,128]{1,0:T(8,128)(2,1)S(1)} %bitcast.8, bf16[16,64,128]{2,1,0:T(8,128)(2,1)S(1)} %bitcast.10), custom_call_target="tpu_custom_call" | custom-call | tf_op jit(solution)/shard_map/shrink/pallas_call | solution.py:140
  38.0 0.0 copy-start.3
  38.0 18.5 %all_to_all.15.refs_4_ = bf16[32,8,128]{2,1,0:T(8,128)(2,1)S(1)} all-to-all(bf16[32,8,128]{2,1,0:T(8,128)(2,1)S(1)} %shrink.1), channel_id=1, replica_groups=mesh['rep'=16,'tp'=32] {'tp'}, dimensions={0} | all-to-all | bytes 131072 | tf_op jit(solution)/shard_map/all_to_all | solution.py:256
  56.5 0.0 collective-permute-done.refs_1_
  56.5 0.0 collective-permute-done.1.refs_2_
  56.5 0.0 collective-permute-done.2.refs_3_
  56.5 0.7 project.1
  57.1 19.9 %all_to_all.16.parts_ref = bf16[8,144,256]{2,1,0:T(8,128)(2,1)S(1)} all-to-all(bf16[8,144,256]{2,1,0:T(8,128)(2,1)S(1)} %project.1), channel_id=1, replica_groups={{0,4,8,12,16,20,24,28},{1,5,9,13,17,21,25,29},{2,6,10,14,18,22,26,30},{..., dimensions={0} | all-to-all | bytes 1179648 | tf_op jit(solution)/shard_map/all_to_all | solution.py:257
  77.0 0.0 copy-done.3
  77.0 1.5 %finish.1 = bf16[128,256]{1,0:T(8,128)(2,1)} custom-call(s32[16]{0:T(128)S(1)} %copy-done.5, s32[128,1]{1,0:T(8,128)S(1)} %copy.11.adapter_ref, bf16[8,144,256]{2,1,0:T(8,128)(2,1)S(1)} %all_to_all.16.parts_ref, bf16[16,64,256]{2,1,0:T(8,128)(2,1)S(1)} %copy-done.3), custom_call_target="tpu_custom_call" | custom-call | tf_op jit(solution)/shard_map/finish/pallas_call | solution.py:217
  (1 shorter events, 0.0 us)
Async XLA Ops:
  0.0 15.5 %copy-start.6 = (s32[4]{0:T(128)S(1)}, s32[4]{0:T(128)}, u32[]{:S(2)}) copy-start(s32[4]{0:T(128)} %len_ref.1) | copy-start | bytes 52
  0.0 1.6 %copy-start = (bf16[128,8192]{1,0:T(8,128)(2,1)S(1)}, bf16[128,8192]{1,0:T(8,128)(2,1)}, u32[]{:S(2)}) copy-start(bf16[128,8192]{1,0:T(8,128)(2,1)} %weight_hbm.1) | copy-start | bytes 6291460
  1.6 13.9 %copy-start.1 = (bf16[4,256,512]{2,1,0:T(8,128)(2,1)S(1)}, bf16[4,256,512]{2,1,0:T(8,128)(2,1)}, u32[]{:S(2)}) copy-start(bf16[4,256,512]{2,1,0:T(8,128)(2,1)} %k_ref.1) | copy-start | bytes 3145732
  1.6 13.9 %copy-start.2 = (bf16[4,256,512]{2,1,0:T(8,128)(2,1)S(1)}, bf16[4,256,512]{2,1,0:T(8,128)(2,1)}, u32[]{:S(2)}) copy-start(bf16[4,256,512]{2,1,0:T(8,128)(2,1)} %v_ref.1) | copy-start | bytes 3145732
  1.6 24.6 %copy-start.7 = (s32[128]{0:T(128)S(1)}, s32[128]{0:T(128)}, u32[]{:S(2)}) copy-start(s32[128]{0:T(128)} %param.13) | copy-start | bytes 1540
  1.6 35.2 %copy-start.4 = (bf16[16,128,64]{1,2,0:T(8,128)(2,1)S(1)}, bf16[16,128,64]{1,2,0:T(8,128)(2,1)}, u32[]{:S(2)}) copy-start(bf16[16,128,64]{1,2,0:T(8,128)(2,1)} %param.16) | copy-start | bytes 786436
  1.6 35.2 %copy-start.5 = (s32[16]{0:T(128)S(1)}, s32[16]{0:T(128)}, u32[]{:S(2)}) copy-start(s32[16]{0:T(128)} %block_ref.3) | copy-start | bytes 196
  3.3 53.1 %collective-permute-start = (bf16[128,2048]{1,0:T(8,128)(2,1)}, bf16[128,2048]{1,0:T(8,128)(2,1)S(1)}, u32[]{:S(2)}, u32[]{:S(2)}) collective-permute-start(bf16[128,2048]{1,0:T(8,128)(2,1)} %get-tuple-element.10), channel_id=1, source_target_pairs={{0,1},{1,2},{2,3},{3,0},{4,5},{5,6},{6,7},{7,4},{8,9},{9,10},{10,1... | collective-permute-start | bytes 1572872 | tf_op jit(solution)/shard_map/ppermute | solution.py:253
  6.7 49.7 %collective-permute-start.1 = (bf16[128,2048]{1,0:T(8,128)(2,1)}, bf16[128,2048]{1,0:T(8,128)(2,1)S(1)}, u32[]{:S(2)}, u32[]{:S(2)}) collective-permute-start(bf16[128,2048]{1,0:T(8,128)(2,1)} %get-tuple-element.11), channel_id=1, source_target_pairs={{0,2},{1,3},{2,0},{3,1},{4,6},{5,7},{6,4},{7,5},{8,10},{9,11},{10,... | collective-permute-start | bytes 1572872 | tf_op jit(solution)/shard_map/ppermute | solution.py:253
  11.4 45.1 %collective-permute-start.2 = (bf16[128,2048]{1,0:T(8,128)(2,1)S(1)}, bf16[128,2048]{1,0:T(8,128)(2,1)S(1)}, u32[]{:S(2)}, u32[]{:S(2)}) collective-permute-start(bf16[128,2048]{1,0:T(8,128)(2,1)S(1)} %get-tuple-element.12), channel_id=1, source_target_pairs={{0,3},{1,0},{2,1},{3,2},{4,7},{5,4},{6,5},{7,6},{8,11},{9,8},{10,9... | collective-permute-start | bytes 1572872 | tf_op jit(solution)/shard_map/ppermute | solution.py:253
  18.7 18.2 %all-to-all-start = ((bf16[32,16,128]{2,1,0:T(8,128)(2,1)}), bf16[32,16,128]{2,1,0:T(8,128)(2,1)S(1)}, u32[]{:S(2)}, u32[]{:S(2)}) async-start(bf16[32,16,128]{2,1,0:T(8,128)(2,1)} %attend.1), calls=%async_computation | async-start | bytes 262144 | tf_op jit(solution)/shard_map/all_to_all | solution.py:254
  38.0 39.1 %copy-start.3 = (bf16[16,64,256]{2,1,0:T(8,128)(2,1)S(1)}, bf16[16,64,256]{2,1,0:T(8,128)(2,1)}, u32[]{:S(2)}) copy-start(bf16[16,64,256]{2,1,0:T(8,128)(2,1)} %up_ref.1) | copy-start | bytes 1572868

commit v3 on v2

v3 whole, which is shorter than its diff:
```python
import functools
import math

import jax
import jax.numpy as jnp
from jax import lax
from jax.experimental import pallas as pl
from jax.experimental.pallas import tpu as pltpu
from jax.sharding import PartitionSpec as P

HEAD_SIZE = 128
QUERY_HEADS = 32
KVH = 4
CTX = 256
QUAD = 4
LINE = 256
BF16, F32 = jnp.bfloat16, jnp.float32
VMEM = pl.BlockSpec(memory_space=pltpu.VMEM)
SMEM = pl.BlockSpec(memory_space=pltpu.SMEM)
HBM = pl.BlockSpec(memory_space=pltpu.HBM)
PARAMS = pltpu.CompilerParams(vmem_limit_bytes=32 * 1024 * 1024)


def in_quad(q, m):
    return ((q >> 1) * 2 + (m >> 1)) * 4 + (q & 1) * 2 + (m & 1)


def start_kernel(
    member_ref, len_ref, q_ref, k_hbm, v_hbm, w_hbm, heads_ref, *refs
):
    pieces = refs[: QUAD - 1]
    k_buf, v_buf, k_sem, v_sem, w_sem = refs[QUAD - 1 :]
    rows, size = k_buf.shape[0], HEAD_SIZE
    k_copies = [pltpu.make_async_copy(k_hbm.at[r], k_buf.at[r], k_sem.at[r]) for r in range(rows)]
    v_copies = [pltpu.make_async_copy(v_hbm.at[r], v_buf.at[r], v_sem.at[r]) for r in range(rows)]
    w_copies = []
    for step, piece in enumerate(pieces):
        place = in_quad(0, lax.bitwise_xor(member_ref[0], step + 1))
        for q in range(piece.shape[1] // LINE):
            first = pl.multiple_of((in_quad(q, 0) + place) * LINE, LINE)
            w_copies.append(
                pltpu.make_async_copy(
                    w_hbm.at[:, pl.ds(first, LINE)],
                    piece.at[:, pl.ds(q * LINE, LINE)],
                    w_sem.at[step, q],
                )
            )
    for copy in k_copies + v_copies + w_copies:
        copy.start()

    q = q_ref[...].astype(F32)
    q_rows = jnp.concatenate(
        [q[:, h * size : (h + 1) * size] for h in range(QUERY_HEADS)], axis=0
    )
    q_lanes = q_rows.T.astype(BF16)
    count = rows * QUERY_HEADS
    lane = lax.broadcasted_iota(jnp.int32, (size, count), 1)
    by_key = [
        jnp.where(lane // (count // KVH) == k, q_lanes, jnp.zeros_like(q_lanes))
        for k in range(KVH)
    ]
    request = lax.broadcasted_iota(jnp.int32, (CTX, count), 1) % rows
    position = lax.broadcasted_iota(jnp.int32, (CTX, count), 0)
    spread = jnp.concatenate(by_key, axis=0)
    scores = jnp.zeros((CTX, count), F32)
    length = jnp.zeros((CTX, count), jnp.int32)
    for r in range(rows):
        k_copies[r].wait()
        all_lanes = jnp.dot(k_buf[r], spread, preferred_element_type=F32)
        scores = jnp.where(request == r, all_lanes, scores)
        length = jnp.where(request == r, len_ref[r], length)
    live = position < length
    scores = jnp.where(live, scores * (1.0 / math.sqrt(size)), -1e30)
    raw = jnp.where(live, jnp.exp(scores - jnp.max(scores, axis=0, keepdims=True)), 0.0)
    probs = (raw / jnp.sum(raw, axis=0, keepdims=True)).T.astype(BF16)
    owner = lax.broadcasted_iota(jnp.int32, (count, CTX), 0) % rows
    wide = jnp.zeros((count, KVH * size), F32)
    for r in range(rows):
        v_copies[r].wait()
        mine = jnp.where(owner == r, probs, jnp.zeros_like(probs))
        wide += jnp.dot(mine, v_buf[r], preferred_element_type=F32)
    group = count // KVH
    own = jnp.concatenate(
        [wide[k * group : (k + 1) * group, k * size : (k + 1) * size] for k in range(KVH)], axis=0
    ).astype(BF16)
    pair = 2 * rows
    for quad in range(QUERY_HEADS // QUAD):
        first = in_quad(quad, 0) * rows
        second = in_quad(quad, 2) * rows
        piece = jnp.concatenate([own[first : first + pair], own[second : second + pair]], axis=0)
        for m in range(QUAD):
            heads_ref[in_quad(quad, m)] = piece
    for copy in w_copies:
        copy.wait()


def start(member, lengths, queries, key_cache, value_cache, weight):
    rows = queries.shape[0]
    depth, columns = weight.shape
    piece = jax.ShapeDtypeStruct((depth, columns // QUAD), BF16)
    return pl.pallas_call(
        start_kernel,
        out_shape=(jax.ShapeDtypeStruct((QUERY_HEADS, QUAD * rows, HEAD_SIZE), BF16),)
        + (piece,) * (QUAD - 1),
        in_specs=[SMEM, SMEM, VMEM, HBM, HBM, HBM],
        out_specs=(VMEM,) + (HBM,) * (QUAD - 1),
        scratch_shapes=[
            pltpu.VMEM((rows, CTX, KVH * HEAD_SIZE), BF16),
            pltpu.VMEM((rows, CTX, KVH * HEAD_SIZE), BF16),
            pltpu.SemaphoreType.DMA((rows,)),
            pltpu.SemaphoreType.DMA((rows,)),
            pltpu.SemaphoreType.DMA((QUAD - 1, columns // QUAD // LINE)),
        ],
        compiler_params=pltpu.CompilerParams(vmem_limit_bytes=60 * 1024 * 1024),
        name="start",
    )(member, lengths, queries, key_cache, value_cache, weight)


def pick_rows(spans, index):
    count, size = spans.shape
    rows = count // QUAD
    row = lax.broadcasted_iota(jnp.int32, (rows, count), 0)
    column = lax.broadcasted_iota(jnp.int32, (rows, count), 1)
    wanted = (row // 4) * 16 + index * 4 + row % 4
    choice = jnp.where(column == wanted, 1.0, 0.0).astype(BF16)
    return jnp.dot(choice, spans, preferred_element_type=F32).astype(BF16)


def shrink_kernel(member_ref, block_ref, adapter_ref, spans_ref, down_ref, out_ref):
    devices, half, _ = out_ref.shape
    heads = pick_rows(spans_ref[...], member_ref[0])
    adapter = adapter_ref[...]
    rank = down_ref.shape[1]
    shrink = jnp.zeros((heads.shape[0], rank), F32)
    for b in range(down_ref.shape[0]):
        mine = jnp.where(adapter == block_ref[b], heads, jnp.zeros_like(heads))
        shrink += lax.dot_general(
            mine, down_ref[b], (((1,), (1,)), ((), ())), preferred_element_type=F32
        )
    for quad in range(devices // QUAD):
        base = quad * 2 * half
        pair = jnp.concatenate(
            [shrink[base : base + half], shrink[base + half : base + 2 * half]], axis=1
        ).astype(BF16)
        for m in range(QUAD):
            out_ref[in_quad(quad, m)] = pair


def shrink_parts(member, spans, down, adapter_col, block_adapter):
    devices = spans.shape[0] // (QUAD * 4)
    rows = spans.shape[0] // QUAD
    half = rows // (devices // QUAD) // 2
    return pl.pallas_call(
        shrink_kernel,
        out_shape=jax.ShapeDtypeStruct((devices, half, 2 * down.shape[2]), BF16),
        in_specs=[SMEM, SMEM, VMEM, VMEM, VMEM],
        out_specs=VMEM,
        compiler_params=PARAMS,
        name="shrink",
    )(member, block_adapter, adapter_col, spans, jnp.swapaxes(down, 1, 2))


def project_kernel(member_ref, spans_ref, *refs):
    weight_ref, *piece_refs, shrink_ref, out_ref = refs
    dests, _, width = out_ref.shape
    rows = spans_ref.shape[0] // QUAD
    spans = spans_ref[...]
    heads = jnp.concatenate(
        [pick_rows(spans, lax.bitwise_xor(member_ref[0], step)) for step in range(QUAD)],
        axis=1,
    )
    place = in_quad(0, member_ref[0])
    for d in range(dests):
        first = pl.multiple_of((in_quad(d, 0) + place) * width, width)
        columns = jnp.concatenate(
            [weight_ref[:, pl.ds(first, width)]]
            + [ref[:, d * width : (d + 1) * width] for ref in piece_refs],
            axis=0,
        )
        out_ref[d, :rows, :] = jnp.dot(heads, columns, preferred_element_type=F32).astype(BF16)
    low_rank = shrink_ref[0].astype(F32)
    for s in range(1, shrink_ref.shape[0]):
        low_rank += shrink_ref[s].astype(F32)
    wide = jnp.concatenate([low_rank, jnp.zeros_like(low_rank)], axis=1)
    block = jnp.concatenate([wide, jnp.zeros_like(wide)], axis=0).astype(BF16)
    for d in range(dests):
        out_ref[d, rows:, :] = block


def project(member, spans, weight, pieces, shrinks):
    rows = spans.shape[0] // QUAD
    dests = pieces[0].shape[1] // LINE
    return pl.pallas_call(
        project_kernel,
        out_shape=jax.ShapeDtypeStruct((dests, rows + 2 * shrinks.shape[1], LINE), BF16),
        in_specs=[SMEM] + [VMEM] * (QUAD + 2),
        out_specs=VMEM,
        compiler_params=PARAMS,
        name="project",
    )(member, spans, weight, *pieces, shrinks)


def finish_kernel(block_ref, adapter_ref, parts_ref, up_ref, out_ref):
    count = parts_ref.shape[0]
    rows, width = out_ref.shape
    blocks, rank, _ = up_ref.shape
    lanes = 2 * rank
    half = rows // count // 2
    left = lax.broadcasted_iota(jnp.int32, (half, lanes), 1) < rank
    pieces = []
    for s in range(count):
        pair = parts_ref[s, rows : rows + 2 * half, :lanes].astype(F32)[:half]
        turned = jnp.concatenate([pair[:, rank:], pair[:, :rank]], axis=1)
        pieces += [jnp.where(left, pair, turned), jnp.where(left, turned, pair)]
    low_rank = jnp.concatenate(pieces, axis=0)
    adapter = adapter_ref[...]
    wide_left = lax.broadcasted_iota(jnp.int32, (rows, lanes), 1) < rank
    spread = []
    for b in range(0, blocks, 2):
        match = jnp.where(wide_left, block_ref[b], block_ref[b + 1]) == adapter
        spread.append(jnp.where(match, low_rank, 0.0).astype(BF16))
    lora = jnp.dot(
        jnp.concatenate(spread, axis=1),
        up_ref[...].reshape(blocks * rank, width),
        preferred_element_type=F32,
    )
    total = parts_ref[0, :rows, :].astype(F32)
    for s in range(1, count):
        total += parts_ref[s, :rows, :].astype(F32)
    out_ref[...] = (total + lora).astype(BF16)


def finish(parts, up, adapter_col, block_adapter, rows):
    return pl.pallas_call(
        finish_kernel,
        out_shape=jax.ShapeDtypeStruct((rows, parts.shape[2]), BF16),
        in_specs=[SMEM, VMEM, VMEM, VMEM],
        out_specs=VMEM,
        compiler_params=PARAMS,
        name="finish",
    )(block_adapter, adapter_col, parts, up)


def per_device(
    devices,
    queries,
    key_cache,
    value_cache,
    lengths,
    request_adapter,
    block_adapter,
    output_weight,
    down_factors,
    up_factors,
):
    quads = devices // QUAD
    groups = [[in_quad(q, m) for q in range(quads)] for m in range(QUAD)]
    exchange = functools.partial(
        lax.all_to_all, axis_name="tp", split_axis=0, concat_axis=0, tiled=True
    )
    rows = request_adapter.shape[0]
    adapter_col = request_adapter[:, None]
    place = lax.axis_index("tp")
    member = ((place >> 2 & 1) * 2 + (place & 1)).astype(jnp.int32)[None]

    own, *weights = start(member, lengths, queries, key_cache, value_cache, output_weight)
    for step in range(1, QUAD):
        turn = [(in_quad(q, m), in_quad(q, m ^ step)) for q in range(quads) for m in range(QUAD)]
        weights[step - 1] = lax.ppermute(weights[step - 1], "tp", turn)
    spans = exchange(own).reshape(QUAD * rows, HEAD_SIZE)
    shrinks = exchange(shrink_parts(member, spans, down_factors, adapter_col, block_adapter))
    parts = exchange(project(member, spans, output_weight, weights, shrinks), axis_index_groups=groups)
    return finish(parts, up_factors, adapter_col, block_adapter, rows)


def solution(mesh):
    in_specs = (
        P(("rep", "tp"), None),
        P(("rep", "tp"), None, None),
        P(("rep", "tp"), None, None),
        P(("rep", "tp")),
        P("rep"),
        P("rep"),
        P("tp", None),
        P("rep", "tp", None),
        P("rep", None, "tp"),
    )
    return jax.shard_map(
        functools.partial(per_device, mesh.shape["tp"]),
        mesh=mesh,
        in_specs=in_specs,
        out_specs=P("rep", "tp"),
        check_vma=False,
    )
```

time: 78.9 us -> 129 us (1.63)
  the two profiles are of different devices: /device:TPU:320 before, /device:TPU:200 now
where the time goes in v3:
time: 129 us
  Pallas kernels  54.9 us (43%)
  blocking collectives  34.2 us (27%)
  starting transfers between devices  19.4 us (15%)
  waiting for transfers between devices  18.9 us (15%)
    pallas_call x1, Pallas kernels, start(): pl.pallas_call(start_kernel, out_shape=(jax.ShapeDtypeStruct((QUERY_HEADS...  50.6 us
    all_to_all x1, blocking collectives, per_device(): exchange(project(member, spans, output_weight, weights, shrinks), axis_in...  20.6 us
    all_to_all x1, waiting for transfers between devices, per_device(): spans = exchange(own).reshape(QUAD * rows, HEAD_SIZE)  18.9 us
    all_to_all x1, blocking collectives, per_device(): exchange(shrink_parts(member, spans, down_factors, adapter_col, block_ada...  13.6 us
    all_to_all x1, starting transfers between devices, per_device(): spans = exchange(own).reshape(QUAD * rows, HEAD_SIZE)  10.2 us
    ppermute x3, starting transfers between devices, per_device(): weights[step - 1] = lax.ppermute(weights[step - 1], 'tp', turn)  9.21 us
  transfers between devices with their start and end apart: 4, of which 1 were waited for; matrix products, arithmetic and copies ran while one was open for 0% of the time, Pallas kernels for 1%

profile of v3, /device:TPU:200, one launch (start us, length us, event | category | flops | bytes accessed | tf_op | source)
XLA Modules:
  0.0 128.7 jit_solution(11708971801437736855)
XLA Ops:
  0.0 0.0 copy-start.4
  0.0 0.0 copy-start.3
  0.0 0.0 copy-start
  0.0 50.6 %start.1 = (bf16[32,16,128]{2,1,0:T(8,128)(2,1)}, bf16[128,2048]{1,0:T(8,128)(2,1)}, bf16[128,2048]{1,0:T(8,128)(2,1)}, bf16[128,2048]{1,0:T(8,128)(2,1)}) custom-call(s32[1]{0:T(128)} %bitcast.1.member_ref, s32[4]{0:T(128)} %len_ref.1, bf16[4,4096]{1,0:T(4,128)(2,1)} %q_ref.1, bf16[4,256,512]{2,1,0:T(8,128)(2,1)} %k_hbm.1, bf16[4,256,512]{2,1,0:T(8,128)(2,1)} %v_hbm.1, ...), custom_call_target="tpu_custom_call" | custom-call | tf_op jit(solution)/shard_map/start/pallas_call | solution.py:101
  50.6 3.4 %collective-permute-start = (bf16[128,2048]{1,0:T(8,128)(2,1)}, bf16[128,2048]{1,0:T(8,128)(2,1)S(1)}, u32[]{:S(2)}, u32[]{:S(2)}) collective-permute-start(bf16[128,2048]{1,0:T(8,128)(2,1)} %get-tuple-element.10), channel_id=1, source_target_pairs={{0,1},{1,0},{4,5},{5,4},{2,3},{3,2},{6,7},{7,6},{8,9},{9,8},{12,13... | collective-permute-start | bytes 1572872 | tf_op jit(solution)/shard_map/ppermute | solution.py:269
  54.0 2.4 %collective-permute-start.1 = (bf16[128,2048]{1,0:T(8,128)(2,1)}, bf16[128,2048]{1,0:T(8,128)(2,1)S(1)}, u32[]{:S(2)}, u32[]{:S(2)}) collective-permute-start(bf16[128,2048]{1,0:T(8,128)(2,1)} %get-tuple-element.11), channel_id=1, source_target_pairs={{0,4},{1,5},{4,0},{5,1},{2,6},{3,7},{6,2},{7,3},{8,12},{9,13},{12,... | collective-permute-start | bytes 1572872 | tf_op jit(solution)/shard_map/ppermute | solution.py:269
  56.4 3.5 %collective-permute-start.2 = (bf16[128,2048]{1,0:T(8,128)(2,1)}, bf16[128,2048]{1,0:T(8,128)(2,1)}, u32[]{:S(2)}, u32[]{:S(2)}) collective-permute-start(bf16[128,2048]{1,0:T(8,128)(2,1)} %get-tuple-element.12), channel_id=1, source_target_pairs={{0,5},{1,4},{4,1},{5,0},{2,7},{3,6},{6,3},{7,2},{8,13},{9,12},{12,... | collective-permute-start | bytes 1572872 | tf_op jit(solution)/shard_map/ppermute | solution.py:269
  59.9 10.2 %all-to-all-start = ((bf16[32,16,128]{2,1,0:T(8,128)(2,1)}), bf16[32,16,128]{2,1,0:T(8,128)(2,1)S(1)}, u32[]{:S(2)}, u32[]{:S(2)}) async-start(bf16[32,16,128]{2,1,0:T(8,128)(2,1)} %get-tuple-element.9), calls=%async_computation | async-start | bytes 262144 | tf_op jit(solution)/shard_map/all_to_all | solution.py:270
  70.1 0.0 copy-done.4
  70.1 0.1 copy.11.adapter_ref
  70.2 18.9 %all-to-all-done = bf16[32,16,128]{2,1,0:T(8,128)(2,1)S(1)} async-done(((bf16[32,16,128]{2,1,0:T(8,128)(2,1)}), bf16[32,16,128]{2,1,0:T(8,128)(2,1)S(1)}, u32[]{:S(2)}, u32[]{:S(2)}) %all-to-all-start) | async-done | bytes 131104 | tf_op jit(solution)/shard_map/all_to_all | solution.py:270
  89.1 0.0 copy-done.3
  89.1 0.0 copy-start.2
  89.1 0.9 copy-done.2
  90.1 1.1 shrink.1
  91.2 13.6 %all_to_all.15.refs_4_ = bf16[32,8,128]{2,1,0:T(8,128)(2,1)S(1)} all-to-all(bf16[32,8,128]{2,1,0:T(8,128)(2,1)S(1)} %shrink.1), channel_id=1, replica_groups=mesh['rep'=16,'tp'=32] {'tp'}, dimensions={0} | all-to-all | bytes 131072 | tf_op jit(solution)/shard_map/all_to_all | solution.py:271
  104.8 0.0 copy-start.1
  104.8 0.0 collective-permute-done.refs_1_
  104.8 0.0 collective-permute-done.1.refs_2_
  104.8 0.0 collective-permute-done.2.refs_3_
  104.8 0.0 copy-done
  104.8 1.8 %project.1 = bf16[8,144,256]{2,1,0:T(8,128)(2,1)S(1)} custom-call(s32[1]{0:T(128)} %bitcast.1.member_ref, bf16[512,128]{1,0:T(8,128)(2,1)S(1)} %bitcast.5, bf16[128,8192]{1,0:T(8,128)(2,1)S(1)} %copy-done, bf16[128,2048]{1,0:T(8,128)(2,1)S(1)} %collective-permute-done.refs_1_, bf16[128,2048]{1,0:T(8,128)(2,1)S(1)} %collective-permute-done.1.refs_2_, ...), custom_call_target="tpu_custom_call" | custom-call | tf_op jit(solution)/shard_map/project/pallas_call | solution.py:193
  106.6 20.6 %all_to_all.16.parts_ref = bf16[8,144,256]{2,1,0:T(8,128)(2,1)S(1)} all-to-all(bf16[8,144,256]{2,1,0:T(8,128)(2,1)S(1)} %project.1), channel_id=1, replica_groups={{0,2,8,10,16,18,24,26},{1,3,9,11,17,19,25,27},{4,6,12,14,20,22,28,30},{..., dimensions={0} | all-to-all | bytes 1179648 | tf_op jit(solution)/shard_map/all_to_all | solution.py:272
  127.2 0.0 copy-done.1
  127.2 1.5 %finish.1 = bf16[128,256]{1,0:T(8,128)(2,1)} custom-call(s32[16]{0:T(128)S(1)} %copy-done.3, s32[128,1]{1,0:T(8,128)S(1)} %copy.11.adapter_ref, bf16[8,144,256]{2,1,0:T(8,128)(2,1)S(1)} %all_to_all.16.parts_ref, bf16[16,64,256]{2,1,0:T(8,128)(2,1)S(1)} %copy-done.1), custom_call_target="tpu_custom_call" | custom-call | tf_op jit(solution)/shard_map/finish/pallas_call | solution.py:234
Async XLA Ops:
  0.0 70.1 %copy-start.4 = (s32[128]{0:T(128)S(1)}, s32[128]{0:T(128)}, u32[]{:S(2)}) copy-start(s32[128]{0:T(128)} %param.13) | copy-start | bytes 1540
  0.0 89.1 %copy-start.3 = (s32[16]{0:T(128)S(1)}, s32[16]{0:T(128)}, u32[]{:S(2)}) copy-start(s32[16]{0:T(128)} %block_ref.3) | copy-start | bytes 196
  0.0 104.8 %copy-start = (bf16[128,8192]{1,0:T(8,128)(2,1)S(1)}, bf16[128,8192]{1,0:T(8,128)(2,1)}, u32[]{:S(2)}) copy-start(bf16[128,8192]{1,0:T(8,128)(2,1)} %refs_0_.1) | copy-start | bytes 6291460
  50.6 54.2 %collective-permute-start = (bf16[128,2048]{1,0:T(8,128)(2,1)}, bf16[128,2048]{1,0:T(8,128)(2,1)S(1)}, u32[]{:S(2)}, u32[]{:S(2)}) collective-permute-start(bf16[128,2048]{1,0:T(8,128)(2,1)} %get-tuple-element.10), channel_id=1, source_target_pairs={{0,1},{1,0},{4,5},{5,4},{2,3},{3,2},{6,7},{7,6},{8,9},{9,8},{12,13... | collective-permute-start | bytes 1572872 | tf_op jit(solution)/shard_map/ppermute | solution.py:269
  54.0 50.8 %collective-permute-start.1 = (bf16[128,2048]{1,0:T(8,128)(2,1)}, bf16[128,2048]{1,0:T(8,128)(2,1)S(1)}, u32[]{:S(2)}, u32[]{:S(2)}) collective-permute-start(bf16[128,2048]{1,0:T(8,128)(2,1)} %get-tuple-element.11), channel_id=1, source_target_pairs={{0,4},{1,5},{4,0},{5,1},{2,6},{3,7},{6,2},{7,3},{8,12},{9,13},{12,... | collective-permute-start | bytes 1572872 | tf_op jit(solution)/shard_map/ppermute | solution.py:269
  56.4 48.4 %collective-permute-start.2 = (bf16[128,2048]{1,0:T(8,128)(2,1)}, bf16[128,2048]{1,0:T(8,128)(2,1)}, u32[]{:S(2)}, u32[]{:S(2)}) collective-permute-start(bf16[128,2048]{1,0:T(8,128)(2,1)} %get-tuple-element.12), channel_id=1, source_target_pairs={{0,5},{1,4},{4,1},{5,0},{2,7},{3,6},{6,3},{7,2},{8,13},{9,12},{12,... | collective-permute-start | bytes 1572872 | tf_op jit(solution)/shard_map/ppermute | solution.py:269
  59.9 29.2 %all-to-all-start = ((bf16[32,16,128]{2,1,0:T(8,128)(2,1)}), bf16[32,16,128]{2,1,0:T(8,128)(2,1)S(1)}, u32[]{:S(2)}, u32[]{:S(2)}) async-start(bf16[32,16,128]{2,1,0:T(8,128)(2,1)} %get-tuple-element.9), calls=%async_computation | async-start | bytes 262144 | tf_op jit(solution)/shard_map/all_to_all | solution.py:270
  89.1 1.0 copy-start.2
  104.8 22.4 %copy-start.1 = (bf16[16,64,256]{2,1,0:T(8,128)(2,1)S(1)}, bf16[16,64,256]{2,1,0:T(8,128)(2,1)}, u32[]{:S(2)}) copy-start(bf16[16,64,256]{2,1,0:T(8,128)(2,1)} %up_ref.1) | copy-start | bytes 1572868

commit v4 on v3

v4 whole, which is shorter than its diff:
```python
import functools
import math

import jax
import jax.numpy as jnp
from jax import lax
from jax.experimental import pallas as pl
from jax.experimental.pallas import tpu as pltpu
from jax.sharding import PartitionSpec as P

HEAD_SIZE = 128
QUERY_HEADS = 32
KVH = 4
CTX = 256
QUAD = 4
LINE = 256
BF16, F32 = jnp.bfloat16, jnp.float32
VMEM = pl.BlockSpec(memory_space=pltpu.VMEM)
SMEM = pl.BlockSpec(memory_space=pltpu.SMEM)
HBM = pl.BlockSpec(memory_space=pltpu.HBM)
PARAMS = pltpu.CompilerParams(vmem_limit_bytes=16 * 1024 * 1024)
WHOLE = pltpu.CompilerParams(vmem_limit_bytes=60 * 1024 * 1024)


def in_quad(q, m):
    return q * QUAD + m


def regroup_kernel(steps, member_ref, w_hbm, *refs):
    *pieces, sem = refs
    copies = []
    for i, (step, piece) in enumerate(zip(steps, pieces)):
        m = lax.rem(member_ref[0] + step, QUAD)
        for q in range(piece.shape[1] // LINE):
            first = pl.multiple_of(in_quad(q, m) * LINE, LINE)
            copies.append(
                pltpu.make_async_copy(
                    w_hbm.at[:, pl.ds(first, LINE)], piece.at[:, pl.ds(q * LINE, LINE)], sem.at[i, q]
                )
            )
    for copy in copies:
        copy.start()
    for copy in copies:
        copy.wait()


def regroup(member, weight, steps):
    depth, columns = weight.shape
    piece = jax.ShapeDtypeStruct((depth, columns // QUAD), BF16)
    return pl.pallas_call(
        functools.partial(regroup_kernel, steps),
        out_shape=(piece,) * len(steps),
        in_specs=[SMEM, HBM],
        out_specs=(VMEM,) * len(steps),
        scratch_shapes=[pltpu.SemaphoreType.DMA((len(steps), columns // QUAD // LINE))],
        compiler_params=WHOLE,
        name="regroup",
    )(member, weight)


def attend_kernel(len_ref, q_ref, k_ref, v_ref, heads_ref):
    rows, size = k_ref.shape[0], HEAD_SIZE
    q = q_ref[...].astype(F32)
    q_rows = jnp.concatenate(
        [q[:, h * size : (h + 1) * size] for h in range(QUERY_HEADS)], axis=0
    )
    q_lanes = q_rows.T.astype(BF16)
    count = rows * QUERY_HEADS
    lane = lax.broadcasted_iota(jnp.int32, (size, count), 1)
    by_key = [
        jnp.where(lane // (count // KVH) == k, q_lanes, jnp.zeros_like(q_lanes))
        for k in range(KVH)
    ]
    request = lax.broadcasted_iota(jnp.int32, (CTX, count), 1) % rows
    position = lax.broadcasted_iota(jnp.int32, (CTX, count), 0)
    spread = jnp.concatenate(by_key, axis=0)
    scores = jnp.zeros((CTX, count), F32)
    length = jnp.zeros((CTX, count), jnp.int32)
    for r in range(rows):
        all_lanes = jnp.dot(k_ref[r], spread, preferred_element_type=F32)
        scores = jnp.where(request == r, all_lanes, scores)
        length = jnp.where(request == r, len_ref[r], length)
    live = position < length
    scores = jnp.where(live, scores * (1.0 / math.sqrt(size)), -1e30)
    raw = jnp.where(live, jnp.exp(scores - jnp.max(scores, axis=0, keepdims=True)), 0.0)
    probs = (raw / jnp.sum(raw, axis=0, keepdims=True)).T.astype(BF16)
    owner = lax.broadcasted_iota(jnp.int32, (count, CTX), 0) % rows
    wide = jnp.zeros((count, KVH * size), F32)
    for r in range(rows):
        mine = jnp.where(owner == r, probs, jnp.zeros_like(probs))
        wide += jnp.dot(mine, v_ref[r], preferred_element_type=F32)
    group = count // KVH
    own = jnp.concatenate(
        [wide[k * group : (k + 1) * group, k * size : (k + 1) * size] for k in range(KVH)], axis=0
    ).astype(BF16)
    span = QUAD * rows
    for quad in range(QUERY_HEADS // QUAD):
        for m in range(QUAD):
            heads_ref[in_quad(quad, m)] = own[quad * span : (quad + 1) * span]


def attend(lengths, queries, key_cache, value_cache):
    rows = queries.shape[0]
    return pl.pallas_call(
        attend_kernel,
        out_shape=jax.ShapeDtypeStruct((QUERY_HEADS, QUAD * rows, HEAD_SIZE), BF16),
        in_specs=[SMEM, VMEM, VMEM, VMEM],
        out_specs=VMEM,
        compiler_params=PARAMS,
        name="attend",
    )(lengths, queries, key_cache, value_cache)


def pick_rows(spans, index):
    count, size = spans.shape
    rows = count // QUAD
    row = lax.broadcasted_iota(jnp.int32, (rows, count), 0)
    column = lax.broadcasted_iota(jnp.int32, (rows, count), 1)
    wanted = (row // 4) * 16 + index * 4 + row % 4
    choice = jnp.where(column == wanted, 1.0, 0.0).astype(BF16)
    return jnp.dot(choice, spans, preferred_element_type=F32).astype(BF16)


def shrink_kernel(member_ref, block_ref, adapter_ref, spans_ref, down_ref, out_ref):
    half = out_ref.shape[1]
    heads = pick_rows(spans_ref[...], member_ref[0])
    adapter = adapter_ref[...]
    rank = down_ref.shape[1]
    shrink = jnp.zeros((heads.shape[0], rank), F32)
    for b in range(down_ref.shape[0]):
        mine = jnp.where(adapter == block_ref[b], heads, jnp.zeros_like(heads))
        shrink += lax.dot_general(
            mine, down_ref[b], (((1,), (1,)), ((), ())), preferred_element_type=F32
        )
    packed = jnp.concatenate([shrink[:half], shrink[half:]], axis=1).astype(BF16)
    for m in range(QUAD):
        out_ref[m] = packed


def shrink_parts(member, spans, down, adapter_col, block_adapter):
    half = spans.shape[0] // QUAD // 2
    return pl.pallas_call(
        shrink_kernel,
        out_shape=jax.ShapeDtypeStruct((QUAD, half, 2 * down.shape[2]), BF16),
        in_specs=[SMEM, SMEM, VMEM, VMEM, VMEM],
        out_specs=VMEM,
        compiler_params=PARAMS,
        name="shrink",
    )(member, block_adapter, adapter_col, spans, jnp.swapaxes(down, 1, 2))


def project_kernel(member_ref, spans_ref, *refs):
    weight_ref, *piece_refs, shrink_ref, out_ref = refs
    dests, _, width = out_ref.shape
    rows = spans_ref.shape[0] // QUAD
    spans = spans_ref[...]
    heads = jnp.concatenate(
        [pick_rows(spans, lax.rem(member_ref[0] + QUAD - step, QUAD)) for step in range(QUAD)],
        axis=1,
    )
    place = in_quad(0, member_ref[0])
    for d in range(dests):
        first = pl.multiple_of((in_quad(d, 0) + place) * width, width)
        columns = jnp.concatenate(
            [weight_ref[:, pl.ds(first, width)]]
            + [ref[:, d * width : (d + 1) * width] for ref in piece_refs],
            axis=0,
        )
        out_ref[d, :rows, :] = jnp.dot(heads, columns, preferred_element_type=F32).astype(BF16)
    shrink = shrink_ref[0].astype(F32)
    for m in range(1, QUAD):
        shrink += shrink_ref[m].astype(F32)
    half = shrink.shape[0] // 2
    packed = jnp.concatenate([shrink[:half], shrink[half:]], axis=1).astype(BF16)
    for d in range(dests):
        out_ref[d, rows:, :] = packed


def project(member, spans, weight, pieces, shrinks):
    rows = spans.shape[0] // QUAD
    dests = pieces[0].shape[1] // LINE
    return pl.pallas_call(
        project_kernel,
        out_shape=jax.ShapeDtypeStruct((dests, rows + shrinks.shape[1] // 2, LINE), BF16),
        in_specs=[SMEM] + [VMEM] * (QUAD + 2),
        out_specs=VMEM,
        compiler_params=PARAMS,
        name="project",
    )(member, spans, weight, *pieces, shrinks)


def finish_kernel(block_ref, adapter_ref, parts_ref, up_ref, out_ref):
    count = parts_ref.shape[0]
    rows, width = out_ref.shape
    blocks, rank, _ = up_ref.shape
    lanes = 2 * rank
    packed = parts_ref[0, rows:, :].astype(F32)
    for s in range(1, count):
        packed += parts_ref[s, rows:, :].astype(F32)
    pair = jnp.concatenate([packed[:, :lanes], packed[:, lanes:]], axis=0)
    turned = jnp.concatenate([pair[:, rank:], pair[:, :rank]], axis=1)
    left = lax.broadcasted_iota(jnp.int32, pair.shape, 1) < rank
    low_rank = jnp.concatenate(
        [jnp.where(left, pair, turned), jnp.where(left, turned, pair)], axis=0
    )
    adapter = adapter_ref[...]
    wide_left = lax.broadcasted_iota(jnp.int32, (rows, lanes), 1) < rank
    spread = []
    for b in range(0, blocks, 2):
        match = jnp.where(wide_left, block_ref[b], block_ref[b + 1]) == adapter
        spread.append(jnp.where(match, low_rank, 0.0).astype(BF16))
    lora = jnp.dot(
        jnp.concatenate(spread, axis=1),
        up_ref[...].reshape(blocks * rank, width),
        preferred_element_type=F32,
    )
    total = parts_ref[0, :rows, :].astype(F32)
    for s in range(1, count):
        total += parts_ref[s, :rows, :].astype(F32)
    out_ref[...] = (total + lora).astype(BF16)


def finish(parts, up, adapter_col, block_adapter, rows):
    return pl.pallas_call(
        finish_kernel,
        out_shape=jax.ShapeDtypeStruct((rows, parts.shape[2]), BF16),
        in_specs=[SMEM, VMEM, VMEM, VMEM],
        out_specs=VMEM,
        compiler_params=PARAMS,
        name="finish",
    )(block_adapter, adapter_col, parts, up)


def per_device(
    devices,
    queries,
    key_cache,
    value_cache,
    lengths,
    request_adapter,
    block_adapter,
    output_weight,
    down_factors,
    up_factors,
):
    quads = devices // QUAD
    groups = [[in_quad(q, m) for q in range(quads)] for m in range(QUAD)]
    lines = [[in_quad(q, m) for m in range(QUAD)] for q in range(quads)]
    exchange = functools.partial(
        lax.all_to_all, axis_name="tp", split_axis=0, concat_axis=0, tiled=True
    )
    rows = request_adapter.shape[0]
    adapter_col = request_adapter[:, None]
    member = (lax.axis_index("tp") & (QUAD - 1)).astype(jnp.int32)[None]

    def ahead(piece, step):
        turn = [
            (in_quad(q, m), in_quad(q, (m + step) % QUAD)) for q in range(quads) for m in range(QUAD)
        ]
        return lax.ppermute(piece, "tp", turn)

    steps = range(1, QUAD)
    weights = regroup(member, output_weight, steps)
    weights = [ahead(piece, step) for piece, step in zip(weights, steps)]
    own = attend(lengths, queries, key_cache, value_cache)
    spans = exchange(own).reshape(QUAD * rows, HEAD_SIZE)
    shrinks = exchange(
        shrink_parts(member, spans, down_factors, adapter_col, block_adapter),
        axis_index_groups=lines,
    )
    parts = exchange(project(member, spans, output_weight, weights, shrinks), axis_index_groups=groups)
    return finish(parts, up_factors, adapter_col, block_adapter, rows)


def solution(mesh):
    in_specs = (
        P(("rep", "tp"), None),
        P(("rep", "tp"), None, None),
        P(("rep", "tp"), None, None),
        P(("rep", "tp")),
        P("rep"),
        P("rep"),
        P("tp", None),
        P("rep", "tp", None),
        P("rep", None, "tp"),
    )
    return jax.shard_map(
        functools.partial(per_device, mesh.shape["tp"]),
        mesh=mesh,
        in_specs=in_specs,
        out_specs=P("rep", "tp"),
        check_vma=False,
    )
```

time: 129 us -> 75.7 us (0.59)
  the two profiles are of different devices: /device:TPU:200 before, /device:TPU:384 now
where the time goes in v4:
time: 75.7 us; the launch traced here: 75.3 us
  blocking collectives  34.5 us (46%)
  starting transfers between devices  19 us (25%)
  waiting for transfers between devices  10.5 us (14%)
  Pallas kernels  9.66 us (13%)
  local copies, waits for them, and re-layouts  1.37 us (2%)
    all_to_all x1, blocking collectives, per_device(): exchange(project(member, spans, output_weight, weights, shrinks), axis_in...  25.6 us
    ppermute x3, starting transfers between devices, ahead(): return lax.ppermute(piece, 'tp', turn)  11.5 us
    all_to_all x1, waiting for transfers between devices, per_device(): spans = exchange(own).reshape(QUAD * rows, HEAD_SIZE)  10.5 us
    all_to_all x1, blocking collectives, per_device(): exchange(shrink_parts(member, spans, down_factors, adapter_col, block_ada...  8.94 us
    all_to_all x1, starting transfers between devices, per_device(): spans = exchange(own).reshape(QUAD * rows, HEAD_SIZE)  7.52 us
    pallas_call x1, Pallas kernels, regroup(): pl.pallas_call(functools.partial(regroup_kernel, steps), out_shape=(piece...  2.87 us
    pallas_call x1, Pallas kernels, attend(): pl.pallas_call(attend_kernel, out_shape=jax.ShapeDtypeStruct((QUERY_HEADS...  2.13 us
    pallas_call x1, Pallas kernels, project(): pl.pallas_call(project_kernel, out_shape=jax.ShapeDtypeStruct((dests, row...  2.07 us
  transfers between devices with their start and end apart: 4, of which 1 were waited for; matrix products, arithmetic and copies ran while one was open for 0% of the time, Pallas kernels for 4%

profile of v4, /device:TPU:384, one launch (start us, length us, event | category | flops | bytes accessed | tf_op | source)
XLA Modules:
  0.0 75.3 jit_solution(537762385641217226)
XLA Ops:
  0.0 0.0 copy-start.7
  0.0 0.0 copy-start.1
  0.0 0.0 copy-start.8
  0.0 0.0 copy-start.4
  0.0 0.0 copy-start.6
  0.0 2.9 %regroup.1 = (bf16[128,2048]{1,0:T(8,128)(2,1)}, bf16[128,2048]{1,0:T(8,128)(2,1)}, bf16[128,2048]{1,0:T(8,128)(2,1)}) custom-call(s32[1]{0:T(128)} %bitcast.1.member_ref, bf16[128,8192]{1,0:T(8,128)(2,1)} %refs_0_.1), custom_call_target="tpu_custom_call" | custom-call | tf_op jit(solution)/shard_map/regroup/pallas_call | solution.py:50
  2.9 0.0 copy-start
  2.9 3.5 %collective-permute-start = (bf16[128,2048]{1,0:T(8,128)(2,1)}, bf16[128,2048]{1,0:T(8,128)(2,1)}, u32[]{:S(2)}, u32[]{:S(2)}) collective-permute-start(bf16[128,2048]{1,0:T(8,128)(2,1)} %get-tuple-element.8), channel_id=1, source_target_pairs={{0,1},{1,2},{2,3},{3,0},{4,5},{5,6},{6,7},{7,4},{8,9},{9,10},{10,1... | collective-permute-start | bytes 1572872 | tf_op jit(solution)/shard_map/ppermute | solution.py:260
  6.5 4.6 %collective-permute-start.1 = (bf16[128,2048]{1,0:T(8,128)(2,1)}, bf16[128,2048]{1,0:T(8,128)(2,1)}, u32[]{:S(2)}, u32[]{:S(2)}) collective-permute-start(bf16[128,2048]{1,0:T(8,128)(2,1)} %get-tuple-element.9), channel_id=1, source_target_pairs={{0,2},{1,3},{2,0},{3,1},{4,6},{5,7},{6,4},{7,5},{8,10},{9,11},{10,... | collective-permute-start | bytes 1572872 | tf_op jit(solution)/shard_map/ppermute | solution.py:260
  11.1 3.3 %collective-permute-start.2 = (bf16[128,2048]{1,0:T(8,128)(2,1)}, bf16[128,2048]{1,0:T(8,128)(2,1)}, u32[]{:S(2)}, u32[]{:S(2)}) collective-permute-start(bf16[128,2048]{1,0:T(8,128)(2,1)} %get-tuple-element.10), channel_id=1, source_target_pairs={{0,3},{1,0},{2,1},{3,2},{4,7},{5,4},{6,5},{7,6},{8,11},{9,8},{10,9... | collective-permute-start | bytes 1572872 | tf_op jit(solution)/shard_map/ppermute | solution.py:260
  14.5 0.0 copy-done.7
  14.5 0.0 copy-done.1
  14.5 0.0 copy-done.5
  14.5 0.0 copy-start.2
  14.5 1.2 %copy-done.2 = bf16[4,256,512]{2,1,0:T(8,128)(2,1)S(1)} copy-done((bf16[4,256,512]{2,1,0:T(8,128)(2,1)S(1)}, bf16[4,256,512]{2,1,0:T(8,128)(2,1)}, u32[]{:S(2)}) %copy-start.2) | copy-done | bytes 1048600
  15.7 2.1 %attend.1 = bf16[32,16,128]{2,1,0:T(8,128)(2,1)} custom-call(s32[4]{0:T(128)S(1)} %copy-done.7, bf16[4,4096]{1,0:T(4,128)(2,1)S(1)} %copy-done.5, bf16[4,256,512]{2,1,0:T(8,128)(2,1)S(1)} %copy-done.1, bf16[4,256,512]{2,1,0:T(8,128)(2,1)S(1)} %copy-done.2), custom_call_target="tpu_custom_call" | custom-call | tf_op jit(solution)/shard_map/attend/pallas_call | solution.py:104
  17.9 7.5 %all-to-all-start = ((bf16[32,16,128]{2,1,0:T(8,128)(2,1)}), bf16[32,16,128]{2,1,0:T(8,128)(2,1)S(1)}, u32[]{:S(2)}, u32[]{:S(2)}) async-start(bf16[32,16,128]{2,1,0:T(8,128)(2,1)} %attend.1), calls=%async_computation | async-start | bytes 262144 | tf_op jit(solution)/shard_map/all_to_all | solution.py:266
  25.4 0.0 copy-done.8
  25.4 0.1 copy.11.adapter_ref
  25.5 10.5 %all-to-all-done = bf16[32,16,128]{2,1,0:T(8,128)(2,1)S(1)} async-done(((bf16[32,16,128]{2,1,0:T(8,128)(2,1)}), bf16[32,16,128]{2,1,0:T(8,128)(2,1)S(1)}, u32[]{:S(2)}, u32[]{:S(2)}) %all-to-all-start) | async-done | bytes 131104 | tf_op jit(solution)/shard_map/all_to_all | solution.py:266
  36.0 0.0 copy-done.4
  36.0 0.0 copy-done.6
  36.0 1.1 %shrink.1 = bf16[4,64,128]{2,1,0:T(8,128)(2,1)S(1)} custom-call(s32[1]{0:T(128)} %bitcast.1.member_ref, s32[16]{0:T(128)S(1)} %copy-done.6, s32[128,1]{1,0:T(8,128)S(1)} %copy.11.adapter_ref, bf16[512,128]{1,0:T(8,128)(2,1)S(1)} %bitcast.4, bf16[16,64,128]{2,1,0:T(8,128)(2,1)S(1)} %bitcast.6), custom_call_target="tpu_custom_call" | custom-call | tf_op jit(solution)/shard_map/shrink/pallas_call | solution.py:142
  37.2 8.9 %all_to_all.15.refs_4_ = bf16[4,64,128]{2,1,0:T(8,128)(2,1)S(1)} all-to-all(bf16[4,64,128]{2,1,0:T(8,128)(2,1)S(1)} %shrink.1), channel_id=1, replica_groups={{0,1,2,3},{4,5,6,7},{8,9,10,11},{12,13,14,15},{16,17,18,19},{20,21,22,2..., dimensions={0} | all-to-all | bytes 131072 | tf_op jit(solution)/shard_map/all_to_all | solution.py:267
  46.1 0.0 collective-permute-done.refs_1_
  46.1 0.0 collective-permute-done.1.refs_2_
  46.1 0.0 collective-permute-done.2.refs_3_
  46.1 0.0 copy-done
  46.1 2.1 %project.1 = bf16[8,160,256]{2,1,0:T(8,128)(2,1)S(1)} custom-call(s32[1]{0:T(128)} %bitcast.1.member_ref, bf16[512,128]{1,0:T(8,128)(2,1)S(1)} %bitcast.5, bf16[128,8192]{1,0:T(8,128)(2,1)S(1)} %copy-done, bf16[128,2048]{1,0:T(8,128)(2,1)} %collective-permute-done.refs_1_, bf16[128,2048]{1,0:T(8,128)(2,1)} %collective-permute-done.1.refs_2_, ...), custom_call_target="tpu_custom_call" | custom-call | tf_op jit(solution)/shard_map/project/pallas_call | solution.py:182
  48.2 25.6 %all_to_all.16.parts_ref = bf16[8,160,256]{2,1,0:T(8,128)(2,1)S(1)} all-to-all(bf16[8,160,256]{2,1,0:T(8,128)(2,1)S(1)} %project.1), channel_id=1, replica_groups={{0,4,8,12,16,20,24,28},{1,5,9,13,17,21,25,29},{2,6,10,14,18,22,26,30},{..., dimensions={0} | all-to-all | bytes 1310720 | tf_op jit(solution)/shard_map/all_to_all | solution.py:271
  73.8 0.0 copy-done.3
  73.8 1.5 %finish.1 = bf16[128,256]{1,0:T(8,128)(2,1)} custom-call(s32[16]{0:T(128)S(1)} %copy-done.6, s32[128,1]{1,0:T(8,128)S(1)} %copy.11.adapter_ref, bf16[8,160,256]{2,1,0:T(8,128)(2,1)S(1)} %all_to_all.16.parts_ref, bf16[16,64,256]{2,1,0:T(8,128)(2,1)S(1)} %copy-done.3), custom_call_target="tpu_custom_call" | custom-call | tf_op jit(solution)/shard_map/finish/pallas_call | solution.py:224
  (2 shorter events, 0.0 us)
Async XLA Ops:
  0.0 14.5 %copy-start.7 = (s32[4]{0:T(128)S(1)}, s32[4]{0:T(128)}, u32[]{:S(2)}) copy-start(s32[4]{0:T(128)} %len_ref.1) | copy-start | bytes 52
  0.0 14.5 %copy-start.1 = (bf16[4,256,512]{2,1,0:T(8,128)(2,1)S(1)}, bf16[4,256,512]{2,1,0:T(8,128)(2,1)}, u32[]{:S(2)}) copy-start(bf16[4,256,512]{2,1,0:T(8,128)(2,1)} %k_ref.1) | copy-start | bytes 3145732
  0.0 14.5 %copy-start.5 = (bf16[4,4096]{1,0:T(4,128)(2,1)S(1)}, bf16[4,4096]{1,0:T(4,128)(2,1)}, u32[]{:S(2)}) copy-start(bf16[4,4096]{1,0:T(4,128)(2,1)} %q_ref.1) | copy-start | bytes 98308
  0.0 25.4 %copy-start.8 = (s32[128]{0:T(128)S(1)}, s32[128]{0:T(128)}, u32[]{:S(2)}) copy-start(s32[128]{0:T(128)} %param.13) | copy-start | bytes 1540
  0.0 36.0 %copy-start.4 = (bf16[16,128,64]{1,2,0:T(8,128)(2,1)S(1)}, bf16[16,128,64]{1,2,0:T(8,128)(2,1)}, u32[]{:S(2)}) copy-start(bf16[16,128,64]{1,2,0:T(8,128)(2,1)} %param.16) | copy-start | bytes 786436
  0.0 36.0 %copy-start.6 = (s32[16]{0:T(128)S(1)}, s32[16]{0:T(128)}, u32[]{:S(2)}) copy-start(s32[16]{0:T(128)} %block_ref.3) | copy-start | bytes 196
  2.9 43.2 %copy-start = (bf16[128,8192]{1,0:T(8,128)(2,1)S(1)}, bf16[128,8192]{1,0:T(8,128)(2,1)}, u32[]{:S(2)}) copy-start(bf16[128,8192]{1,0:T(8,128)(2,1)} %refs_0_.1) | copy-start | bytes 6291460
  2.9 43.2 %collective-permute-start = (bf16[128,2048]{1,0:T(8,128)(2,1)}, bf16[128,2048]{1,0:T(8,128)(2,1)}, u32[]{:S(2)}, u32[]{:S(2)}) collective-permute-start(bf16[128,2048]{1,0:T(8,128)(2,1)} %get-tuple-element.8), channel_id=1, source_target_pairs={{0,1},{1,2},{2,3},{3,0},{4,5},{5,6},{6,7},{7,4},{8,9},{9,10},{10,1... | collective-permute-start | bytes 1572872 | tf_op jit(solution)/shard_map/ppermute | solution.py:260
  6.5 39.6 %collective-permute-start.1 = (bf16[128,2048]{1,0:T(8,128)(2,1)}, bf16[128,2048]{1,0:T(8,128)(2,1)}, u32[]{:S(2)}, u32[]{:S(2)}) collective-permute-start(bf16[128,2048]{1,0:T(8,128)(2,1)} %get-tuple-element.9), channel_id=1, source_target_pairs={{0,2},{1,3},{2,0},{3,1},{4,6},{5,7},{6,4},{7,5},{8,10},{9,11},{10,... | collective-permute-start | bytes 1572872 | tf_op jit(solution)/shard_map/ppermute | solution.py:260
  11.1 35.0 %collective-permute-start.2 = (bf16[128,2048]{1,0:T(8,128)(2,1)}, bf16[128,2048]{1,0:T(8,128)(2,1)}, u32[]{:S(2)}, u32[]{:S(2)}) collective-permute-start(bf16[128,2048]{1,0:T(8,128)(2,1)} %get-tuple-element.10), channel_id=1, source_target_pairs={{0,3},{1,0},{2,1},{3,2},{4,7},{5,4},{6,5},{7,6},{8,11},{9,8},{10,9... | collective-permute-start | bytes 1572872 | tf_op jit(solution)/shard_map/ppermute | solution.py:260
  14.5 1.2 %copy-start.2 = (bf16[4,256,512]{2,1,0:T(8,128)(2,1)S(1)}, bf16[4,256,512]{2,1,0:T(8,128)(2,1)}, u32[]{:S(2)}) copy-start(bf16[4,256,512]{2,1,0:T(8,128)(2,1)} %v_ref.1) | copy-start | bytes 3145732
  17.9 18.2 %all-to-all-start = ((bf16[32,16,128]{2,1,0:T(8,128)(2,1)}), bf16[32,16,128]{2,1,0:T(8,128)(2,1)S(1)}, u32[]{:S(2)}, u32[]{:S(2)}) async-start(bf16[32,16,128]{2,1,0:T(8,128)(2,1)} %attend.1), calls=%async_computation | async-start | bytes 262144 | tf_op jit(solution)/shard_map/all_to_all | solution.py:266
  46.1 27.7 %copy-start.3 = (bf16[16,64,256]{2,1,0:T(8,128)(2,1)S(1)}, bf16[16,64,256]{2,1,0:T(8,128)(2,1)}, u32[]{:S(2)}) copy-start(bf16[16,64,256]{2,1,0:T(8,128)(2,1)} %up_ref.1) | copy-start | bytes 1572868

commit v5 on v4

--- a/solution.py
+++ b/solution.py
@@ -26,40 +26,31 @@
     return q * QUAD + m
 
 
-def regroup_kernel(steps, member_ref, w_hbm, *refs):
-    *pieces, sem = refs
-    copies = []
-    for i, (step, piece) in enumerate(zip(steps, pieces)):
-        m = lax.rem(member_ref[0] + step, QUAD)
-        for q in range(piece.shape[1] // LINE):
-            first = pl.multiple_of(in_quad(q, m) * LINE, LINE)
-            copies.append(
-                pltpu.make_async_copy(
-                    w_hbm.at[:, pl.ds(first, LINE)], piece.at[:, pl.ds(q * LINE, LINE)], sem.at[i, q]
-                )
-            )
-    for copy in copies:
+def start_kernel(
+    place_ref, len_ref, q_ref, k_hbm, v_hbm, w_hbm, heads_ref, near_ref, far_ref, k_ref, v_ref, k_sem, v_sem, w_sem
+):
+    rows, size = k_ref.shape[0], HEAD_SIZE
+    k_copies = [pltpu.make_async_copy(k_hbm.at[r], k_ref.at[r], k_sem.at[r]) for r in range(rows)]
+    v_copies = [pltpu.make_async_copy(v_hbm.at[r], v_ref.at[r], v_sem.at[r]) for r in range(rows)]
+    member, core = place_ref[0] & (QUAD - 1), lax.div(place_ref[0], QUAD)
+    near = lax.rem(member + 1 + 2 * core, QUAD)
+    far = lax.rem(member + 2, QUAD)
+    depth = far_ref.shape[0]
+    half = pl.ds(pl.multiple_of(core * depth, depth), depth)
+    w_copies = []
+    for q in range(near_ref.shape[1] // LINE):
+        columns = pl.ds(q * LINE, LINE)
+        source = pl.ds(pl.multiple_of(in_quad(q, near) * LINE, LINE), LINE)
+        w_copies.append(
+            pltpu.make_async_copy(w_hbm.at[:, source], near_ref.at[:, columns], w_sem.at[0, q])
+        )
+        source = pl.ds(pl.multiple_of(in_quad(q, far) * LINE, LINE), LINE)
+        w_copies.append(
+            pltpu.make_async_copy(w_hbm.at[half, source], far_ref.at[:, columns], w_sem.at[1, q])
+        )
+    for copy in k_copies + v_copies + w_copies:
         copy.start()
-    for copy in copies:
-        copy.wait()
-
-
-def regroup(member, weight, steps):
-    depth, columns = weight.shape
-    piece = jax.ShapeDtypeStruct((depth, columns // QUAD), BF16)
-    return pl.pallas_call(
-        functools.partial(regroup_kernel, steps),
-        out_shape=(piece,) * len(steps),
-        in_specs=[SMEM, HBM],
-        out_specs=(VMEM,) * len(steps),
-        scratch_shapes=[pltpu.SemaphoreType.DMA((len(steps), columns // QUAD // LINE))],
-        compiler_params=WHOLE,
-        name="regroup",
-    )(member, weight)
-
-
-def attend_kernel(len_ref, q_ref, k_ref, v_ref, heads_ref):
-    rows, size = k_ref.shape[0], HEAD_SIZE
+
     q = q_ref[...].astype(F32)
     q_rows = jnp.concatenate(
         [q[:, h * size : (h + 1) * size] for h in range(QUERY_HEADS)], axis=0
@@ -77,6 +68,7 @@
     scores = jnp.zeros((CTX, count), F32)
     length = jnp.zeros((CTX, count), jnp.int32)
     for r in range(rows):
+        k_copies[r].wait()
         all_lanes = jnp.dot(k_ref[r], spread, preferred_element_type=F32)
         scores = jnp.where(request == r, all_lanes, scores)
         length = jnp.where(request == r, len_ref[r], length)
@@ -87,6 +79,7 @@
     owner = lax.broadcasted_iota(jnp.int32, (count, CTX), 0) % rows
     wide = jnp.zeros((count, KVH * size), F32)
     for r in range(rows):
+        v_copies[r].wait()
         mine = jnp.where(owner == r, probs, jnp.zeros_like(probs))
         wide += jnp.dot(mine, v_ref[r], preferred_element_type=F32)
     group = count // KVH
@@ -97,18 +90,30 @@
     for quad in range(QUERY_HEADS // QUAD):
         for m in range(QUAD):
             heads_ref[in_quad(quad, m)] = own[quad * span : (quad + 1) * span]
-
-
-def attend(lengths, queries, key_cache, value_cache):
+    for copy in w_copies:
+        copy.wait()
+
+
+def start(place, lengths, queries, key_cache, value_cache, weight):
     rows = queries.shape[0]
-    return pl.pallas_call(
-        attend_kernel,
-        out_shape=jax.ShapeDtypeStruct((QUERY_HEADS, QUAD * rows, HEAD_SIZE), BF16),
-        in_specs=[SMEM, VMEM, VMEM, VMEM],
-        out_specs=VMEM,
-        compiler_params=PARAMS,
-        name="attend",
-    )(lengths, queries, key_cache, value_cache)
+    depth, columns = weight.shape
+    span = columns // QUAD
+    cache = pltpu.VMEM((rows, CTX, KVH * HEAD_SIZE), BF16)
+    return pl.pallas_call(
+        start_kernel,
+        out_shape=(
+            jax.ShapeDtypeStruct((QUERY_HEADS, QUAD * rows, HEAD_SIZE), BF16),
+            jax.ShapeDtypeStruct((depth, span), BF16),
+            jax.ShapeDtypeStruct((depth // 2, span), BF16),
+        ),
+        in_specs=[SMEM, SMEM, VMEM, HBM, HBM, HBM],
+        out_specs=(VMEM,) * 3,
+        scratch_shapes=[cache, cache]
+        + [pltpu.SemaphoreType.DMA((rows,))] * 2
+        + [pltpu.SemaphoreType.DMA((2, span // LINE))],
+        compiler_params=WHOLE,
+        name="start",
+    )(place, lengths, queries, key_cache, value_cache, weight)
 
 
 def pick_rows(spans, index):
@@ -121,9 +126,9 @@
     return jnp.dot(choice, spans, preferred_element_type=F32).astype(BF16)
 
 
-def shrink_kernel(member_ref, block_ref, adapter_ref, spans_ref, down_ref, out_ref):
+def shrink_kernel(place_ref, block_ref, adapter_ref, spans_ref, down_ref, out_ref):
     half = out_ref.shape[1]
-    heads = pick_rows(spans_ref[...], member_ref[0])
+    heads = pick_rows(spans_ref[...], place_ref[0] & (QUAD - 1))
     adapter = adapter_ref[...]
     rank = down_ref.shape[1]
     shrink = jnp.zeros((heads.shape[0], rank), F32)
@@ -137,7 +142,7 @@
         out_ref[m] = packed
 
 
-def shrink_parts(member, spans, down, adapter_col, block_adapter):
+def shrink_parts(place, spans, down, adapter_col, block_adapter):
     half = spans.shape[0] // QUAD // 2
     return pl.pallas_call(
         shrink_kernel,
@@ -146,27 +151,55 @@
         out_specs=VMEM,
         compiler_params=PARAMS,
         name="shrink",
-    )(member, block_adapter, adapter_col, spans, jnp.swapaxes(down, 1, 2))
-
-
-def project_kernel(member_ref, spans_ref, *refs):
-    weight_ref, *piece_refs, shrink_ref, out_ref = refs
+    )(place, block_adapter, adapter_col, spans, jnp.swapaxes(down, 1, 2))
+
+
+def arrange_kernel(place_ref, spans_ref, out_ref):
+    spans = spans_ref[...]
+    member, core = place_ref[0] & (QUAD - 1), lax.div(place_ref[0], QUAD)
+    near, other = lax.rem(member + 3 + 2 * core, QUAD), lax.rem(member + 1 + 2 * core, QUAD)
+    size = spans.shape[1]
+    for i, block in enumerate((member, near, other)):
+        out_ref[:, i * size : (i + 1) * size] = pick_rows(spans, block)
+    opposite = pick_rows(spans, lax.rem(member + 2, QUAD))
+    turned = jnp.concatenate([opposite[:, size // 2 :], opposite[:, : size // 2]], axis=1)
+    out_ref[:, 3 * size :] = jnp.where(core == 0, opposite, turned)
+
+
+def arrange(place, spans):
+    count, size = spans.shape
+    return pl.pallas_call(
+        arrange_kernel,
+        out_shape=jax.ShapeDtypeStruct((count // QUAD, QUAD * size), BF16),
+        in_specs=[SMEM, VMEM],
+        out_specs=VMEM,
+        compiler_params=PARAMS,
+        cost_estimate=pl.CostEstimate(flops=2 * 10**10, bytes_accessed=2**18, transcendentals=0),
+        name="arrange",
+    )(place, spans)
+
+
+def project_kernel(
+    place_ref, heads_ref, weight_ref, near_ref, far_ref, other_ref, shrink_ref, out_ref
+):
     dests, _, width = out_ref.shape
-    rows = spans_ref.shape[0] // QUAD
-    spans = spans_ref[...]
-    heads = jnp.concatenate(
-        [pick_rows(spans, lax.rem(member_ref[0] + QUAD - step, QUAD)) for step in range(QUAD)],
-        axis=1,
-    )
-    place = in_quad(0, member_ref[0])
+    rows = heads_ref.shape[0]
+    heads = heads_ref[...]
+    member, depth = place_ref[0] & (QUAD - 1), far_ref.shape[0]
     for d in range(dests):
-        first = pl.multiple_of((in_quad(d, 0) + place) * width, width)
-        columns = jnp.concatenate(
-            [weight_ref[:, pl.ds(first, width)]]
-            + [ref[:, d * width : (d + 1) * width] for ref in piece_refs],
+        first = pl.multiple_of(in_quad(d, member) * width, width)
+        columns = pl.ds(d * width, width)
+        stacked = jnp.concatenate(
+            [
+                weight_ref[:, pl.ds(first, width)],
+                near_ref[:, columns],
+                other_ref[: 2 * depth, columns],
+                far_ref[:, columns],
+                other_ref[2 * depth :, columns],
+            ],
             axis=0,
         )
-        out_ref[d, :rows, :] = jnp.dot(heads, columns, preferred_element_type=F32).astype(BF16)
+        out_ref[d, :rows, :] = jnp.dot(heads, stacked, preferred_element_type=F32).astype(BF16)
     shrink = shrink_ref[0].astype(F32)
     for m in range(1, QUAD):
         shrink += shrink_ref[m].astype(F32)
@@ -176,17 +209,17 @@
         out_ref[d, rows:, :] = packed
 
 
-def project(member, spans, weight, pieces, shrinks):
-    rows = spans.shape[0] // QUAD
-    dests = pieces[0].shape[1] // LINE
+def project(place, heads, weight, near, far, other, shrinks):
+    rows = heads.shape[0]
+    dests = near.shape[1] // LINE
     return pl.pallas_call(
         project_kernel,
         out_shape=jax.ShapeDtypeStruct((dests, rows + shrinks.shape[1] // 2, LINE), BF16),
-        in_specs=[SMEM] + [VMEM] * (QUAD + 2),
+        in_specs=[SMEM] + [VMEM] * 6,
         out_specs=VMEM,
         compiler_params=PARAMS,
         name="project",
-    )(member, spans, weight, *pieces, shrinks)
+    )(place, heads, weight, near, far, other, shrinks)
 
 
 def finish_kernel(block_ref, adapter_ref, parts_ref, up_ref, out_ref):
@@ -232,6 +265,7 @@
 
 
 def per_device(
+    reps,
     devices,
     queries,
     key_cache,
@@ -251,24 +285,32 @@
     )
     rows = request_adapter.shape[0]
     adapter_col = request_adapter[:, None]
-    member = (lax.axis_index("tp") & (QUAD - 1)).astype(jnp.int32)[None]
-
-    def ahead(piece, step):
-        turn = [
-            (in_quad(q, m), in_quad(q, (m + step) % QUAD)) for q in range(quads) for m in range(QUAD)
-        ]
-        return lax.ppermute(piece, "tp", turn)
-
-    steps = range(1, QUAD)
-    weights = regroup(member, output_weight, steps)
-    weights = [ahead(piece, step) for piece, step in zip(weights, steps)]
-    own = attend(lengths, queries, key_cache, value_cache)
+    place = (lax.axis_index("tp") & (QUAD - 1)) + (lax.axis_index("rep") & 1) * QUAD
+    place = place.astype(jnp.int32)[None]
+
+    own, near, far = start(place, lengths, queries, key_cache, value_cache, output_weight)
+    near = lax.ppermute(
+        near,
+        ("rep", "tp"),
+        [
+            (r * devices + in_quad(q, m), r * devices + in_quad(q, (m + 1 + 2 * (r & 1)) % QUAD))
+            for r in range(reps)
+            for q in range(quads)
+            for m in range(QUAD)
+        ],
+    )
+    far = lax.ppermute(
+        far, "tp", [(in_quad(q, m), in_quad(q, (m + 2) % QUAD)) for q in range(quads) for m in range(QUAD)]
+    )
     spans = exchange(own).reshape(QUAD * rows, HEAD_SIZE)
-    shrinks = exchange(
-        shrink_parts(member, spans, down_factors, adapter_col, block_adapter),
-        axis_index_groups=lines,
-    )
-    parts = exchange(project(member, spans, output_weight, weights, shrinks), axis_index_groups=groups)
+    partial = shrink_parts(place, spans, down_factors, adapter_col, block_adapter)
+    shrinks = exchange(partial, axis_index_groups=lines)
+    held, _ = lax.optimization_barrier((jnp.concatenate([near, far], axis=0), partial))
+    other = lax.ppermute(held, "rep", [(r, r ^ 1) for r in range(reps)])
+    heads = arrange(place, spans)
+    parts = exchange(
+        project(place, heads, output_weight, near, far, other, shrinks), axis_index_groups=groups
+    )
     return finish(parts, up_factors, adapter_col, block_adapter, rows)
 
 
@@ -285,7 +327,7 @@
         P("rep", None, "tp"),
     )
     return jax.shard_map(
-        functools.partial(per_device, mesh.shape["tp"]),
+        functools.partial(per_device, mesh.shape["rep"], mesh.shape["tp"]),
         mesh=mesh,
         in_specs=in_specs,
         out_specs=P("rep", "tp"),

time: 75.7 us -> 70.6 us (0.933)
  the two profiles are of different devices: /device:TPU:384 before, /device:TPU:1 now
where the time goes in v5:
time: 70.6 us; the launch traced here: 70.1 us
  starting transfers between devices  24.4 us (35%)
  blocking collectives  23.3 us (33%)
  waiting for transfers between devices  11.1 us (16%)
  Pallas kernels  10.1 us (14%)
  other arithmetic  0.98 us (1%)
    all_to_all x1, blocking collectives, per_device(): exchange(project(place, heads, output_weight, near, far, other, shrinks),...  23.3 us
    all_to_all x1, starting transfers between devices, per_device(): spans = exchange(own).reshape(QUAD * rows, HEAD_SIZE)  9.39 us
    all_to_all x1, waiting for transfers between devices, per_device(): spans = exchange(own).reshape(QUAD * rows, HEAD_SIZE)  9.22 us
    ppermute x1, starting transfers between devices, per_device(): lax.ppermute(near, ('rep', 'tp'), [(r * devices + in_quad(q, m), r * devi...  5.23 us
    pallas_call x1, Pallas kernels, start(): pl.pallas_call(start_kernel, out_shape=(jax.ShapeDtypeStruct((QUERY_HEADS...  4.91 us
    ppermute x1, starting transfers between devices, per_device(): other = lax.ppermute(held, 'rep', [(r, r ^ 1) for r in range(reps)])  4.11 us
    all_to_all x1, starting transfers between devices, per_device(): shrinks = exchange(partial, axis_index_groups=lines)  3.28 us
    ppermute x1, starting transfers between devices, per_device(): lax.ppermute(far, 'tp', [(in_quad(q, m), in_quad(q, (m + 2) % QUAD)) for...  2.42 us
  transfers between devices with their start and end apart: 5, of which 2 were waited for; matrix products, arithmetic and copies ran while one was open for 2% of the time, Pallas kernels for 3%

profile of v5, /device:TPU:1, one launch (start us, length us, event | category | flops | bytes accessed | tf_op | source)
XLA Modules:
  0.0 70.1 jit_solution(6337492423211655189)
XLA Ops:
  0.0 0.0 copy-start.4
  0.0 0.0 copy-start.2
  0.0 0.0 copy-start.3
  0.0 4.9 %start.1 = (bf16[32,16,128]{2,1,0:T(8,128)(2,1)}, bf16[128,2048]{1,0:T(8,128)(2,1)}, bf16[64,2048]{1,0:T(8,128)(2,1)}) custom-call(s32[1]{0:T(128)} %bitcast.1.place_ref, s32[4]{0:T(128)} %len_ref.1, bf16[4,4096]{1,0:T(4,128)(2,1)} %q_ref.1, bf16[4,256,512]{2,1,0:T(8,128)(2,1)} %k_hbm.1, bf16[4,256,512]{2,1,0:T(8,128)(2,1)} %v_hbm.1, ...), custom_call_target="tpu_custom_call" | custom-call | tf_op jit(solution)/shard_map/start/pallas_call | solution.py:102
  4.9 5.2 %collective-permute-start = (bf16[128,2048]{1,0:T(8,128)(2,1)}, bf16[128,2048]{1,0:T(8,128)(2,1)S(1)}, u32[]{:S(2)}, u32[]{:S(2)}) collective-permute-start(bf16[128,2048]{1,0:T(8,128)(2,1)} %get-tuple-element.10), channel_id=1, source_target_pairs={{0,1},{1,2},{2,3},{3,0},{4,5},{5,6},{6,7},{7,4},{8,9},{9,10},{10,1... | collective-permute-start | bytes 1572872 | tf_op jit(solution)/shard_map/ppermute | solution.py:292
  10.2 2.4 %collective-permute-start.1 = (bf16[64,2048]{1,0:T(8,128)(2,1)}, bf16[64,2048]{1,0:T(8,128)(2,1)S(1)}, u32[]{:S(2)}, u32[]{:S(2)}) collective-permute-start(bf16[64,2048]{1,0:T(8,128)(2,1)} %get-tuple-element.11), channel_id=1, source_target_pairs={{0,2},{1,3},{2,0},{3,1},{4,6},{5,7},{6,4},{7,5},{8,10},{9,11},{10,... | collective-permute-start | bytes 786440 | tf_op jit(solution)/shard_map/ppermute | solution.py:302
  12.6 9.4 %all-to-all-start = ((bf16[32,16,128]{2,1,0:T(8,128)(2,1)}), bf16[32,16,128]{2,1,0:T(8,128)(2,1)S(1)}, u32[]{:S(2)}, u32[]{:S(2)}) async-start(bf16[32,16,128]{2,1,0:T(8,128)(2,1)} %get-tuple-element.9), calls=%async_computation | async-start | bytes 262144 | tf_op jit(solution)/shard_map/all_to_all | solution.py:305
  22.0 0.0 copy-done.4
  22.0 0.1 copy.11.adapter_ref
  22.1 9.2 %all-to-all-done = bf16[32,16,128]{2,1,0:T(8,128)(2,1)S(1)} async-done(((bf16[32,16,128]{2,1,0:T(8,128)(2,1)}), bf16[32,16,128]{2,1,0:T(8,128)(2,1)S(1)}, u32[]{:S(2)}, u32[]{:S(2)}) %all-to-all-start) | async-done | bytes 131104 | tf_op jit(solution)/shard_map/all_to_all | solution.py:305
  31.3 0.0 copy-done.2
  31.3 0.0 copy-done.3
  31.3 1.8 %shrink.1 = bf16[4,64,128]{2,1,0:T(8,128)(2,1)} custom-call(s32[1]{0:T(128)} %bitcast.1.place_ref, s32[16]{0:T(128)S(1)} %copy-done.3, s32[128,1]{1,0:T(8,128)S(1)} %copy.11.adapter_ref, bf16[512,128]{1,0:T(8,128)(2,1)S(1)} %bitcast.4, bf16[16,64,128]{2,1,0:T(8,128)(2,1)S(1)} %bitcast.6), custom_call_target="tpu_custom_call" | custom-call | tf_op jit(solution)/shard_map/shrink/pallas_call | solution.py:147
  33.1 3.3 %all-to-all-start.1 = ((bf16[4,64,128]{2,1,0:T(8,128)(2,1)}), bf16[4,64,128]{2,1,0:T(8,128)(2,1)S(1)}, u32[]{:S(2)}, u32[]{:S(2)}) async-start(bf16[4,64,128]{2,1,0:T(8,128)(2,1)} %shrink.1), calls=%async_computation.1 | async-start | bytes 131072 | tf_op jit(solution)/shard_map/all_to_all | solution.py:307
  36.4 0.0 collective-permute-done.1.far_ref
  36.4 0.0 collective-permute-done.near_ref
  36.4 1.0 %pad_maximum_fusion = bf16[192,2048]{1,0:T(8,128)(2,1)} fusion(bf16[64,2048]{1,0:T(8,128)(2,1)S(1)} %collective-permute-done.1.far_ref, bf16[128,2048]{1,0:T(8,128)(2,1)S(1)} %collective-permute-done.near_ref), kind=kLoop, calls=%fused_computation | loop fusion | flops 1572864 | bytes 1572864 | tf_op jit(solution)/shard_map/concatenate | solution.py:308
  37.4 0.0 copy-start
  37.4 4.1 %collective-permute-start.2 = (bf16[192,2048]{1,0:T(8,128)(2,1)}, bf16[192,2048]{1,0:T(8,128)(2,1)}, u32[]{:S(2)}, u32[]{:S(2)}) collective-permute-start(bf16[192,2048]{1,0:T(8,128)(2,1)} %pad_maximum_fusion), channel_id=1, source_target_pairs={{0,32},{32,0},{64,96},{96,64},{128,160},{160,128},{192,224},{224,1... | collective-permute-start | bytes 2359304 | tf_op jit(solution)/shard_map/ppermute | solution.py:309
  41.5 0.4 arrange.1.heads_ref
  41.9 0.0 all-to-all-done.1.shrink_ref
  41.9 1.9 %collective-permute-done.2.other_ref = bf16[192,2048]{1,0:T(8,128)(2,1)} collective-permute-done((bf16[192,2048]{1,0:T(8,128)(2,1)}, bf16[192,2048]{1,0:T(8,128)(2,1)}, u32[]{:S(2)}, u32[]{:S(2)}) %collective-permute-start.2) | collective-permute-done | bytes 786464 | tf_op jit(solution)/shard_map/ppermute | solution.py:309
  43.7 0.0 copy-done
  43.7 1.6 %project.1 = bf16[8,160,256]{2,1,0:T(8,128)(2,1)S(1)} custom-call(s32[1]{0:T(128)} %bitcast.1.place_ref, bf16[128,512]{1,0:T(8,128)(2,1)S(1)} %arrange.1.heads_ref, bf16[128,8192]{1,0:T(8,128)(2,1)S(1)} %copy-done, bf16[128,2048]{1,0:T(8,128)(2,1)S(1)} %collective-permute-done.near_ref, bf16[64,2048]{1,0:T(8,128)(2,1)S(1)} %collective-permute-done.1.far_ref, ...), custom_call_target="tpu_custom_call" | custom-call | tf_op jit(solution)/shard_map/project/pallas_call | solution.py:215
  45.4 0.0 copy-start.1
  45.4 23.3 %all_to_all.15.parts_ref = bf16[8,160,256]{2,1,0:T(8,128)(2,1)S(1)} all-to-all(bf16[8,160,256]{2,1,0:T(8,128)(2,1)S(1)} %project.1), channel_id=1, replica_groups={{0,4,8,12,16,20,24,28},{1,5,9,13,17,21,25,29},{2,6,10,14,18,22,26,30},{..., dimensions={0} | all-to-all | bytes 1310720 | tf_op jit(solution)/shard_map/all_to_all | solution.py:311
  68.7 0.0 copy-done.1
  68.7 1.5 %finish.1 = bf16[128,256]{1,0:T(8,128)(2,1)} custom-call(s32[16]{0:T(128)S(1)} %copy-done.3, s32[128,1]{1,0:T(8,128)S(1)} %copy.11.adapter_ref, bf16[8,160,256]{2,1,0:T(8,128)(2,1)S(1)} %all_to_all.15.parts_ref, bf16[16,64,256]{2,1,0:T(8,128)(2,1)S(1)} %copy-done.1), custom_call_target="tpu_custom_call" | custom-call | tf_op jit(solution)/shard_map/finish/pallas_call | solution.py:257
Async XLA Ops:
  0.0 22.0 %copy-start.4 = (s32[128]{0:T(128)S(1)}, s32[128]{0:T(128)}, u32[]{:S(2)}) copy-start(s32[128]{0:T(128)} %param.13) | copy-start | bytes 1540
  0.0 31.3 %copy-start.2 = (bf16[16,128,64]{1,2,0:T(8,128)(2,1)S(1)}, bf16[16,128,64]{1,2,0:T(8,128)(2,1)}, u32[]{:S(2)}) copy-start(bf16[16,128,64]{1,2,0:T(8,128)(2,1)} %param.16) | copy-start | bytes 786436
  0.0 31.3 %copy-start.3 = (s32[16]{0:T(128)S(1)}, s32[16]{0:T(128)}, u32[]{:S(2)}) copy-start(s32[16]{0:T(128)} %block_ref.3) | copy-start | bytes 196
  4.9 31.5 %collective-permute-start = (bf16[128,2048]{1,0:T(8,128)(2,1)}, bf16[128,2048]{1,0:T(8,128)(2,1)S(1)}, u32[]{:S(2)}, u32[]{:S(2)}) collective-permute-start(bf16[128,2048]{1,0:T(8,128)(2,1)} %get-tuple-element.10), channel_id=1, source_target_pairs={{0,1},{1,2},{2,3},{3,0},{4,5},{5,6},{6,7},{7,4},{8,9},{9,10},{10,1... | collective-permute-start | bytes 1572872 | tf_op jit(solution)/shard_map/ppermute | solution.py:292
  10.2 26.2 %collective-permute-start.1 = (bf16[64,2048]{1,0:T(8,128)(2,1)}, bf16[64,2048]{1,0:T(8,128)(2,1)S(1)}, u32[]{:S(2)}, u32[]{:S(2)}) collective-permute-start(bf16[64,2048]{1,0:T(8,128)(2,1)} %get-tuple-element.11), channel_id=1, source_target_pairs={{0,2},{1,3},{2,0},{3,1},{4,6},{5,7},{6,4},{7,5},{8,10},{9,11},{10,... | collective-permute-start | bytes 786440 | tf_op jit(solution)/shard_map/ppermute | solution.py:302
  12.6 18.7 %all-to-all-start = ((bf16[32,16,128]{2,1,0:T(8,128)(2,1)}), bf16[32,16,128]{2,1,0:T(8,128)(2,1)S(1)}, u32[]{:S(2)}, u32[]{:S(2)}) async-start(bf16[32,16,128]{2,1,0:T(8,128)(2,1)} %get-tuple-element.9), calls=%async_computation | async-start | bytes 262144 | tf_op jit(solution)/shard_map/all_to_all | solution.py:305
  33.1 8.8 %all-to-all-start.1 = ((bf16[4,64,128]{2,1,0:T(8,128)(2,1)}), bf16[4,64,128]{2,1,0:T(8,128)(2,1)S(1)}, u32[]{:S(2)}, u32[]{:S(2)}) async-start(bf16[4,64,128]{2,1,0:T(8,128)(2,1)} %shrink.1), calls=%async_computation.1 | async-start | bytes 131072 | tf_op jit(solution)/shard_map/all_to_all | solution.py:307
  37.4 6.4 %copy-start = (bf16[128,8192]{1,0:T(8,128)(2,1)S(1)}, bf16[128,8192]{1,0:T(8,128)(2,1)}, u32[]{:S(2)}) copy-start(bf16[128,8192]{1,0:T(8,128)(2,1)} %weight_ref.1) | copy-start | bytes 6291460
  37.4 6.3 %collective-permute-start.2 = (bf16[192,2048]{1,0:T(8,128)(2,1)}, bf16[192,2048]{1,0:T(8,128)(2,1)}, u32[]{:S(2)}, u32[]{:S(2)}) collective-permute-start(bf16[192,2048]{1,0:T(8,128)(2,1)} %pad_maximum_fusion), channel_id=1, source_target_pairs={{0,32},{32,0},{64,96},{96,64},{128,160},{160,128},{192,224},{224,1... | collective-permute-start | bytes 2359304 | tf_op jit(solution)/shard_map/ppermute | solution.py:309
  45.4 23.3 %copy-start.1 = (bf16[16,64,256]{2,1,0:T(8,128)(2,1)S(1)}, bf16[16,64,256]{2,1,0:T(8,128)(2,1)}, u32[]{:S(2)}) copy-start(bf16[16,64,256]{2,1,0:T(8,128)(2,1)} %up_ref.1) | copy-start | bytes 1572868

commit v6 on v5

--- a/solution.py
+++ b/solution.py
@@ -150,6 +150,7 @@
         in_specs=[SMEM, SMEM, VMEM, VMEM, VMEM],
         out_specs=VMEM,
         compiler_params=PARAMS,
+        cost_estimate=pl.CostEstimate(flops=10**9, bytes_accessed=2**20, transcendentals=0),
         name="shrink",
     )(place, block_adapter, adapter_col, spans, jnp.swapaxes(down, 1, 2))
 

time: 70.6 us -> 68.5 us (0.970)
  waiting for transfers between devices: 11.1 us -> 6.54 us
  starting transfers between devices: 24.4 us -> 26.9 us
    all_to_all x1, waiting for transfers between devices: 9.22 us -> 4.67 us  [per_device(): spans = exchange(own).reshape(QUAD * rows, HEAD_SIZE)]
    ppermute x1, starting transfers between devices: 2.42 us -> 4.64 us  [per_device(): lax.ppermute(far, 'tp', [(in_quad(q, m), in_quad(q, (m + 2) % QUAD)) for...]
    ppermute x1, starting transfers between devices: 4.11 us -> 6.25 us  [per_device(): other = lax.ppermute(held, 'rep', [(r, r ^ 1) for r in range(reps)])]
    all_to_all x1, starting transfers between devices: 9.39 us -> 7.49 us  [per_device(): spans = exchange(own).reshape(QUAD * rows, HEAD_SIZE)]
where the time goes in v6:
time: 68.5 us; the launch traced here: 68.1 us
  starting transfers between devices  26.9 us (39%)
  blocking collectives  23.3 us (34%)
  Pallas kernels  10.1 us (15%)
  waiting for transfers between devices  6.54 us (10%)
  other arithmetic  0.98 us (1%)
    all_to_all x1, blocking collectives, per_device(): exchange(project(place, heads, output_weight, near, far, other, shrinks),...  23.3 us
    all_to_all x1, starting transfers between devices, per_device(): spans = exchange(own).reshape(QUAD * rows, HEAD_SIZE)  7.49 us
    ppermute x1, starting transfers between devices, per_device(): other = lax.ppermute(held, 'rep', [(r, r ^ 1) for r in range(reps)])  6.25 us
    ppermute x1, starting transfers between devices, per_device(): lax.ppermute(near, ('rep', 'tp'), [(r * devices + in_quad(q, m), r * devi...  5.23 us
    pallas_call x1, Pallas kernels, start(): pl.pallas_call(start_kernel, out_shape=(jax.ShapeDtypeStruct((QUERY_HEADS...  4.91 us
    all_to_all x1, waiting for transfers between devices, per_device(): spans = exchange(own).reshape(QUAD * rows, HEAD_SIZE)  4.67 us
    ppermute x1, starting transfers between devices, per_device(): lax.ppermute(far, 'tp', [(in_quad(q, m), in_quad(q, (m + 2) % QUAD)) for...  4.64 us
    all_to_all x1, starting transfers between devices, per_device(): shrinks = exchange(partial, axis_index_groups=lines)  3.28 us
  transfers between devices with their start and end apart: 5, of which 2 were waited for; matrix products, arithmetic and copies ran while one was open for 2% of the time, Pallas kernels for 3%

profile of v6, /device:TPU:1, one launch (start us, length us, event | category | flops | bytes accessed | tf_op | source)
XLA Modules:
  0.0 68.1 jit_solution(12073277047387668938)
XLA Ops:
  0.0 0.0 copy-start.4
  0.0 0.0 copy-start.2
  0.0 0.0 copy-start.3
  0.0 4.9 %start.1 = (bf16[32,16,128]{2,1,0:T(8,128)(2,1)}, bf16[128,2048]{1,0:T(8,128)(2,1)}, bf16[64,2048]{1,0:T(8,128)(2,1)}) custom-call(s32[1]{0:T(128)} %bitcast.1.place_ref, s32[4]{0:T(128)} %len_ref.1, bf16[4,4096]{1,0:T(4,128)(2,1)} %q_ref.1, bf16[4,256,512]{2,1,0:T(8,128)(2,1)} %k_hbm.1, bf16[4,256,512]{2,1,0:T(8,128)(2,1)} %v_hbm.1, ...), custom_call_target="tpu_custom_call" | custom-call | tf_op jit(solution)/shard_map/start/pallas_call | solution.py:102
  4.9 5.2 %collective-permute-start = (bf16[128,2048]{1,0:T(8,128)(2,1)}, bf16[128,2048]{1,0:T(8,128)(2,1)S(1)}, u32[]{:S(2)}, u32[]{:S(2)}) collective-permute-start(bf16[128,2048]{1,0:T(8,128)(2,1)} %get-tuple-element.10), channel_id=1, source_target_pairs={{0,1},{1,2},{2,3},{3,0},{4,5},{5,6},{6,7},{7,4},{8,9},{9,10},{10,1... | collective-permute-start | bytes 1572872 | tf_op jit(solution)/shard_map/ppermute | solution.py:293
  10.2 7.5 %all-to-all-start = ((bf16[32,16,128]{2,1,0:T(8,128)(2,1)}), bf16[32,16,128]{2,1,0:T(8,128)(2,1)S(1)}, u32[]{:S(2)}, u32[]{:S(2)}) async-start(bf16[32,16,128]{2,1,0:T(8,128)(2,1)} %get-tuple-element.9), calls=%async_computation | async-start | bytes 262144 | tf_op jit(solution)/shard_map/all_to_all | solution.py:306
  17.7 4.6 %collective-permute-start.1 = (bf16[64,2048]{1,0:T(8,128)(2,1)}, bf16[64,2048]{1,0:T(8,128)(2,1)S(1)}, u32[]{:S(2)}, u32[]{:S(2)}) collective-permute-start(bf16[64,2048]{1,0:T(8,128)(2,1)} %get-tuple-element.11), channel_id=1, source_target_pairs={{0,2},{1,3},{2,0},{3,1},{4,6},{5,7},{6,4},{7,5},{8,10},{9,11},{10,... | collective-permute-start | bytes 786440 | tf_op jit(solution)/shard_map/ppermute | solution.py:303
  22.3 0.0 copy-done.4
  22.3 0.1 copy.11.adapter_ref
  22.4 4.7 %all-to-all-done = bf16[32,16,128]{2,1,0:T(8,128)(2,1)S(1)} async-done(((bf16[32,16,128]{2,1,0:T(8,128)(2,1)}), bf16[32,16,128]{2,1,0:T(8,128)(2,1)S(1)}, u32[]{:S(2)}, u32[]{:S(2)}) %all-to-all-start) | async-done | bytes 131104 | tf_op jit(solution)/shard_map/all_to_all | solution.py:306
  27.1 0.0 copy-done.2
  27.1 0.0 copy-done.3
  27.1 1.8 %shrink.1 = bf16[4,64,128]{2,1,0:T(8,128)(2,1)} custom-call(s32[1]{0:T(128)} %bitcast.1.place_ref, s32[16]{0:T(128)S(1)} %copy-done.2, s32[128,1]{1,0:T(8,128)S(1)} %copy.11.adapter_ref, bf16[512,128]{1,0:T(8,128)(2,1)S(1)} %bitcast.4, bf16[16,64,128]{2,1,0:T(8,128)(2,1)S(1)} %bitcast.6), custom_call_target="tpu_custom_call" | custom-call | flops 1000000000 | bytes 1048576 | tf_op jit(solution)/shard_map/shrink/pallas_call | solution.py:147
  28.9 3.3 %all-to-all-start.1 = ((bf16[4,64,128]{2,1,0:T(8,128)(2,1)}), bf16[4,64,128]{2,1,0:T(8,128)(2,1)S(1)}, u32[]{:S(2)}, u32[]{:S(2)}) async-start(bf16[4,64,128]{2,1,0:T(8,128)(2,1)} %shrink.1), calls=%async_computation.1 | async-start | bytes 131072 | tf_op jit(solution)/shard_map/all_to_all | solution.py:308
  32.2 0.0 collective-permute-done.1.far_ref
  32.2 0.0 collective-permute-done.near_ref
  32.2 1.0 %pad_maximum_fusion = bf16[192,2048]{1,0:T(8,128)(2,1)} fusion(bf16[64,2048]{1,0:T(8,128)(2,1)S(1)} %collective-permute-done.1.far_ref, bf16[128,2048]{1,0:T(8,128)(2,1)S(1)} %collective-permute-done.near_ref), kind=kLoop, calls=%fused_computation | loop fusion | flops 1572864 | bytes 1572864 | tf_op jit(solution)/shard_map/concatenate | solution.py:309
  33.2 0.0 copy-start
  33.2 6.2 %collective-permute-start.2 = (bf16[192,2048]{1,0:T(8,128)(2,1)}, bf16[192,2048]{1,0:T(8,128)(2,1)}, u32[]{:S(2)}, u32[]{:S(2)}) collective-permute-start(bf16[192,2048]{1,0:T(8,128)(2,1)} %pad_maximum_fusion), channel_id=1, source_target_pairs={{0,32},{32,0},{64,96},{96,64},{128,160},{160,128},{192,224},{224,1... | collective-permute-start | bytes 2359304 | tf_op jit(solution)/shard_map/ppermute | solution.py:310
  39.4 0.4 arrange.1.heads_ref
  39.8 0.0 all-to-all-done.1.shrink_ref
  39.8 1.9 %collective-permute-done.2.other_ref = bf16[192,2048]{1,0:T(8,128)(2,1)} collective-permute-done((bf16[192,2048]{1,0:T(8,128)(2,1)}, bf16[192,2048]{1,0:T(8,128)(2,1)}, u32[]{:S(2)}, u32[]{:S(2)}) %collective-permute-start.2) | collective-permute-done | bytes 786464 | tf_op jit(solution)/shard_map/ppermute | solution.py:310
  41.7 0.0 copy-done
  41.7 1.6 %project.1 = bf16[8,160,256]{2,1,0:T(8,128)(2,1)S(1)} custom-call(s32[1]{0:T(128)} %bitcast.1.place_ref, bf16[128,512]{1,0:T(8,128)(2,1)S(1)} %arrange.1.heads_ref, bf16[128,8192]{1,0:T(8,128)(2,1)S(1)} %copy-done, bf16[128,2048]{1,0:T(8,128)(2,1)S(1)} %collective-permute-done.near_ref, bf16[64,2048]{1,0:T(8,128)(2,1)S(1)} %collective-permute-done.1.far_ref, ...), custom_call_target="tpu_custom_call" | custom-call | tf_op jit(solution)/shard_map/project/pallas_call | solution.py:216
  43.3 0.0 copy-start.1
  43.3 23.3 %all_to_all.15.parts_ref = bf16[8,160,256]{2,1,0:T(8,128)(2,1)S(1)} all-to-all(bf16[8,160,256]{2,1,0:T(8,128)(2,1)S(1)} %project.1), channel_id=1, replica_groups={{0,4,8,12,16,20,24,28},{1,5,9,13,17,21,25,29},{2,6,10,14,18,22,26,30},{..., dimensions={0} | all-to-all | bytes 1310720 | tf_op jit(solution)/shard_map/all_to_all | solution.py:312
  66.6 0.0 copy-done.1
  66.6 1.5 %finish.1 = bf16[128,256]{1,0:T(8,128)(2,1)} custom-call(s32[16]{0:T(128)S(1)} %copy-done.2, s32[128,1]{1,0:T(8,128)S(1)} %copy.11.adapter_ref, bf16[8,160,256]{2,1,0:T(8,128)(2,1)S(1)} %all_to_all.15.parts_ref, bf16[16,64,256]{2,1,0:T(8,128)(2,1)S(1)} %copy-done.1), custom_call_target="tpu_custom_call" | custom-call | tf_op jit(solution)/shard_map/finish/pallas_call | solution.py:258
Async XLA Ops:
  0.0 22.3 %copy-start.4 = (s32[128]{0:T(128)S(1)}, s32[128]{0:T(128)}, u32[]{:S(2)}) copy-start(s32[128]{0:T(128)} %param.13) | copy-start | bytes 1540
  0.0 27.1 %copy-start.2 = (s32[16]{0:T(128)S(1)}, s32[16]{0:T(128)}, u32[]{:S(2)}) copy-start(s32[16]{0:T(128)} %block_ref.3) | copy-start | bytes 196
  0.0 27.1 %copy-start.3 = (bf16[16,128,64]{1,2,0:T(8,128)(2,1)S(1)}, bf16[16,128,64]{1,2,0:T(8,128)(2,1)}, u32[]{:S(2)}) copy-start(bf16[16,128,64]{1,2,0:T(8,128)(2,1)} %param.16) | copy-start | bytes 786436
  4.9 27.2 %collective-permute-start = (bf16[128,2048]{1,0:T(8,128)(2,1)}, bf16[128,2048]{1,0:T(8,128)(2,1)S(1)}, u32[]{:S(2)}, u32[]{:S(2)}) collective-permute-start(bf16[128,2048]{1,0:T(8,128)(2,1)} %get-tuple-element.10), channel_id=1, source_target_pairs={{0,1},{1,2},{2,3},{3,0},{4,5},{5,6},{6,7},{7,4},{8,9},{9,10},{10,1... | collective-permute-start | bytes 1572872 | tf_op jit(solution)/shard_map/ppermute | solution.py:293
  10.2 16.9 %all-to-all-start = ((bf16[32,16,128]{2,1,0:T(8,128)(2,1)}), bf16[32,16,128]{2,1,0:T(8,128)(2,1)S(1)}, u32[]{:S(2)}, u32[]{:S(2)}) async-start(bf16[32,16,128]{2,1,0:T(8,128)(2,1)} %get-tuple-element.9), calls=%async_computation | async-start | bytes 262144 | tf_op jit(solution)/shard_map/all_to_all | solution.py:306
  17.7 14.5 %collective-permute-start.1 = (bf16[64,2048]{1,0:T(8,128)(2,1)}, bf16[64,2048]{1,0:T(8,128)(2,1)S(1)}, u32[]{:S(2)}, u32[]{:S(2)}) collective-permute-start(bf16[64,2048]{1,0:T(8,128)(2,1)} %get-tuple-element.11), channel_id=1, source_target_pairs={{0,2},{1,3},{2,0},{3,1},{4,6},{5,7},{6,4},{7,5},{8,10},{9,11},{10,... | collective-permute-start | bytes 786440 | tf_op jit(solution)/shard_map/ppermute | solution.py:303
  28.9 10.9 %all-to-all-start.1 = ((bf16[4,64,128]{2,1,0:T(8,128)(2,1)}), bf16[4,64,128]{2,1,0:T(8,128)(2,1)S(1)}, u32[]{:S(2)}, u32[]{:S(2)}) async-start(bf16[4,64,128]{2,1,0:T(8,128)(2,1)} %shrink.1), calls=%async_computation.1 | async-start | bytes 131072 | tf_op jit(solution)/shard_map/all_to_all | solution.py:308
  33.2 8.5 %copy-start = (bf16[128,8192]{1,0:T(8,128)(2,1)S(1)}, bf16[128,8192]{1,0:T(8,128)(2,1)}, u32[]{:S(2)}) copy-start(bf16[128,8192]{1,0:T(8,128)(2,1)} %weight_ref.1) | copy-start | bytes 6291460
  33.2 8.5 %collective-permute-start.2 = (bf16[192,2048]{1,0:T(8,128)(2,1)}, bf16[192,2048]{1,0:T(8,128)(2,1)}, u32[]{:S(2)}, u32[]{:S(2)}) collective-permute-start(bf16[192,2048]{1,0:T(8,128)(2,1)} %pad_maximum_fusion), channel_id=1, source_target_pairs={{0,32},{32,0},{64,96},{96,64},{128,160},{160,128},{192,224},{224,1... | collective-permute-start | bytes 2359304 | tf_op jit(solution)/shard_map/ppermute | solution.py:310
  43.3 23.3 %copy-start.1 = (bf16[16,64,256]{2,1,0:T(8,128)(2,1)S(1)}, bf16[16,64,256]{2,1,0:T(8,128)(2,1)}, u32[]{:S(2)}) copy-start(bf16[16,64,256]{2,1,0:T(8,128)(2,1)} %up_ref.1) | copy-start | bytes 1572868

commit v7 on v5

--- a/solution.py
+++ b/solution.py
@@ -126,12 +126,17 @@
     return jnp.dot(choice, spans, preferred_element_type=F32).astype(BF16)
 
 
-def shrink_kernel(place_ref, block_ref, adapter_ref, spans_ref, down_ref, out_ref):
+def shrink_kernel(
+    place_ref, block_ref, adapter_ref, spans_ref, down_hbm, out_ref, down_ref, down_sem
+):
+    down_copy = pltpu.make_async_copy(down_hbm, down_ref, down_sem)
+    down_copy.start()
     half = out_ref.shape[1]
     heads = pick_rows(spans_ref[...], place_ref[0] & (QUAD - 1))
     adapter = adapter_ref[...]
     rank = down_ref.shape[1]
     shrink = jnp.zeros((heads.shape[0], rank), F32)
+    down_copy.wait()
     for b in range(down_ref.shape[0]):
         mine = jnp.where(adapter == block_ref[b], heads, jnp.zeros_like(heads))
         shrink += lax.dot_general(
@@ -144,14 +149,17 @@
 
 def shrink_parts(place, spans, down, adapter_col, block_adapter):
     half = spans.shape[0] // QUAD // 2
+    down = jnp.swapaxes(down, 1, 2)
     return pl.pallas_call(
         shrink_kernel,
-        out_shape=jax.ShapeDtypeStruct((QUAD, half, 2 * down.shape[2]), BF16),
-        in_specs=[SMEM, SMEM, VMEM, VMEM, VMEM],
-        out_specs=VMEM,
-        compiler_params=PARAMS,
+        out_shape=jax.ShapeDtypeStruct((QUAD, half, 2 * down.shape[1]), BF16),
+        in_specs=[SMEM, SMEM, VMEM, VMEM, HBM],
+        out_specs=VMEM,
+        scratch_shapes=[pltpu.VMEM(down.shape, BF16), pltpu.SemaphoreType.DMA],
+        compiler_params=PARAMS,
+        cost_estimate=pl.CostEstimate(flops=6*10**9, bytes_accessed=2**20, transcendentals=0),
         name="shrink",
-    )(place, block_adapter, adapter_col, spans, jnp.swapaxes(down, 1, 2))
+    )(place, block_adapter, adapter_col, spans, down)
 
 
 def arrange_kernel(place_ref, spans_ref, out_ref):
@@ -180,15 +188,31 @@
 
 
 def project_kernel(
-    place_ref, heads_ref, weight_ref, near_ref, far_ref, other_ref, shrink_ref, out_ref
+    place_ref, heads_ref, weight_ref, near_ref, far_ref, other_hbm, shrink_ref, out_ref, other_ref, sem
 ):
     dests, _, width = out_ref.shape
+    copies = []
+    for d in range(dests):
+        columns = pl.ds(d * width, width)
+        copies.append(
+            pltpu.make_async_copy(other_hbm.at[:, columns], other_ref.at[:, columns], sem.at[d])
+        )
+    for copy in copies:
+        copy.start()
     rows = heads_ref.shape[0]
     heads = heads_ref[...]
     member, depth = place_ref[0] & (QUAD - 1), far_ref.shape[0]
+    shrink = shrink_ref[0].astype(F32)
+    for m in range(1, QUAD):
+        shrink += shrink_ref[m].astype(F32)
+    half = shrink.shape[0] // 2
+    packed = jnp.concatenate([shrink[:half], shrink[half:]], axis=1).astype(BF16)
+    for d in range(dests):
+        out_ref[d, rows:, :] = packed
     for d in range(dests):
         first = pl.multiple_of(in_quad(d, member) * width, width)
         columns = pl.ds(d * width, width)
+        copies[d].wait()
         stacked = jnp.concatenate(
             [
                 weight_ref[:, pl.ds(first, width)],
@@ -200,13 +224,6 @@
             axis=0,
         )
         out_ref[d, :rows, :] = jnp.dot(heads, stacked, preferred_element_type=F32).astype(BF16)
-    shrink = shrink_ref[0].astype(F32)
-    for m in range(1, QUAD):
-        shrink += shrink_ref[m].astype(F32)
-    half = shrink.shape[0] // 2
-    packed = jnp.concatenate([shrink[:half], shrink[half:]], axis=1).astype(BF16)
-    for d in range(dests):
-        out_ref[d, rows:, :] = packed
 
 
 def project(place, heads, weight, near, far, other, shrinks):
@@ -215,14 +232,36 @@
     return pl.pallas_call(
         project_kernel,
         out_shape=jax.ShapeDtypeStruct((dests, rows + shrinks.shape[1] // 2, LINE), BF16),
-        in_specs=[SMEM] + [VMEM] * 6,
-        out_specs=VMEM,
+        in_specs=[SMEM] + [VMEM] * 4 + [HBM, VMEM],
+        out_specs=VMEM,
+        scratch_shapes=[pltpu.VMEM(other.shape, BF16), pltpu.SemaphoreType.DMA((dests,))],
         compiler_params=PARAMS,
         name="project",
     )(place, heads, weight, near, far, other, shrinks)
 
 
-def finish_kernel(block_ref, adapter_ref, parts_ref, up_ref, out_ref):
+def mask_kernel(block_ref, adapter_ref, out_ref):
+    rank = out_ref.shape[1] // block_ref.shape[0]
+    adapter = adapter_ref[...]
+    left = lax.broadcasted_iota(jnp.int32, (out_ref.shape[0], 2 * rank), 1) < rank
+    for b in range(0, block_ref.shape[0], 2):
+        match = jnp.where(left, block_ref[b], block_ref[b + 1]) == adapter
+        out_ref[:, b * rank : (b + 2) * rank] = jnp.where(match, 1.0, 0.0).astype(BF16)
+
+
+def mask(adapter_col, block_adapter, rank):
+    return pl.pallas_call(
+        mask_kernel,
+        out_shape=jax.ShapeDtypeStruct((adapter_col.shape[0], block_adapter.shape[0] * rank), BF16),
+        in_specs=[SMEM, VMEM],
+        out_specs=VMEM,
+        compiler_params=PARAMS,
+        cost_estimate=pl.CostEstimate(flops=2 * 10**10, bytes_accessed=2**18, transcendentals=0),
+        name="mask",
+    )(block_adapter, adapter_col)
+
+
+def finish_kernel(mask_ref, parts_ref, up_ref, out_ref):
     count = parts_ref.shape[0]
     rows, width = out_ref.shape
     blocks, rank, _ = up_ref.shape
@@ -236,14 +275,9 @@
     low_rank = jnp.concatenate(
         [jnp.where(left, pair, turned), jnp.where(left, turned, pair)], axis=0
     )
-    adapter = adapter_ref[...]
-    wide_left = lax.broadcasted_iota(jnp.int32, (rows, lanes), 1) < rank
-    spread = []
-    for b in range(0, blocks, 2):
-        match = jnp.where(wide_left, block_ref[b], block_ref[b + 1]) == adapter
-        spread.append(jnp.where(match, low_rank, 0.0).astype(BF16))
+    wide = jnp.concatenate([low_rank.astype(BF16)] * (blocks // 2), axis=1)
     lora = jnp.dot(
-        jnp.concatenate(spread, axis=1),
+        wide * mask_ref[...],
         up_ref[...].reshape(blocks * rank, width),
         preferred_element_type=F32,
     )
@@ -253,15 +287,15 @@
     out_ref[...] = (total + lora).astype(BF16)
 
 
-def finish(parts, up, adapter_col, block_adapter, rows):
+def finish(parts, up, chosen):
     return pl.pallas_call(
         finish_kernel,
-        out_shape=jax.ShapeDtypeStruct((rows, parts.shape[2]), BF16),
-        in_specs=[SMEM, VMEM, VMEM, VMEM],
+        out_shape=jax.ShapeDtypeStruct((chosen.shape[0], parts.shape[2]), BF16),
+        in_specs=[VMEM] * 3,
         out_specs=VMEM,
         compiler_params=PARAMS,
         name="finish",
-    )(block_adapter, adapter_col, parts, up)
+    )(chosen, parts, up)
 
 
 def per_device(
@@ -311,7 +345,8 @@
     parts = exchange(
         project(place, heads, output_weight, near, far, other, shrinks), axis_index_groups=groups
     )
-    return finish(parts, up_factors, adapter_col, block_adapter, rows)
+    chosen = mask(adapter_col, block_adapter, up_factors.shape[1])
+    return finish(parts, up_factors, chosen)
 
 
 def solution(mesh):

time: 70.6 us -> 73.6 us (1.042)
  blocking collectives: 23.3 us -> 0 us
  waiting for transfers between devices: 11.1 us -> 26.9 us
  starting transfers between devices: 24.4 us -> 32.6 us
  Pallas kernels: 10.1 us -> 12.4 us
    all_to_all x1 -> x0, blocking collectives: 23.3 us -> none  [per_device(): exchange(project(place, heads, output_weight, near, far, other, shrinks),...]
    all_to_all x0 -> x1, waiting for transfers between devices: none -> 20.1 us  [per_device(): exchange(project(place, heads, output_weight, near, far, other, shrinks),...]
    all_to_all x1, waiting for transfers between devices: 9.22 us -> 2.38 us  [per_device(): spans = exchange(own).reshape(QUAD * rows, HEAD_SIZE)]
    all_to_all x0 -> x1, starting transfers between devices: none -> 6.1 us  [per_device(): exchange(project(place, heads, output_weight, near, far, other, shrinks),...]
    pallas_call x1, Pallas kernels: 1.62 us -> 3.59 us  [project(): pl.pallas_call(project_kernel, out_shape=jax.ShapeDtypeStruct((dests, row...]
    ppermute x1, starting transfers between devices: 4.11 us -> 5.89 us  [per_device(): other = lax.ppermute(held, 'rep', [(r, r ^ 1) for r in range(reps)])]
    ppermute x1, waiting for transfers between devices: 0.01 us -> 1.5 us  [per_device(): lax.ppermute(far, 'tp', [(in_quad(q, m), in_quad(q, (m + 2) % QUAD)) for...]
    all_to_all x1, starting transfers between devices: 9.39 us -> 10.5 us  [per_device(): spans = exchange(own).reshape(QUAD * rows, HEAD_SIZE)]
  transfers between devices with their start and end apart: 5 -> 6, of which waited for: 2 -> 5; matrix products, arithmetic and copies ran while one was open for 2% -> 1% of each run, Pallas kernels for 3% -> 4%
where the time goes in v7:
time: 73.6 us; the launch traced here: 73.1 us
  starting transfers between devices  32.6 us (44%)
  waiting for transfers between devices  26.9 us (37%)
  Pallas kernels  12.4 us (17%)
  other arithmetic  0.98 us (1%)
    all_to_all x1, waiting for transfers between devices, per_device(): exchange(project(place, heads, output_weight, near, far, other, shrinks),...  20.1 us
    all_to_all x1, starting transfers between devices, per_device(): spans = exchange(own).reshape(QUAD * rows, HEAD_SIZE)  10.5 us
    all_to_all x1, starting transfers between devices, per_device(): exchange(project(place, heads, output_weight, near, far, other, shrinks),...  6.1 us
    ppermute x1, starting transfers between devices, per_device(): other = lax.ppermute(held, 'rep', [(r, r ^ 1) for r in range(reps)])  5.89 us
    pallas_call x1, Pallas kernels, start(): pl.pallas_call(start_kernel, out_shape=(jax.ShapeDtypeStruct((QUERY_HEADS...  4.92 us
    ppermute x1, starting transfers between devices, per_device(): lax.ppermute(near, ('rep', 'tp'), [(r * devices + in_quad(q, m), r * devi...  4.35 us
    pallas_call x1, Pallas kernels, project(): pl.pallas_call(project_kernel, out_shape=jax.ShapeDtypeStruct((dests, row...  3.59 us
    all_to_all x1, starting transfers between devices, per_device(): shrinks = exchange(partial, axis_index_groups=lines)  3.3 us
  transfers between devices with their start and end apart: 6, of which 5 were waited for; matrix products, arithmetic and copies ran while one was open for 1% of the time, Pallas kernels for 4%

profile of v7, /device:TPU:1, one launch (start us, length us, event | category | flops | bytes accessed | tf_op | source)
XLA Modules:
  0.0 73.1 jit_solution(17883084960599012925)
XLA Ops:
  0.0 0.0 copy-start.4
  0.0 0.0 copy-start.2
  0.0 0.0 copy-start.3
  0.0 4.9 %start.1 = (bf16[32,16,128]{2,1,0:T(8,128)(2,1)}, bf16[128,2048]{1,0:T(8,128)(2,1)}, bf16[64,2048]{1,0:T(8,128)(2,1)}) custom-call(s32[1]{0:T(128)} %bitcast.1.place_ref, s32[4]{0:T(128)} %len_ref.1, bf16[4,4096]{1,0:T(4,128)(2,1)} %q_ref.1, bf16[4,256,512]{2,1,0:T(8,128)(2,1)} %k_hbm.1, bf16[4,256,512]{2,1,0:T(8,128)(2,1)} %v_hbm.1, ...), custom_call_target="tpu_custom_call" | custom-call | tf_op jit(solution)/shard_map/start/pallas_call | solution.py:102
  4.9 10.5 %all-to-all-start = ((bf16[32,16,128]{2,1,0:T(8,128)(2,1)}), bf16[32,16,128]{2,1,0:T(8,128)(2,1)S(1)}, u32[]{:S(2)}, u32[]{:S(2)}) async-start(bf16[32,16,128]{2,1,0:T(8,128)(2,1)} %get-tuple-element.9), calls=%async_computation | async-start | bytes 262144 | tf_op jit(solution)/shard_map/all_to_all | solution.py:339
  15.5 4.3 %collective-permute-start = (bf16[128,2048]{1,0:T(8,128)(2,1)}, bf16[128,2048]{1,0:T(8,128)(2,1)S(1)}, u32[]{:S(2)}, u32[]{:S(2)}) collective-permute-start(bf16[128,2048]{1,0:T(8,128)(2,1)} %get-tuple-element.10), channel_id=1, source_target_pairs={{0,1},{1,2},{2,3},{3,0},{4,5},{5,6},{6,7},{7,4},{8,9},{9,10},{10,1... | collective-permute-start | bytes 1572872 | tf_op jit(solution)/shard_map/ppermute | solution.py:326
  19.8 2.5 %collective-permute-start.1 = (bf16[64,2048]{1,0:T(8,128)(2,1)}, bf16[64,2048]{1,0:T(8,128)(2,1)S(1)}, u32[]{:S(2)}, u32[]{:S(2)}) collective-permute-start(bf16[64,2048]{1,0:T(8,128)(2,1)} %get-tuple-element.11), channel_id=1, source_target_pairs={{0,2},{1,3},{2,0},{3,1},{4,6},{5,7},{6,4},{7,5},{8,10},{9,11},{10,... | collective-permute-start | bytes 786440 | tf_op jit(solution)/shard_map/ppermute | solution.py:336
  22.3 0.0 copy-done.4
  22.3 0.1 copy.10.adapter_ref
  22.4 2.4 %all-to-all-done = bf16[32,16,128]{2,1,0:T(8,128)(2,1)S(1)} async-done(((bf16[32,16,128]{2,1,0:T(8,128)(2,1)}), bf16[32,16,128]{2,1,0:T(8,128)(2,1)S(1)}, u32[]{:S(2)}, u32[]{:S(2)}) %all-to-all-start) | async-done | bytes 131104 | tf_op jit(solution)/shard_map/all_to_all | solution.py:339
  24.8 0.0 copy-done.2
  24.8 0.0 copy-done.3
  24.8 1.9 %shrink.1 = bf16[4,64,128]{2,1,0:T(8,128)(2,1)} custom-call(s32[1]{0:T(128)} %bitcast.1.place_ref, s32[16]{0:T(128)S(1)} %copy-done.3, s32[128,1]{1,0:T(8,128)S(1)} %copy.10.adapter_ref, bf16[512,128]{1,0:T(8,128)(2,1)S(1)} %bitcast.4, bf16[16,64,128]{2,1,0:T(8,128)(2,1)S(1)} %bitcast.6), custom_call_target="tpu_custom_call" | custom-call | flops 6000000000 | bytes 1048576 | tf_op jit(solution)/shard_map/shrink/pallas_call | solution.py:153
  26.8 3.3 %all-to-all-start.1 = ((bf16[4,64,128]{2,1,0:T(8,128)(2,1)}), bf16[4,64,128]{2,1,0:T(8,128)(2,1)S(1)}, u32[]{:S(2)}, u32[]{:S(2)}) async-start(bf16[4,64,128]{2,1,0:T(8,128)(2,1)} %shrink.1), calls=%async_computation.1 | async-start | bytes 131072 | tf_op jit(solution)/shard_map/all_to_all | solution.py:341
  30.1 1.5 %collective-permute-done.1.far_ref = bf16[64,2048]{1,0:T(8,128)(2,1)S(1)} collective-permute-done((bf16[64,2048]{1,0:T(8,128)(2,1)}, bf16[64,2048]{1,0:T(8,128)(2,1)S(1)}, u32[]{:S(2)}, u32[]{:S(2)}) %collective-permute-start.1) | collective-permute-done | bytes 262176 | tf_op jit(solution)/shard_map/ppermute | solution.py:336
  31.6 1.1 %collective-permute-done.near_ref = bf16[128,2048]{1,0:T(8,128)(2,1)S(1)} collective-permute-done((bf16[128,2048]{1,0:T(8,128)(2,1)}, bf16[128,2048]{1,0:T(8,128)(2,1)S(1)}, u32[]{:S(2)}, u32[]{:S(2)}) %collective-permute-start) | collective-permute-done | bytes 524320 | tf_op jit(solution)/shard_map/ppermute | solution.py:326
  32.6 1.0 %pad_maximum_fusion = bf16[192,2048]{1,0:T(8,128)(2,1)} fusion(bf16[64,2048]{1,0:T(8,128)(2,1)S(1)} %collective-permute-done.1.far_ref, bf16[128,2048]{1,0:T(8,128)(2,1)S(1)} %collective-permute-done.near_ref), kind=kLoop, calls=%fused_computation | loop fusion | flops 1572864 | bytes 1572864 | tf_op jit(solution)/shard_map/concatenate | solution.py:342
  33.6 0.0 copy-start
  33.6 5.9 %collective-permute-start.2 = (bf16[192,2048]{1,0:T(8,128)(2,1)}, bf16[192,2048]{1,0:T(8,128)(2,1)}, u32[]{:S(2)}, u32[]{:S(2)}) collective-permute-start(bf16[192,2048]{1,0:T(8,128)(2,1)} %pad_maximum_fusion), channel_id=1, source_target_pairs={{0,32},{32,0},{64,96},{96,64},{128,160},{160,128},{192,224},{224,1... | collective-permute-start | bytes 2359304 | tf_op jit(solution)/shard_map/ppermute | solution.py:343
  39.5 0.4 arrange.1.heads_ref
  39.9 0.0 all-to-all-done.1.shrink_ref
  39.9 1.9 %collective-permute-done.2.other_hbm = bf16[192,2048]{1,0:T(8,128)(2,1)} collective-permute-done((bf16[192,2048]{1,0:T(8,128)(2,1)}, bf16[192,2048]{1,0:T(8,128)(2,1)}, u32[]{:S(2)}, u32[]{:S(2)}) %collective-permute-start.2) | collective-permute-done | bytes 786464 | tf_op jit(solution)/shard_map/ppermute | solution.py:343
  41.8 0.0 copy-done
  41.8 3.6 %project.1 = bf16[8,160,256]{2,1,0:T(8,128)(2,1)} custom-call(s32[1]{0:T(128)} %bitcast.1.place_ref, bf16[128,512]{1,0:T(8,128)(2,1)S(1)} %arrange.1.heads_ref, bf16[128,8192]{1,0:T(8,128)(2,1)S(1)} %copy-done, bf16[128,2048]{1,0:T(8,128)(2,1)S(1)} %collective-permute-done.near_ref, bf16[64,2048]{1,0:T(8,128)(2,1)S(1)} %collective-permute-done.1.far_ref, ...), custom_call_target="tpu_custom_call" | custom-call | tf_op jit(solution)/shard_map/project/pallas_call | solution.py:232
  45.4 6.1 %all-to-all-start.2 = ((bf16[8,160,256]{2,1,0:T(8,128)(2,1)}), bf16[8,160,256]{2,1,0:T(8,128)(2,1)S(1)}, u32[]{:S(2)}, u32[]{:S(2)}) async-start(bf16[8,160,256]{2,1,0:T(8,128)(2,1)} %project.1), calls=%async_computation.2 | async-start | bytes 1310720 | tf_op jit(solution)/shard_map/all_to_all | solution.py:345
  51.5 0.0 copy-start.1
  51.5 0.7 mask.1.mask_ref
  52.1 20.1 %all-to-all-done.2.parts_ref = bf16[8,160,256]{2,1,0:T(8,128)(2,1)S(1)} async-done(((bf16[8,160,256]{2,1,0:T(8,128)(2,1)}), bf16[8,160,256]{2,1,0:T(8,128)(2,1)S(1)}, u32[]{:S(2)}, u32[]{:S(2)}) %all-to-all-start.2) | async-done | bytes 655392 | tf_op jit(solution)/shard_map/all_to_all | solution.py:345
  72.2 0.0 copy-done.1
  72.2 0.9 %finish.1 = bf16[128,256]{1,0:T(8,128)(2,1)} custom-call(bf16[128,1024]{1,0:T(8,128)(2,1)S(1)} %mask.1.mask_ref, bf16[8,160,256]{2,1,0:T(8,128)(2,1)S(1)} %all-to-all-done.2.parts_ref, bf16[16,64,256]{2,1,0:T(8,128)(2,1)S(1)} %copy-done.1), custom_call_target="tpu_custom_call" | custom-call | tf_op jit(solution)/shard_map/finish/pallas_call | solution.py:291
Async XLA Ops:
  0.0 22.3 %copy-start.4 = (s32[128]{0:T(128)S(1)}, s32[128]{0:T(128)}, u32[]{:S(2)}) copy-start(s32[128]{0:T(128)} %param.13) | copy-start | bytes 1540
  0.0 24.8 %copy-start.2 = (bf16[16,128,64]{1,2,0:T(8,128)(2,1)S(1)}, bf16[16,128,64]{1,2,0:T(8,128)(2,1)}, u32[]{:S(2)}) copy-start(bf16[16,128,64]{1,2,0:T(8,128)(2,1)} %param.16) | copy-start | bytes 786436
  0.0 24.8 %copy-start.3 = (s32[16]{0:T(128)S(1)}, s32[16]{0:T(128)}, u32[]{:S(2)}) copy-start(s32[16]{0:T(128)} %block_ref.3) | copy-start | bytes 196
  4.9 19.9 %all-to-all-start = ((bf16[32,16,128]{2,1,0:T(8,128)(2,1)}), bf16[32,16,128]{2,1,0:T(8,128)(2,1)S(1)}, u32[]{:S(2)}, u32[]{:S(2)}) async-start(bf16[32,16,128]{2,1,0:T(8,128)(2,1)} %get-tuple-element.9), calls=%async_computation | async-start | bytes 262144 | tf_op jit(solution)/shard_map/all_to_all | solution.py:339
  15.5 17.2 %collective-permute-start = (bf16[128,2048]{1,0:T(8,128)(2,1)}, bf16[128,2048]{1,0:T(8,128)(2,1)S(1)}, u32[]{:S(2)}, u32[]{:S(2)}) collective-permute-start(bf16[128,2048]{1,0:T(8,128)(2,1)} %get-tuple-element.10), channel_id=1, source_target_pairs={{0,1},{1,2},{2,3},{3,0},{4,5},{5,6},{6,7},{7,4},{8,9},{9,10},{10,1... | collective-permute-start | bytes 1572872 | tf_op jit(solution)/shard_map/ppermute | solution.py:326
  19.8 11.7 %collective-permute-start.1 = (bf16[64,2048]{1,0:T(8,128)(2,1)}, bf16[64,2048]{1,0:T(8,128)(2,1)S(1)}, u32[]{:S(2)}, u32[]{:S(2)}) collective-permute-start(bf16[64,2048]{1,0:T(8,128)(2,1)} %get-tuple-element.11), channel_id=1, source_target_pairs={{0,2},{1,3},{2,0},{3,1},{4,6},{5,7},{6,4},{7,5},{8,10},{9,11},{10,... | collective-permute-start | bytes 786440 | tf_op jit(solution)/shard_map/ppermute | solution.py:336
  26.8 13.1 %all-to-all-start.1 = ((bf16[4,64,128]{2,1,0:T(8,128)(2,1)}), bf16[4,64,128]{2,1,0:T(8,128)(2,1)S(1)}, u32[]{:S(2)}, u32[]{:S(2)}) async-start(bf16[4,64,128]{2,1,0:T(8,128)(2,1)} %shrink.1), calls=%async_computation.1 | async-start | bytes 131072 | tf_op jit(solution)/shard_map/all_to_all | solution.py:341
  33.6 8.1 %copy-start = (bf16[128,8192]{1,0:T(8,128)(2,1)S(1)}, bf16[128,8192]{1,0:T(8,128)(2,1)}, u32[]{:S(2)}) copy-start(bf16[128,8192]{1,0:T(8,128)(2,1)} %weight_ref.1) | copy-start | bytes 6291460
  33.6 8.1 %collective-permute-start.2 = (bf16[192,2048]{1,0:T(8,128)(2,1)}, bf16[192,2048]{1,0:T(8,128)(2,1)}, u32[]{:S(2)}, u32[]{:S(2)}) collective-permute-start(bf16[192,2048]{1,0:T(8,128)(2,1)} %pad_maximum_fusion), channel_id=1, source_target_pairs={{0,32},{32,0},{64,96},{96,64},{128,160},{160,128},{192,224},{224,1... | collective-permute-start | bytes 2359304 | tf_op jit(solution)/shard_map/ppermute | solution.py:343
  45.4 26.9 %all-to-all-start.2 = ((bf16[8,160,256]{2,1,0:T(8,128)(2,1)}), bf16[8,160,256]{2,1,0:T(8,128)(2,1)S(1)}, u32[]{:S(2)}, u32[]{:S(2)}) async-start(bf16[8,160,256]{2,1,0:T(8,128)(2,1)} %project.1), calls=%async_computation.2 | async-start | bytes 1310720 | tf_op jit(solution)/shard_map/all_to_all | solution.py:345
  51.5 20.8 %copy-start.1 = (bf16[16,64,256]{2,1,0:T(8,128)(2,1)S(1)}, bf16[16,64,256]{2,1,0:T(8,128)(2,1)}, u32[]{:S(2)}) copy-start(bf16[16,64,256]{2,1,0:T(8,128)(2,1)} %up_ref.1) | copy-start | bytes 1572868

commit v8 on v6

--- a/solution.py
+++ b/solution.py
@@ -146,13 +146,41 @@
     half = spans.shape[0] // QUAD // 2
     return pl.pallas_call(
         shrink_kernel,
-        out_shape=jax.ShapeDtypeStruct((QUAD, half, 2 * down.shape[2]), BF16),
+        out_shape=jax.ShapeDtypeStruct((QUAD, half, 2 * down.shape[1]), BF16),
         in_specs=[SMEM, SMEM, VMEM, VMEM, VMEM],
         out_specs=VMEM,
         compiler_params=PARAMS,
         cost_estimate=pl.CostEstimate(flops=10**9, bytes_accessed=2**20, transcendentals=0),
         name="shrink",
-    )(place, block_adapter, adapter_col, spans, jnp.swapaxes(down, 1, 2))
+    )(place, block_adapter, adapter_col, spans, down)
+
+
+def prepare_kernel(block_ref, adapter_ref, down_hbm, mask_ref, down_ref, sem):
+    copy = pltpu.make_async_copy(down_hbm, down_ref, sem)
+    copy.start()
+    rank = mask_ref.shape[1] // block_ref.shape[0]
+    adapter = adapter_ref[...]
+    left = lax.broadcasted_iota(jnp.int32, (mask_ref.shape[0], 2 * rank), 1) < rank
+    for b in range(0, block_ref.shape[0], 2):
+        match = jnp.where(left, block_ref[b], block_ref[b + 1]) == adapter
+        mask_ref[:, b * rank : (b + 2) * rank] = jnp.where(match, 1.0, 0.0).astype(BF16)
+    copy.wait()
+
+
+def prepare(adapter_col, block_adapter, down):
+    rows, (blocks, rank, _) = adapter_col.shape[0], down.shape
+    return pl.pallas_call(
+        prepare_kernel,
+        out_shape=(
+            jax.ShapeDtypeStruct((rows, blocks * rank), BF16),
+            jax.ShapeDtypeStruct(down.shape, BF16),
+        ),
+        in_specs=[SMEM, VMEM, HBM],
+        out_specs=(VMEM, VMEM),
+        scratch_shapes=[pltpu.SemaphoreType.DMA],
+        compiler_params=PARAMS,
+        name="prepare",
+    )(block_adapter, adapter_col, down)
 
 
 def arrange_kernel(place_ref, spans_ref, out_ref):
@@ -181,22 +209,22 @@
 
 
 def project_kernel(
-    place_ref, heads_ref, weight_ref, near_ref, far_ref, other_ref, shrink_ref, out_ref
+    place_ref, heads_ref, weight_ref, held_ref, other_ref, shrink_ref, out_ref
 ):
     dests, _, width = out_ref.shape
     rows = heads_ref.shape[0]
     heads = heads_ref[...]
-    member, depth = place_ref[0] & (QUAD - 1), far_ref.shape[0]
+    member, depth = place_ref[0] & (QUAD - 1), weight_ref.shape[0]
     for d in range(dests):
         first = pl.multiple_of(in_quad(d, member) * width, width)
         columns = pl.ds(d * width, width)
         stacked = jnp.concatenate(
             [
                 weight_ref[:, pl.ds(first, width)],
-                near_ref[:, columns],
-                other_ref[: 2 * depth, columns],
-                far_ref[:, columns],
-                other_ref[2 * depth :, columns],
+                held_ref[:depth, columns],
+                other_ref[:depth, columns],
+                held_ref[depth:, columns],
+                other_ref[depth:, columns],
             ],
             axis=0,
         )
@@ -210,20 +238,20 @@
         out_ref[d, rows:, :] = packed
 
 
-def project(place, heads, weight, near, far, other, shrinks):
+def project(place, heads, weight, held, other, shrinks):
     rows = heads.shape[0]
-    dests = near.shape[1] // LINE
+    dests = held.shape[1] // LINE
     return pl.pallas_call(
         project_kernel,
         out_shape=jax.ShapeDtypeStruct((dests, rows + shrinks.shape[1] // 2, LINE), BF16),
-        in_specs=[SMEM] + [VMEM] * 6,
+        in_specs=[SMEM] + [VMEM] * 5,
         out_specs=VMEM,
         compiler_params=PARAMS,
         name="project",
-    )(place, heads, weight, near, far, other, shrinks)
-
-
-def finish_kernel(block_ref, adapter_ref, parts_ref, up_ref, out_ref):
+    )(place, heads, weight, held, other, shrinks)
+
+
+def finish_kernel(mask_ref, parts_ref, up_ref, out_ref):
     count = parts_ref.shape[0]
     rows, width = out_ref.shape
     blocks, rank, _ = up_ref.shape
@@ -237,14 +265,9 @@
     low_rank = jnp.concatenate(
         [jnp.where(left, pair, turned), jnp.where(left, turned, pair)], axis=0
     )
-    adapter = adapter_ref[...]
-    wide_left = lax.broadcasted_iota(jnp.int32, (rows, lanes), 1) < rank
-    spread = []
-    for b in range(0, blocks, 2):
-        match = jnp.where(wide_left, block_ref[b], block_ref[b + 1]) == adapter
-        spread.append(jnp.where(match, low_rank, 0.0).astype(BF16))
+    wide = jnp.concatenate([low_rank.astype(BF16)] * (blocks // 2), axis=1)
     lora = jnp.dot(
-        jnp.concatenate(spread, axis=1),
+        wide * mask_ref[...],
         up_ref[...].reshape(blocks * rank, width),
         preferred_element_type=F32,
     )
@@ -254,15 +277,15 @@
     out_ref[...] = (total + lora).astype(BF16)
 
 
-def finish(parts, up, adapter_col, block_adapter, rows):
+def finish(parts, up, chosen):
     return pl.pallas_call(
         finish_kernel,
-        out_shape=jax.ShapeDtypeStruct((rows, parts.shape[2]), BF16),
-        in_specs=[SMEM, VMEM, VMEM, VMEM],
+        out_shape=jax.ShapeDtypeStruct((chosen.shape[0], parts.shape[2]), BF16),
+        in_specs=[VMEM] * 3,
         out_specs=VMEM,
         compiler_params=PARAMS,
         name="finish",
-    )(block_adapter, adapter_col, parts, up)
+    )(chosen, parts, up)
 
 
 def per_device(
@@ -304,15 +327,16 @@
         far, "tp", [(in_quad(q, m), in_quad(q, (m + 2) % QUAD)) for q in range(quads) for m in range(QUAD)]
     )
     spans = exchange(own).reshape(QUAD * rows, HEAD_SIZE)
-    partial = shrink_parts(place, spans, down_factors, adapter_col, block_adapter)
+    chosen, down = prepare(adapter_col, block_adapter, jnp.swapaxes(down_factors, 1, 2))
+    partial = shrink_parts(place, spans, down, adapter_col, block_adapter)
     shrinks = exchange(partial, axis_index_groups=lines)
     held, _ = lax.optimization_barrier((jnp.concatenate([near, far], axis=0), partial))
     other = lax.ppermute(held, "rep", [(r, r ^ 1) for r in range(reps)])
     heads = arrange(place, spans)
     parts = exchange(
-        project(place, heads, output_weight, near, far, other, shrinks), axis_index_groups=groups
-    )
-    return finish(parts, up_factors, adapter_col, block_adapter, rows)
+        project(place, heads, output_weight, held, other, shrinks), axis_index_groups=groups
+    )
+    return finish(parts, up_factors, chosen)
 
 
 def solution(mesh):

time: 68.5 us -> 66.5 us (0.971)
  the two profiles are of different devices: /device:TPU:1 before, /device:TPU:3 now
where the time goes in v8:
time: 66.5 us; the launch traced here: 66.1 us
  starting transfers between devices  27 us (41%)
  blocking collectives  23.3 us (35%)
  Pallas kernels  10.3 us (15%)
  waiting for transfers between devices  5.15 us (8%)
    all_to_all x1, blocking collectives, per_device(): exchange(project(place, heads, output_weight, held, other, shrinks), axis...  23.3 us
    all_to_all x1, starting transfers between devices, per_device(): spans = exchange(own).reshape(QUAD * rows, HEAD_SIZE)  9.99 us
    ppermute x1, starting transfers between devices, per_device(): other = lax.ppermute(held, 'rep', [(r, r ^ 1) for r in range(reps)])  6.54 us
    pallas_call x1, Pallas kernels, start(): pl.pallas_call(start_kernel, out_shape=(jax.ShapeDtypeStruct((QUERY_HEADS...  4.91 us
    all_to_all x1, starting transfers between devices, per_device(): shrinks = exchange(partial, axis_index_groups=lines)  4.9 us
    ppermute x1, starting transfers between devices, per_device(): lax.ppermute(far, 'tp', [(in_quad(q, m), in_quad(q, (m + 2) % QUAD)) for...  3.7 us
    all_to_all x1, waiting for transfers between devices, per_device(): spans = exchange(own).reshape(QUAD * rows, HEAD_SIZE)  3.49 us
    ppermute x1, starting transfers between devices, per_device(): lax.ppermute(near, ('rep', 'tp'), [(r * devices + in_quad(q, m), r * devi...  1.92 us
  transfers between devices with their start and end apart: 5, of which 2 were waited for; matrix products, arithmetic and copies ran while one was open for 0% of the time, Pallas kernels for 4%

profile of v8, /device:TPU:3, one launch (start us, length us, event | category | flops | bytes accessed | tf_op | source)
XLA Modules:
  0.0 66.1 jit_solution(8154011023522833061)
XLA Ops:
  0.0 0.0 copy-start.4
  0.0 0.0 copy-start.2
  0.0 0.0 copy-start.3
  0.0 4.9 %start.1 = (bf16[32,16,128]{2,1,0:T(8,128)(2,1)}, bf16[128,2048]{1,0:T(8,128)(2,1)}, bf16[64,2048]{1,0:T(8,128)(2,1)}) custom-call(s32[1]{0:T(128)} %bitcast.2.place_ref, s32[4]{0:T(128)} %len_ref.1, bf16[4,4096]{1,0:T(4,128)(2,1)} %q_ref.1, bf16[4,256,512]{2,1,0:T(8,128)(2,1)} %k_hbm.1, bf16[4,256,512]{2,1,0:T(8,128)(2,1)} %v_hbm.1, ...), custom_call_target="tpu_custom_call" | custom-call | tf_op jit(solution)/shard_map/start/pallas_call | solution.py:102
  4.9 1.9 %collective-permute-start = (bf16[128,2048]{1,0:T(8,128)(2,1)}, bf16[128,2048]{1,0:T(8,128)(2,1)S(1)}, u32[]{:S(2)}, u32[]{:S(2)}) collective-permute-start(bf16[128,2048]{1,0:T(8,128)(2,1)} %get-tuple-element.13), channel_id=1, source_target_pairs={{0,1},{1,2},{2,3},{3,0},{4,5},{5,6},{6,7},{7,4},{8,9},{9,10},{10,1... | collective-permute-start | bytes 1572872 | tf_op jit(solution)/shard_map/ppermute | solution.py:316
  6.9 10.0 %all-to-all-start = ((bf16[32,16,128]{2,1,0:T(8,128)(2,1)}), bf16[32,16,128]{2,1,0:T(8,128)(2,1)S(1)}, u32[]{:S(2)}, u32[]{:S(2)}) async-start(bf16[32,16,128]{2,1,0:T(8,128)(2,1)} %get-tuple-element.12), calls=%async_computation | async-start | bytes 262144 | tf_op jit(solution)/shard_map/all_to_all | solution.py:329
  16.8 3.7 %collective-permute-start.1 = (bf16[64,2048]{1,0:T(8,128)(2,1)}, bf16[64,2048]{1,0:T(8,128)(2,1)S(1)}, u32[]{:S(2)}, u32[]{:S(2)}) collective-permute-start(bf16[64,2048]{1,0:T(8,128)(2,1)} %get-tuple-element.14), channel_id=1, source_target_pairs={{0,2},{1,3},{2,0},{3,1},{4,6},{5,7},{6,4},{7,5},{8,10},{9,11},{10,... | collective-permute-start | bytes 786440 | tf_op jit(solution)/shard_map/ppermute | solution.py:326
  20.6 0.0 copy-done.4
  20.6 0.1 copy.10.adapter_ref
  20.7 0.0 copy-done.2
  20.7 0.0 copy-done.3
  20.7 0.7 %prepare.1 = (bf16[128,1024]{1,0:T(8,128)(2,1)S(1)}, bf16[16,64,128]{2,1,0:T(8,128)(2,1)S(1)}) custom-call(s32[16]{0:T(128)S(1)} %copy-done.3, s32[128,1]{1,0:T(8,128)S(1)} %copy.10.adapter_ref, bf16[16,64,128]{2,1,0:T(8,128)(2,1)S(1)} %bitcast.4), custom_call_target="tpu_custom_call" | custom-call | tf_op jit(solution)/shard_map/prepare/pallas_call | solution.py:172
  21.4 3.5 %all-to-all-done = bf16[32,16,128]{2,1,0:T(8,128)(2,1)S(1)} async-done(((bf16[32,16,128]{2,1,0:T(8,128)(2,1)}), bf16[32,16,128]{2,1,0:T(8,128)(2,1)S(1)}, u32[]{:S(2)}, u32[]{:S(2)}) %all-to-all-start) | async-done | bytes 131104 | tf_op jit(solution)/shard_map/all_to_all | solution.py:329
  24.9 1.8 %shrink.1 = bf16[4,64,128]{2,1,0:T(8,128)(2,1)} custom-call(s32[1]{0:T(128)} %bitcast.2.place_ref, s32[16]{0:T(128)S(1)} %copy-done.3, s32[128,1]{1,0:T(8,128)S(1)} %copy.10.adapter_ref, bf16[512,128]{1,0:T(8,128)(2,1)S(1)} %bitcast.5, bf16[16,64,128]{2,1,0:T(8,128)(2,1)S(1)} %get-tuple-element.15.down_ref), custom_call_target="tpu_custom_call" | custom-call | flops 1000000000 | bytes 1048576 | tf_op jit(solution)/shard_map/shrink/pallas_call | solution.py:147
  26.6 4.9 %all-to-all-start.1 = ((bf16[4,64,128]{2,1,0:T(8,128)(2,1)}), bf16[4,64,128]{2,1,0:T(8,128)(2,1)S(1)}, u32[]{:S(2)}, u32[]{:S(2)}) async-start(bf16[4,64,128]{2,1,0:T(8,128)(2,1)} %shrink.1), calls=%async_computation.1 | async-start | bytes 131072 | tf_op jit(solution)/shard_map/all_to_all | solution.py:332
  31.5 0.0 collective-permute-done.1
  31.5 0.0 collective-permute-done
  31.5 0.1 pad_maximum_fusion.held_ref
  31.6 0.0 copy-start
  31.6 6.5 %collective-permute-start.2 = (bf16[192,2048]{1,0:T(8,128)(2,1)S(1)}, bf16[192,2048]{1,0:T(8,128)(2,1)}, u32[]{:S(2)}, u32[]{:S(2)}) collective-permute-start(bf16[192,2048]{1,0:T(8,128)(2,1)S(1)} %pad_maximum_fusion.held_ref), channel_id=1, source_target_pairs={{0,32},{32,0},{64,96},{96,64},{128,160},{160,128},{192,224},{224,1... | collective-permute-start | bytes 2359304 | tf_op jit(solution)/shard_map/ppermute | solution.py:334
  38.2 0.4 arrange.1.heads_ref
  38.5 0.0 all-to-all-done.1.shrink_ref
  38.5 1.7 %collective-permute-done.2.other_ref = bf16[192,2048]{1,0:T(8,128)(2,1)} collective-permute-done((bf16[192,2048]{1,0:T(8,128)(2,1)S(1)}, bf16[192,2048]{1,0:T(8,128)(2,1)}, u32[]{:S(2)}, u32[]{:S(2)}) %collective-permute-start.2) | collective-permute-done | bytes 786464 | tf_op jit(solution)/shard_map/ppermute | solution.py:334
  40.2 0.0 copy-done
  40.2 1.6 %project.1 = bf16[8,160,256]{2,1,0:T(8,128)(2,1)S(1)} custom-call(s32[1]{0:T(128)} %bitcast.2.place_ref, bf16[128,512]{1,0:T(8,128)(2,1)S(1)} %arrange.1.heads_ref, bf16[128,8192]{1,0:T(8,128)(2,1)S(1)} %copy-done, bf16[192,2048]{1,0:T(8,128)(2,1)S(1)} %pad_maximum_fusion.held_ref, bf16[192,2048]{1,0:T(8,128)(2,1)} %collective-permute-done.2.other_ref, ...), custom_call_target="tpu_custom_call" | custom-call | tf_op jit(solution)/shard_map/project/pallas_call | solution.py:244
  41.8 0.0 copy-start.1
  41.8 23.3 %all_to_all.15.parts_ref = bf16[8,160,256]{2,1,0:T(8,128)(2,1)S(1)} all-to-all(bf16[8,160,256]{2,1,0:T(8,128)(2,1)S(1)} %project.1), channel_id=1, replica_groups={{0,4,8,12,16,20,24,28},{1,5,9,13,17,21,25,29},{2,6,10,14,18,22,26,30},{..., dimensions={0} | all-to-all | bytes 1310720 | tf_op jit(solution)/shard_map/all_to_all | solution.py:336
  65.1 0.0 copy-done.1
  65.1 0.9 %finish.1 = bf16[128,256]{1,0:T(8,128)(2,1)} custom-call(bf16[128,1024]{1,0:T(8,128)(2,1)S(1)} %get-tuple-element.11.mask_ref, bf16[8,160,256]{2,1,0:T(8,128)(2,1)S(1)} %all_to_all.15.parts_ref, bf16[16,64,256]{2,1,0:T(8,128)(2,1)S(1)} %copy-done.1), custom_call_target="tpu_custom_call" | custom-call | tf_op jit(solution)/shard_map/finish/pallas_call | solution.py:281
Async XLA Ops:
  0.0 20.6 %copy-start.4 = (s32[128]{0:T(128)S(1)}, s32[128]{0:T(128)}, u32[]{:S(2)}) copy-start(s32[128]{0:T(128)} %param.13) | copy-start | bytes 1540
  0.0 20.7 %copy-start.2 = (bf16[16,128,64]{1,2,0:T(8,128)(2,1)S(1)}, bf16[16,128,64]{1,2,0:T(8,128)(2,1)}, u32[]{:S(2)}) copy-start(bf16[16,128,64]{1,2,0:T(8,128)(2,1)} %param.16) | copy-start | bytes 786436
  0.0 20.7 %copy-start.3 = (s32[16]{0:T(128)S(1)}, s32[16]{0:T(128)}, u32[]{:S(2)}) copy-start(s32[16]{0:T(128)} %block_ref.3) | copy-start | bytes 196
  4.9 26.6 %collective-permute-start = (bf16[128,2048]{1,0:T(8,128)(2,1)}, bf16[128,2048]{1,0:T(8,128)(2,1)S(1)}, u32[]{:S(2)}, u32[]{:S(2)}) collective-permute-start(bf16[128,2048]{1,0:T(8,128)(2,1)} %get-tuple-element.13), channel_id=1, source_target_pairs={{0,1},{1,2},{2,3},{3,0},{4,5},{5,6},{6,7},{7,4},{8,9},{9,10},{10,1... | collective-permute-start | bytes 1572872 | tf_op jit(solution)/shard_map/ppermute | solution.py:316
  6.9 18.0 %all-to-all-start = ((bf16[32,16,128]{2,1,0:T(8,128)(2,1)}), bf16[32,16,128]{2,1,0:T(8,128)(2,1)S(1)}, u32[]{:S(2)}, u32[]{:S(2)}) async-start(bf16[32,16,128]{2,1,0:T(8,128)(2,1)} %get-tuple-element.12), calls=%async_computation | async-start | bytes 262144 | tf_op jit(solution)/shard_map/all_to_all | solution.py:329
  16.8 14.7 %collective-permute-start.1 = (bf16[64,2048]{1,0:T(8,128)(2,1)}, bf16[64,2048]{1,0:T(8,128)(2,1)S(1)}, u32[]{:S(2)}, u32[]{:S(2)}) collective-permute-start(bf16[64,2048]{1,0:T(8,128)(2,1)} %get-tuple-element.14), channel_id=1, source_target_pairs={{0,2},{1,3},{2,0},{3,1},{4,6},{5,7},{6,4},{7,5},{8,10},{9,11},{10,... | collective-permute-start | bytes 786440 | tf_op jit(solution)/shard_map/ppermute | solution.py:326
  26.6 11.9 %all-to-all-start.1 = ((bf16[4,64,128]{2,1,0:T(8,128)(2,1)}), bf16[4,64,128]{2,1,0:T(8,128)(2,1)S(1)}, u32[]{:S(2)}, u32[]{:S(2)}) async-start(bf16[4,64,128]{2,1,0:T(8,128)(2,1)} %shrink.1), calls=%async_computation.1 | async-start | bytes 131072 | tf_op jit(solution)/shard_map/all_to_all | solution.py:332
  31.6 8.6 %copy-start = (bf16[128,8192]{1,0:T(8,128)(2,1)S(1)}, bf16[128,8192]{1,0:T(8,128)(2,1)}, u32[]{:S(2)}) copy-start(bf16[128,8192]{1,0:T(8,128)(2,1)} %weight_ref.1) | copy-start | bytes 6291460
  31.6 8.6 %collective-permute-start.2 = (bf16[192,2048]{1,0:T(8,128)(2,1)S(1)}, bf16[192,2048]{1,0:T(8,128)(2,1)}, u32[]{:S(2)}, u32[]{:S(2)}) collective-permute-start(bf16[192,2048]{1,0:T(8,128)(2,1)S(1)} %pad_maximum_fusion.held_ref), channel_id=1, source_target_pairs={{0,32},{32,0},{64,96},{96,64},{128,160},{160,128},{192,224},{224,1... | collective-permute-start | bytes 2359304 | tf_op jit(solution)/shard_map/ppermute | solution.py:334
  41.8 23.3 %copy-start.1 = (bf16[16,64,256]{2,1,0:T(8,128)(2,1)S(1)}, bf16[16,64,256]{2,1,0:T(8,128)(2,1)}, u32[]{:S(2)}) copy-start(bf16[16,64,256]{2,1,0:T(8,128)(2,1)} %up_ref.1) | copy-start | bytes 1572868

commit v9 on v8

--- a/solution.py
+++ b/solution.py
@@ -27,11 +27,12 @@
 
 
 def start_kernel(
-    place_ref, len_ref, q_ref, k_hbm, v_hbm, w_hbm, heads_ref, near_ref, far_ref, k_ref, v_ref, k_sem, v_sem, w_sem
+    place_ref, len_ref, q_hbm, k_hbm, v_hbm, w_hbm, heads_ref, near_ref, far_ref, *scratch
 ):
+    q_ref, k_ref, v_ref, q_sem, k_sem, v_sem, w_sem = scratch
     rows, size = k_ref.shape[0], HEAD_SIZE
-    k_copies = [pltpu.make_async_copy(k_hbm.at[r], k_ref.at[r], k_sem.at[r]) for r in range(rows)]
-    v_copies = [pltpu.make_async_copy(v_hbm.at[r], v_ref.at[r], v_sem.at[r]) for r in range(rows)]
+    k_copies = [pltpu.make_async_copy(k_hbm, k_ref, k_sem)]
+    v_copies = [pltpu.make_async_copy(v_hbm, v_ref, v_sem)]
     member, core = place_ref[0] & (QUAD - 1), lax.div(place_ref[0], QUAD)
     near = lax.rem(member + 1 + 2 * core, QUAD)
     far = lax.rem(member + 2, QUAD)
@@ -48,15 +49,19 @@
         w_copies.append(
             pltpu.make_async_copy(w_hbm.at[half, source], far_ref.at[:, columns], w_sem.at[1, q])
         )
-    for copy in k_copies + v_copies + w_copies:
+    q_copy = pltpu.make_async_copy(q_hbm, q_ref, q_sem)
+    for copy in [q_copy] + k_copies + v_copies:
         copy.start()
 
+    q_copy.wait()
     q = q_ref[...].astype(F32)
     q_rows = jnp.concatenate(
         [q[:, h * size : (h + 1) * size] for h in range(QUERY_HEADS)], axis=0
     )
     q_lanes = q_rows.T.astype(BF16)
     count = rows * QUERY_HEADS
+    for copy in w_copies:
+        copy.start()
     lane = lax.broadcasted_iota(jnp.int32, (size, count), 1)
     by_key = [
         jnp.where(lane // (count // KVH) == k, q_lanes, jnp.zeros_like(q_lanes))
@@ -68,7 +73,8 @@
     scores = jnp.zeros((CTX, count), F32)
     length = jnp.zeros((CTX, count), jnp.int32)
     for r in range(rows):
-        k_copies[r].wait()
+        if r == 0:
+            k_copies[0].wait()
         all_lanes = jnp.dot(k_ref[r], spread, preferred_element_type=F32)
         scores = jnp.where(request == r, all_lanes, scores)
         length = jnp.where(request == r, len_ref[r], length)
@@ -79,7 +85,8 @@
     owner = lax.broadcasted_iota(jnp.int32, (count, CTX), 0) % rows
     wide = jnp.zeros((count, KVH * size), F32)
     for r in range(rows):
-        v_copies[r].wait()
+        if r == 0:
+            v_copies[0].wait()
         mine = jnp.where(owner == r, probs, jnp.zeros_like(probs))
         wide += jnp.dot(mine, v_ref[r], preferred_element_type=F32)
     group = count // KVH
@@ -106,10 +113,10 @@
             jax.ShapeDtypeStruct((depth, span), BF16),
             jax.ShapeDtypeStruct((depth // 2, span), BF16),
         ),
-        in_specs=[SMEM, SMEM, VMEM, HBM, HBM, HBM],
+        in_specs=[SMEM, SMEM, HBM, HBM, HBM, HBM],
         out_specs=(VMEM,) * 3,
-        scratch_shapes=[cache, cache]
-        + [pltpu.SemaphoreType.DMA((rows,))] * 2
+        scratch_shapes=[pltpu.VMEM(queries.shape, BF16), cache, cache, pltpu.SemaphoreType.DMA]
+        + [pltpu.SemaphoreType.DMA] * 2
         + [pltpu.SemaphoreType.DMA((2, span // LINE))],
         compiler_params=WHOLE,
         name="start",
@@ -126,33 +133,39 @@
     return jnp.dot(choice, spans, preferred_element_type=F32).astype(BF16)
 
 
-def shrink_kernel(place_ref, block_ref, adapter_ref, spans_ref, down_ref, out_ref):
+def shrink_kernel(place_ref, spans_ref, down_ref, mask_ref, out_ref):
+    heads = pick_rows(spans_ref[...], place_ref[0] & (QUAD - 1))
+    blocks, rank, depth = down_ref.shape
+    every = lax.dot_general(
+        heads,
+        down_ref[...].reshape(blocks * rank, depth),
+        (((1,), (1,)), ((), ())),
+        preferred_element_type=F32,
+    )
+    every = jnp.where(mask_ref[...].astype(F32) > 0, every, 0.0)
+    lanes = 2 * rank
+    pair = every[:, :lanes]
+    for b in range(lanes, blocks * rank, lanes):
+        pair += every[:, b : b + lanes]
+    twice = pair + jnp.concatenate([pair[:, rank:], pair[:, :rank]], axis=1)
     half = out_ref.shape[1]
-    heads = pick_rows(spans_ref[...], place_ref[0] & (QUAD - 1))
-    adapter = adapter_ref[...]
-    rank = down_ref.shape[1]
-    shrink = jnp.zeros((heads.shape[0], rank), F32)
-    for b in range(down_ref.shape[0]):
-        mine = jnp.where(adapter == block_ref[b], heads, jnp.zeros_like(heads))
-        shrink += lax.dot_general(
-            mine, down_ref[b], (((1,), (1,)), ((), ())), preferred_element_type=F32
-        )
-    packed = jnp.concatenate([shrink[:half], shrink[half:]], axis=1).astype(BF16)
+    left = lax.broadcasted_iota(jnp.int32, (half, lanes), 1) < rank
+    packed = jnp.where(left, twice[:half], twice[half:]).astype(BF16)
     for m in range(QUAD):
         out_ref[m] = packed
 
 
-def shrink_parts(place, spans, down, adapter_col, block_adapter):
+def shrink_parts(place, spans, down, chosen):
     half = spans.shape[0] // QUAD // 2
     return pl.pallas_call(
         shrink_kernel,
         out_shape=jax.ShapeDtypeStruct((QUAD, half, 2 * down.shape[1]), BF16),
-        in_specs=[SMEM, SMEM, VMEM, VMEM, VMEM],
+        in_specs=[SMEM, VMEM, VMEM, VMEM],
         out_specs=VMEM,
         compiler_params=PARAMS,
         cost_estimate=pl.CostEstimate(flops=10**9, bytes_accessed=2**20, transcendentals=0),
         name="shrink",
-    )(place, block_adapter, adapter_col, spans, down)
+    )(place, spans, down, chosen)
 
 
 def prepare_kernel(block_ref, adapter_ref, down_hbm, mask_ref, down_ref, sem):
@@ -328,7 +341,7 @@
     )
     spans = exchange(own).reshape(QUAD * rows, HEAD_SIZE)
     chosen, down = prepare(adapter_col, block_adapter, jnp.swapaxes(down_factors, 1, 2))
-    partial = shrink_parts(place, spans, down, adapter_col, block_adapter)
+    partial = shrink_parts(place, spans, down, chosen)
     shrinks = exchange(partial, axis_index_groups=lines)
     held, _ = lax.optimization_barrier((jnp.concatenate([near, far], axis=0), partial))
     other = lax.ppermute(held, "rep", [(r, r ^ 1) for r in range(reps)])

time: 66.5 us -> 65 us (0.977)
  Pallas kernels: 10.3 us -> 8.73 us
    pallas_call x1, Pallas kernels: 4.91 us -> 4.08 us  [start(): pl.pallas_call(start_kernel, out_shape=(jax.ShapeDtypeStruct((QUERY_HEADS...]
    pallas_call x1, Pallas kernels: 1.75 us -> 1.05 us  [shrink_parts(): pl.pallas_call(shrink_kernel, out_shape=jax.ShapeDtypeStruct((QUAD, half,...]
  transfers between devices with their start and end apart: 5 -> 5, of which waited for: 2 -> 2; matrix products, arithmetic and copies ran while one was open for 0% -> 0% of each run, Pallas kernels for 4% -> 3%
where the time goes in v9:
time: 65 us; the launch traced here: 64.5 us
  starting transfers between devices  27 us (42%)
  blocking collectives  23.3 us (36%)
  Pallas kernels  8.73 us (13%)
  waiting for transfers between devices  5.15 us (8%)
    all_to_all x1, blocking collectives, per_device(): exchange(project(place, heads, output_weight, held, other, shrinks), axis...  23.3 us
    all_to_all x1, starting transfers between devices, per_device(): spans = exchange(own).reshape(QUAD * rows, HEAD_SIZE)  9.98 us
    ppermute x1, starting transfers between devices, per_device(): other = lax.ppermute(held, 'rep', [(r, r ^ 1) for r in range(reps)])  6.55 us
    all_to_all x1, starting transfers between devices, per_device(): shrinks = exchange(partial, axis_index_groups=lines)  4.9 us
    pallas_call x1, Pallas kernels, start(): pl.pallas_call(start_kernel, out_shape=(jax.ShapeDtypeStruct((QUERY_HEADS...  4.08 us
    ppermute x1, starting transfers between devices, per_device(): lax.ppermute(far, 'tp', [(in_quad(q, m), in_quad(q, (m + 2) % QUAD)) for...  3.7 us
    all_to_all x1, waiting for transfers between devices, per_device(): spans = exchange(own).reshape(QUAD * rows, HEAD_SIZE)  3.49 us
    ppermute x1, starting transfers between devices, per_device(): lax.ppermute(near, ('rep', 'tp'), [(r * devices + in_quad(q, m), r * devi...  1.92 us
  transfers between devices with their start and end apart: 5, of which 2 were waited for; matrix products, arithmetic and copies ran while one was open for 0% of the time, Pallas kernels for 3%

profile of v9, /device:TPU:3, one launch (start us, length us, event | category | flops | bytes accessed | tf_op | source)
XLA Modules:
  0.0 64.5 jit_solution(12540775973647053052)
XLA Ops:
  0.0 0.0 copy-start.4
  0.0 0.0 copy-start.2
  0.0 0.0 copy-start.3
  0.0 4.1 %start.1 = (bf16[32,16,128]{2,1,0:T(8,128)(2,1)}, bf16[128,2048]{1,0:T(8,128)(2,1)}, bf16[64,2048]{1,0:T(8,128)(2,1)}) custom-call(s32[1]{0:T(128)} %bitcast.2.place_ref, s32[4]{0:T(128)} %len_ref.1, bf16[4,4096]{1,0:T(4,128)(2,1)} %q_hbm.1, bf16[4,256,512]{2,1,0:T(8,128)(2,1)} %k_hbm.1, bf16[4,256,512]{2,1,0:T(8,128)(2,1)} %v_hbm.1, ...), custom_call_target="tpu_custom_call" | custom-call | tf_op jit(solution)/shard_map/start/pallas_call | solution.py:109
  4.1 1.9 %collective-permute-start = (bf16[128,2048]{1,0:T(8,128)(2,1)}, bf16[128,2048]{1,0:T(8,128)(2,1)S(1)}, u32[]{:S(2)}, u32[]{:S(2)}) collective-permute-start(bf16[128,2048]{1,0:T(8,128)(2,1)} %get-tuple-element.13), channel_id=1, source_target_pairs={{0,1},{1,2},{2,3},{3,0},{4,5},{5,6},{6,7},{7,4},{8,9},{9,10},{10,1... | collective-permute-start | bytes 1572872 | tf_op jit(solution)/shard_map/ppermute | solution.py:329
  6.0 10.0 %all-to-all-start = ((bf16[32,16,128]{2,1,0:T(8,128)(2,1)}), bf16[32,16,128]{2,1,0:T(8,128)(2,1)S(1)}, u32[]{:S(2)}, u32[]{:S(2)}) async-start(bf16[32,16,128]{2,1,0:T(8,128)(2,1)} %get-tuple-element.12), calls=%async_computation | async-start | bytes 262144 | tf_op jit(solution)/shard_map/all_to_all | solution.py:342
  16.0 3.7 %collective-permute-start.1 = (bf16[64,2048]{1,0:T(8,128)(2,1)}, bf16[64,2048]{1,0:T(8,128)(2,1)S(1)}, u32[]{:S(2)}, u32[]{:S(2)}) collective-permute-start(bf16[64,2048]{1,0:T(8,128)(2,1)} %get-tuple-element.14), channel_id=1, source_target_pairs={{0,2},{1,3},{2,0},{3,1},{4,6},{5,7},{6,4},{7,5},{8,10},{9,11},{10,... | collective-permute-start | bytes 786440 | tf_op jit(solution)/shard_map/ppermute | solution.py:339
  19.7 0.0 copy-done.4
  19.7 0.1 copy.10.adapter_ref
  19.8 0.0 copy-done.2
  19.8 0.0 copy-done.3
  19.9 0.7 %prepare.1 = (bf16[128,1024]{1,0:T(8,128)(2,1)S(1)}, bf16[16,64,128]{2,1,0:T(8,128)(2,1)S(1)}) custom-call(s32[16]{0:T(128)S(1)} %copy-done.3, s32[128,1]{1,0:T(8,128)S(1)} %copy.10.adapter_ref, bf16[16,64,128]{2,1,0:T(8,128)(2,1)S(1)} %bitcast.4), custom_call_target="tpu_custom_call" | custom-call | tf_op jit(solution)/shard_map/prepare/pallas_call | solution.py:185
  20.6 3.5 %all-to-all-done = bf16[32,16,128]{2,1,0:T(8,128)(2,1)S(1)} async-done(((bf16[32,16,128]{2,1,0:T(8,128)(2,1)}), bf16[32,16,128]{2,1,0:T(8,128)(2,1)S(1)}, u32[]{:S(2)}, u32[]{:S(2)}) %all-to-all-start) | async-done | bytes 131104 | tf_op jit(solution)/shard_map/all_to_all | solution.py:342
  24.0 1.1 %shrink.1 = bf16[4,64,128]{2,1,0:T(8,128)(2,1)} custom-call(s32[1]{0:T(128)} %bitcast.2.place_ref, bf16[512,128]{1,0:T(8,128)(2,1)S(1)} %bitcast.5, bf16[16,64,128]{2,1,0:T(8,128)(2,1)S(1)} %get-tuple-element.15.down_ref, bf16[128,1024]{1,0:T(8,128)(2,1)S(1)} %get-tuple-element.11.mask_ref), custom_call_target="tpu_custom_call" | custom-call | flops 1000000000 | bytes 1048576 | tf_op jit(solution)/shard_map/shrink/pallas_call | solution.py:160
  25.1 4.9 %all-to-all-start.1 = ((bf16[4,64,128]{2,1,0:T(8,128)(2,1)}), bf16[4,64,128]{2,1,0:T(8,128)(2,1)S(1)}, u32[]{:S(2)}, u32[]{:S(2)}) async-start(bf16[4,64,128]{2,1,0:T(8,128)(2,1)} %shrink.1), calls=%async_computation.1 | async-start | bytes 131072 | tf_op jit(solution)/shard_map/all_to_all | solution.py:345
  30.0 0.0 collective-permute-done.1
  30.0 0.0 collective-permute-done
  30.0 0.1 pad_maximum_fusion.held_ref
  30.1 0.0 copy-start
  30.1 6.6 %collective-permute-start.2 = (bf16[192,2048]{1,0:T(8,128)(2,1)S(1)}, bf16[192,2048]{1,0:T(8,128)(2,1)}, u32[]{:S(2)}, u32[]{:S(2)}) collective-permute-start(bf16[192,2048]{1,0:T(8,128)(2,1)S(1)} %pad_maximum_fusion.held_ref), channel_id=1, source_target_pairs={{0,32},{32,0},{64,96},{96,64},{128,160},{160,128},{192,224},{224,1... | collective-permute-start | bytes 2359304 | tf_op jit(solution)/shard_map/ppermute | solution.py:347
  36.6 0.4 arrange.1.heads_ref
  37.0 0.0 all-to-all-done.1.shrink_ref
  37.0 1.7 %collective-permute-done.2.other_ref = bf16[192,2048]{1,0:T(8,128)(2,1)} collective-permute-done((bf16[192,2048]{1,0:T(8,128)(2,1)S(1)}, bf16[192,2048]{1,0:T(8,128)(2,1)}, u32[]{:S(2)}, u32[]{:S(2)}) %collective-permute-start.2) | collective-permute-done | bytes 786464 | tf_op jit(solution)/shard_map/ppermute | solution.py:347
  38.7 0.0 copy-done
  38.7 1.6 %project.1 = bf16[8,160,256]{2,1,0:T(8,128)(2,1)S(1)} custom-call(s32[1]{0:T(128)} %bitcast.2.place_ref, bf16[128,512]{1,0:T(8,128)(2,1)S(1)} %arrange.1.heads_ref, bf16[128,8192]{1,0:T(8,128)(2,1)S(1)} %copy-done, bf16[192,2048]{1,0:T(8,128)(2,1)S(1)} %pad_maximum_fusion.held_ref, bf16[192,2048]{1,0:T(8,128)(2,1)} %collective-permute-done.2.other_ref, ...), custom_call_target="tpu_custom_call" | custom-call | tf_op jit(solution)/shard_map/project/pallas_call | solution.py:257
  40.3 0.0 copy-start.1
  40.3 23.3 %all_to_all.15.parts_ref = bf16[8,160,256]{2,1,0:T(8,128)(2,1)S(1)} all-to-all(bf16[8,160,256]{2,1,0:T(8,128)(2,1)S(1)} %project.1), channel_id=1, replica_groups={{0,4,8,12,16,20,24,28},{1,5,9,13,17,21,25,29},{2,6,10,14,18,22,26,30},{..., dimensions={0} | all-to-all | bytes 1310720 | tf_op jit(solution)/shard_map/all_to_all | solution.py:349
  63.6 0.0 copy-done.1
  63.6 0.9 %finish.1 = bf16[128,256]{1,0:T(8,128)(2,1)} custom-call(bf16[128,1024]{1,0:T(8,128)(2,1)S(1)} %get-tuple-element.11.mask_ref, bf16[8,160,256]{2,1,0:T(8,128)(2,1)S(1)} %all_to_all.15.parts_ref, bf16[16,64,256]{2,1,0:T(8,128)(2,1)S(1)} %copy-done.1), custom_call_target="tpu_custom_call" | custom-call | tf_op jit(solution)/shard_map/finish/pallas_call | solution.py:294
Async XLA Ops:
  0.0 19.7 %copy-start.4 = (s32[128]{0:T(128)S(1)}, s32[128]{0:T(128)}, u32[]{:S(2)}) copy-start(s32[128]{0:T(128)} %param.13) | copy-start | bytes 1540
  0.0 19.8 %copy-start.2 = (bf16[16,128,64]{1,2,0:T(8,128)(2,1)S(1)}, bf16[16,128,64]{1,2,0:T(8,128)(2,1)}, u32[]{:S(2)}) copy-start(bf16[16,128,64]{1,2,0:T(8,128)(2,1)} %param.16) | copy-start | bytes 786436
  0.0 19.8 %copy-start.3 = (s32[16]{0:T(128)S(1)}, s32[16]{0:T(128)}, u32[]{:S(2)}) copy-start(s32[16]{0:T(128)} %block_ref.1) | copy-start | bytes 196
  4.1 25.9 %collective-permute-start = (bf16[128,2048]{1,0:T(8,128)(2,1)}, bf16[128,2048]{1,0:T(8,128)(2,1)S(1)}, u32[]{:S(2)}, u32[]{:S(2)}) collective-permute-start(bf16[128,2048]{1,0:T(8,128)(2,1)} %get-tuple-element.13), channel_id=1, source_target_pairs={{0,1},{1,2},{2,3},{3,0},{4,5},{5,6},{6,7},{7,4},{8,9},{9,10},{10,1... | collective-permute-start | bytes 1572872 | tf_op jit(solution)/shard_map/ppermute | solution.py:329
  6.0 18.0 %all-to-all-start = ((bf16[32,16,128]{2,1,0:T(8,128)(2,1)}), bf16[32,16,128]{2,1,0:T(8,128)(2,1)S(1)}, u32[]{:S(2)}, u32[]{:S(2)}) async-start(bf16[32,16,128]{2,1,0:T(8,128)(2,1)} %get-tuple-element.12), calls=%async_computation | async-start | bytes 262144 | tf_op jit(solution)/shard_map/all_to_all | solution.py:342
  16.0 14.0 %collective-permute-start.1 = (bf16[64,2048]{1,0:T(8,128)(2,1)}, bf16[64,2048]{1,0:T(8,128)(2,1)S(1)}, u32[]{:S(2)}, u32[]{:S(2)}) collective-permute-start(bf16[64,2048]{1,0:T(8,128)(2,1)} %get-tuple-element.14), channel_id=1, source_target_pairs={{0,2},{1,3},{2,0},{3,1},{4,6},{5,7},{6,4},{7,5},{8,10},{9,11},{10,... | collective-permute-start | bytes 786440 | tf_op jit(solution)/shard_map/ppermute | solution.py:339
  25.1 11.9 %all-to-all-start.1 = ((bf16[4,64,128]{2,1,0:T(8,128)(2,1)}), bf16[4,64,128]{2,1,0:T(8,128)(2,1)S(1)}, u32[]{:S(2)}, u32[]{:S(2)}) async-start(bf16[4,64,128]{2,1,0:T(8,128)(2,1)} %shrink.1), calls=%async_computation.1 | async-start | bytes 131072 | tf_op jit(solution)/shard_map/all_to_all | solution.py:345
  30.1 8.6 %copy-start = (bf16[128,8192]{1,0:T(8,128)(2,1)S(1)}, bf16[128,8192]{1,0:T(8,128)(2,1)}, u32[]{:S(2)}) copy-start(bf16[128,8192]{1,0:T(8,128)(2,1)} %weight_ref.1) | copy-start | bytes 6291460
  30.1 8.6 %collective-permute-start.2 = (bf16[192,2048]{1,0:T(8,128)(2,1)S(1)}, bf16[192,2048]{1,0:T(8,128)(2,1)}, u32[]{:S(2)}, u32[]{:S(2)}) collective-permute-start(bf16[192,2048]{1,0:T(8,128)(2,1)S(1)} %pad_maximum_fusion.held_ref), channel_id=1, source_target_pairs={{0,32},{32,0},{64,96},{96,64},{128,160},{160,128},{192,224},{224,1... | collective-permute-start | bytes 2359304 | tf_op jit(solution)/shard_map/ppermute | solution.py:347
  40.3 23.3 %copy-start.1 = (bf16[16,64,256]{2,1,0:T(8,128)(2,1)S(1)}, bf16[16,64,256]{2,1,0:T(8,128)(2,1)}, u32[]{:S(2)}) copy-start(bf16[16,64,256]{2,1,0:T(8,128)(2,1)} %up_ref.1) | copy-start | bytes 1572868

commit v10 on v9

--- a/solution.py
+++ b/solution.py
@@ -163,7 +163,6 @@
         in_specs=[SMEM, VMEM, VMEM, VMEM],
         out_specs=VMEM,
         compiler_params=PARAMS,
-        cost_estimate=pl.CostEstimate(flops=10**9, bytes_accessed=2**20, transcendentals=0),
         name="shrink",
     )(place, spans, down, chosen)
 
@@ -194,6 +193,23 @@
         compiler_params=PARAMS,
         name="prepare",
     )(block_adapter, adapter_col, down)
+
+
+def pass_kernel(held_hbm, after_hbm, out_hbm):
+    del held_hbm, after_hbm, out_hbm
+
+
+def pass_on(held, after):
+    return pl.pallas_call(
+        pass_kernel,
+        out_shape=jax.ShapeDtypeStruct(held.shape, held.dtype),
+        in_specs=[HBM] * 2,
+        out_specs=HBM,
+        input_output_aliases={0: 0},
+        compiler_params=PARAMS,
+        cost_estimate=pl.CostEstimate(flops=10**10, bytes_accessed=2**18, transcendentals=0),
+        name="pass_on",
+    )(held, after)
 
 
 def arrange_kernel(place_ref, spans_ref, out_ref):
@@ -343,6 +359,7 @@
     chosen, down = prepare(adapter_col, block_adapter, jnp.swapaxes(down_factors, 1, 2))
     partial = shrink_parts(place, spans, down, chosen)
     shrinks = exchange(partial, axis_index_groups=lines)
+    far = pass_on(far, partial)
     held, _ = lax.optimization_barrier((jnp.concatenate([near, far], axis=0), partial))
     other = lax.ppermute(held, "rep", [(r, r ^ 1) for r in range(reps)])
     heads = arrange(place, spans)

time: 65 us -> 64.7 us (level)
  the two profiles are of different devices: /device:TPU:3 before, /device:TPU:1 now
where the time goes in v10:
time: 64.7 us; the launch traced here: 64 us
  starting transfers between devices  25.3 us (39%)
  blocking collectives  23.7 us (37%)
  Pallas kernels  8.69 us (13%)
  waiting for transfers between devices  5.88 us (9%)
    all_to_all x1, blocking collectives, per_device(): exchange(project(place, heads, output_weight, held, other, shrinks), axis...  23.7 us
    all_to_all x1, starting transfers between devices, per_device(): spans = exchange(own).reshape(QUAD * rows, HEAD_SIZE)  7.8 us
    ppermute x1, starting transfers between devices, per_device(): lax.ppermute(far, 'tp', [(in_quad(q, m), in_quad(q, (m + 2) % QUAD)) for...  5.48 us
    ppermute x1, starting transfers between devices, per_device(): other = lax.ppermute(held, 'rep', [(r, r ^ 1) for r in range(reps)])  4.42 us
    ppermute x1, starting transfers between devices, per_device(): lax.ppermute(near, ('rep', 'tp'), [(r * devices + in_quad(q, m), r * devi...  4.35 us
    all_to_all x1, waiting for transfers between devices, per_device(): spans = exchange(own).reshape(QUAD * rows, HEAD_SIZE)  4.22 us
    pallas_call x1, Pallas kernels, start(): pl.pallas_call(start_kernel, out_shape=(jax.ShapeDtypeStruct((QUERY_HEADS...  4.08 us
    all_to_all x1, starting transfers between devices, per_device(): shrinks = exchange(partial, axis_index_groups=lines)  3.28 us
  transfers between devices with their start and end apart: 5, of which 2 were waited for; matrix products, arithmetic and copies ran while one was open for 0% of the time, Pallas kernels for 3%

profile of v10, /device:TPU:1, one launch (start us, length us, event | category | flops | bytes accessed | tf_op | source)
XLA Modules:
  0.0 64.0 jit_solution(3968125798760886781)
XLA Ops:
  0.0 0.0 copy-start.4
  0.0 0.0 copy-start.2
  0.0 0.0 copy-start.3
  0.0 4.1 %start.1 = (bf16[32,16,128]{2,1,0:T(8,128)(2,1)}, bf16[128,2048]{1,0:T(8,128)(2,1)}, bf16[64,2048]{1,0:T(8,128)(2,1)}) custom-call(s32[1]{0:T(128)} %bitcast.2.place_ref, s32[4]{0:T(128)} %len_ref.1, bf16[4,4096]{1,0:T(4,128)(2,1)} %q_hbm.1, bf16[4,256,512]{2,1,0:T(8,128)(2,1)} %k_hbm.1, bf16[4,256,512]{2,1,0:T(8,128)(2,1)} %v_hbm.1, ...), custom_call_target="tpu_custom_call" | custom-call | tf_op jit(solution)/shard_map/start/pallas_call | solution.py:109
  4.1 5.5 %collective-permute-start.1 = (bf16[64,2048]{1,0:T(8,128)(2,1)}, bf16[64,2048]{1,0:T(8,128)(2,1)S(1)}, u32[]{:S(2)}, u32[]{:S(2)}) collective-permute-start(bf16[64,2048]{1,0:T(8,128)(2,1)} %get-tuple-element.14), channel_id=1, source_target_pairs={{0,2},{1,3},{2,0},{3,1},{4,6},{5,7},{6,4},{7,5},{8,10},{9,11},{10,... | collective-permute-start | bytes 786440 | tf_op jit(solution)/shard_map/ppermute | solution.py:355
  9.6 7.8 %all-to-all-start = ((bf16[32,16,128]{2,1,0:T(8,128)(2,1)}), bf16[32,16,128]{2,1,0:T(8,128)(2,1)S(1)}, u32[]{:S(2)}, u32[]{:S(2)}) async-start(bf16[32,16,128]{2,1,0:T(8,128)(2,1)} %get-tuple-element.12), calls=%async_computation | async-start | bytes 262144 | tf_op jit(solution)/shard_map/all_to_all | solution.py:358
  17.4 4.3 %collective-permute-start = (bf16[128,2048]{1,0:T(8,128)(2,1)}, bf16[128,2048]{1,0:T(8,128)(2,1)S(1)}, u32[]{:S(2)}, u32[]{:S(2)}) collective-permute-start(bf16[128,2048]{1,0:T(8,128)(2,1)} %get-tuple-element.13), channel_id=1, source_target_pairs={{0,1},{1,2},{2,3},{3,0},{4,5},{5,6},{6,7},{7,4},{8,9},{9,10},{10,1... | collective-permute-start | bytes 1572872 | tf_op jit(solution)/shard_map/ppermute | solution.py:345
  21.7 0.0 copy-done.4
  21.8 0.1 copy.11.adapter_ref
  21.9 0.0 copy-done.2
  21.9 0.0 copy-done.3
  21.9 0.7 %prepare.1 = (bf16[128,1024]{1,0:T(8,128)(2,1)S(1)}, bf16[16,64,128]{2,1,0:T(8,128)(2,1)S(1)}) custom-call(s32[16]{0:T(128)S(1)} %copy-done.3, s32[128,1]{1,0:T(8,128)S(1)} %copy.11.adapter_ref, bf16[16,64,128]{2,1,0:T(8,128)(2,1)S(1)} %bitcast.6), custom_call_target="tpu_custom_call" | custom-call | tf_op jit(solution)/shard_map/prepare/pallas_call | solution.py:184
  22.6 4.2 %all-to-all-done = bf16[32,16,128]{2,1,0:T(8,128)(2,1)S(1)} async-done(((bf16[32,16,128]{2,1,0:T(8,128)(2,1)}), bf16[32,16,128]{2,1,0:T(8,128)(2,1)S(1)}, u32[]{:S(2)}, u32[]{:S(2)}) %all-to-all-start) | async-done | bytes 131104 | tf_op jit(solution)/shard_map/all_to_all | solution.py:358
  26.8 1.1 %shrink.1.after_hbm = bf16[4,64,128]{2,1,0:T(8,128)(2,1)} custom-call(s32[1]{0:T(128)} %bitcast.2.place_ref, bf16[512,128]{1,0:T(8,128)(2,1)S(1)} %bitcast.4, bf16[16,64,128]{2,1,0:T(8,128)(2,1)S(1)} %get-tuple-element.15.down_ref, bf16[128,1024]{1,0:T(8,128)(2,1)S(1)} %get-tuple-element.11.mask_ref), custom_call_target="tpu_custom_call" | custom-call | tf_op jit(solution)/shard_map/shrink/pallas_call | solution.py:160
  27.9 3.3 %all-to-all-start.1 = ((bf16[4,64,128]{2,1,0:T(8,128)(2,1)}), bf16[4,64,128]{2,1,0:T(8,128)(2,1)S(1)}, u32[]{:S(2)}, u32[]{:S(2)}) async-start(bf16[4,64,128]{2,1,0:T(8,128)(2,1)} %shrink.1.after_hbm), calls=%async_computation.1 | async-start | bytes 131072 | tf_op jit(solution)/shard_map/all_to_all | solution.py:361
  31.1 0.0 collective-permute-done.1.held_hbm
  31.2 0.0 collective-permute-done
  31.2 0.1 pad_maximum_fusion.held_ref
  31.3 0.0 copy-start
  31.3 4.4 %collective-permute-start.2 = (bf16[192,2048]{1,0:T(8,128)(2,1)S(1)}, bf16[192,2048]{1,0:T(8,128)(2,1)}, u32[]{:S(2)}, u32[]{:S(2)}) collective-permute-start(bf16[192,2048]{1,0:T(8,128)(2,1)S(1)} %pad_maximum_fusion.held_ref), channel_id=1, source_target_pairs={{0,32},{32,0},{64,96},{96,64},{128,160},{160,128},{192,224},{224,1... | collective-permute-start | bytes 2359304 | tf_op jit(solution)/shard_map/ppermute | solution.py:364
  35.7 0.4 arrange.1.heads_ref
  36.0 0.0 all-to-all-done.1.shrink_ref
  36.1 1.7 %collective-permute-done.2.other_ref = bf16[192,2048]{1,0:T(8,128)(2,1)} collective-permute-done((bf16[192,2048]{1,0:T(8,128)(2,1)S(1)}, bf16[192,2048]{1,0:T(8,128)(2,1)}, u32[]{:S(2)}, u32[]{:S(2)}) %collective-permute-start.2) | collective-permute-done | bytes 786464 | tf_op jit(solution)/shard_map/ppermute | solution.py:364
  37.7 0.0 copy-done
  37.7 1.6 %project.1 = bf16[8,160,256]{2,1,0:T(8,128)(2,1)S(1)} custom-call(s32[1]{0:T(128)} %bitcast.2.place_ref, bf16[128,512]{1,0:T(8,128)(2,1)S(1)} %arrange.1.heads_ref, bf16[128,8192]{1,0:T(8,128)(2,1)S(1)} %copy-done, bf16[192,2048]{1,0:T(8,128)(2,1)S(1)} %pad_maximum_fusion.held_ref, bf16[192,2048]{1,0:T(8,128)(2,1)} %collective-permute-done.2.other_ref, ...), custom_call_target="tpu_custom_call" | custom-call | tf_op jit(solution)/shard_map/project/pallas_call | solution.py:273
  39.3 0.0 copy-start.1
  39.3 23.7 %all_to_all.15.parts_ref = bf16[8,160,256]{2,1,0:T(8,128)(2,1)S(1)} all-to-all(bf16[8,160,256]{2,1,0:T(8,128)(2,1)S(1)} %project.1), channel_id=1, replica_groups={{0,4,8,12,16,20,24,28},{1,5,9,13,17,21,25,29},{2,6,10,14,18,22,26,30},{..., dimensions={0} | all-to-all | bytes 1310720 | tf_op jit(solution)/shard_map/all_to_all | solution.py:366
  63.0 0.0 copy-done.1
  63.0 0.9 %finish.1 = bf16[128,256]{1,0:T(8,128)(2,1)} custom-call(bf16[128,1024]{1,0:T(8,128)(2,1)S(1)} %get-tuple-element.11.mask_ref, bf16[8,160,256]{2,1,0:T(8,128)(2,1)S(1)} %all_to_all.15.parts_ref, bf16[16,64,256]{2,1,0:T(8,128)(2,1)S(1)} %copy-done.1), custom_call_target="tpu_custom_call" | custom-call | tf_op jit(solution)/shard_map/finish/pallas_call | solution.py:310
  (1 shorter events, 0.0 us)
Async XLA Ops:
  0.0 21.8 %copy-start.4 = (s32[128]{0:T(128)S(1)}, s32[128]{0:T(128)}, u32[]{:S(2)}) copy-start(s32[128]{0:T(128)} %param.13) | copy-start | bytes 1540
  0.0 21.9 %copy-start.2 = (bf16[16,128,64]{1,2,0:T(8,128)(2,1)S(1)}, bf16[16,128,64]{1,2,0:T(8,128)(2,1)}, u32[]{:S(2)}) copy-start(bf16[16,128,64]{1,2,0:T(8,128)(2,1)} %param.16) | copy-start | bytes 786436
  0.0 21.9 %copy-start.3 = (s32[16]{0:T(128)S(1)}, s32[16]{0:T(128)}, u32[]{:S(2)}) copy-start(s32[16]{0:T(128)} %block_ref.1) | copy-start | bytes 196
  4.1 27.1 %collective-permute-start.1 = (bf16[64,2048]{1,0:T(8,128)(2,1)}, bf16[64,2048]{1,0:T(8,128)(2,1)S(1)}, u32[]{:S(2)}, u32[]{:S(2)}) collective-permute-start(bf16[64,2048]{1,0:T(8,128)(2,1)} %get-tuple-element.14), channel_id=1, source_target_pairs={{0,2},{1,3},{2,0},{3,1},{4,6},{5,7},{6,4},{7,5},{8,10},{9,11},{10,... | collective-permute-start | bytes 786440 | tf_op jit(solution)/shard_map/ppermute | solution.py:355
  9.6 17.2 %all-to-all-start = ((bf16[32,16,128]{2,1,0:T(8,128)(2,1)}), bf16[32,16,128]{2,1,0:T(8,128)(2,1)S(1)}, u32[]{:S(2)}, u32[]{:S(2)}) async-start(bf16[32,16,128]{2,1,0:T(8,128)(2,1)} %get-tuple-element.12), calls=%async_computation | async-start | bytes 262144 | tf_op jit(solution)/shard_map/all_to_all | solution.py:358
  17.4 13.8 %collective-permute-start = (bf16[128,2048]{1,0:T(8,128)(2,1)}, bf16[128,2048]{1,0:T(8,128)(2,1)S(1)}, u32[]{:S(2)}, u32[]{:S(2)}) collective-permute-start(bf16[128,2048]{1,0:T(8,128)(2,1)} %get-tuple-element.13), channel_id=1, source_target_pairs={{0,1},{1,2},{2,3},{3,0},{4,5},{5,6},{6,7},{7,4},{8,9},{9,10},{10,1... | collective-permute-start | bytes 1572872 | tf_op jit(solution)/shard_map/ppermute | solution.py:345
  27.9 8.2 %all-to-all-start.1 = ((bf16[4,64,128]{2,1,0:T(8,128)(2,1)}), bf16[4,64,128]{2,1,0:T(8,128)(2,1)S(1)}, u32[]{:S(2)}, u32[]{:S(2)}) async-start(bf16[4,64,128]{2,1,0:T(8,128)(2,1)} %shrink.1.after_hbm), calls=%async_computation.1 | async-start | bytes 131072 | tf_op jit(solution)/shard_map/all_to_all | solution.py:361
  31.3 6.5 %copy-start = (bf16[128,8192]{1,0:T(8,128)(2,1)S(1)}, bf16[128,8192]{1,0:T(8,128)(2,1)}, u32[]{:S(2)}) copy-start(bf16[128,8192]{1,0:T(8,128)(2,1)} %weight_ref.1) | copy-start | bytes 6291460
  31.3 6.4 %collective-permute-start.2 = (bf16[192,2048]{1,0:T(8,128)(2,1)S(1)}, bf16[192,2048]{1,0:T(8,128)(2,1)}, u32[]{:S(2)}, u32[]{:S(2)}) collective-permute-start(bf16[192,2048]{1,0:T(8,128)(2,1)S(1)} %pad_maximum_fusion.held_ref), channel_id=1, source_target_pairs={{0,32},{32,0},{64,96},{96,64},{128,160},{160,128},{192,224},{224,1... | collective-permute-start | bytes 2359304 | tf_op jit(solution)/shard_map/ppermute | solution.py:364
  39.3 23.7 %copy-start.1 = (bf16[16,64,256]{2,1,0:T(8,128)(2,1)S(1)}, bf16[16,64,256]{2,1,0:T(8,128)(2,1)}, u32[]{:S(2)}) copy-start(bf16[16,64,256]{2,1,0:T(8,128)(2,1)} %up_ref.1) | copy-start | bytes 1572868

commit v11 on v10

--- a/solution.py
+++ b/solution.py
@@ -237,9 +237,7 @@
     )(place, spans)
 
 
-def project_kernel(
-    place_ref, heads_ref, weight_ref, held_ref, other_ref, shrink_ref, out_ref
-):
+def project_kernel(place_ref, heads_ref, weight_ref, held_ref, other_ref, out_ref):
     dests, _, width = out_ref.shape
     rows = heads_ref.shape[0]
     heads = heads_ref[...]
@@ -258,26 +256,46 @@
             axis=0,
         )
         out_ref[d, :rows, :] = jnp.dot(heads, stacked, preferred_element_type=F32).astype(BF16)
+
+
+def project(place, heads, weight, held, other, extra):
+    rows = heads.shape[0]
+    dests = held.shape[1] // LINE
+    return pl.pallas_call(
+        project_kernel,
+        out_shape=jax.ShapeDtypeStruct((dests, rows + extra, LINE), BF16),
+        in_specs=[SMEM] + [VMEM] * 4,
+        out_specs=VMEM,
+        compiler_params=PARAMS,
+        cost_estimate=pl.CostEstimate(flops=2**20, bytes_accessed=2**10, transcendentals=0),
+        name="project",
+    )(place, heads, weight, held, other)
+
+
+def append_kernel(parts_hbm, shrink_ref, out_ref):
+    del parts_hbm
     shrink = shrink_ref[0].astype(F32)
     for m in range(1, QUAD):
         shrink += shrink_ref[m].astype(F32)
     half = shrink.shape[0] // 2
     packed = jnp.concatenate([shrink[:half], shrink[half:]], axis=1).astype(BF16)
-    for d in range(dests):
-        out_ref[d, rows:, :] = packed
-
-
-def project(place, heads, weight, held, other, shrinks):
-    rows = heads.shape[0]
-    dests = held.shape[1] // LINE
-    return pl.pallas_call(
-        project_kernel,
-        out_shape=jax.ShapeDtypeStruct((dests, rows + shrinks.shape[1] // 2, LINE), BF16),
-        in_specs=[SMEM] + [VMEM] * 5,
-        out_specs=VMEM,
-        compiler_params=PARAMS,
-        name="project",
-    )(place, heads, weight, held, other, shrinks)
+    for d in range(out_ref.shape[0]):
+        out_ref[d] = packed
+
+
+def append(parts, shrinks):
+    dests, rows, width = parts.shape
+    extra = shrinks.shape[1] // 2
+    return pl.pallas_call(
+        append_kernel,
+        out_shape=jax.ShapeDtypeStruct(parts.shape, parts.dtype),
+        grid=(1,),
+        in_specs=[HBM, VMEM],
+        out_specs=pl.BlockSpec((dests, extra, width), lambda i: (0, rows // extra - 1, 0)),
+        input_output_aliases={0: 0},
+        compiler_params=PARAMS,
+        name="append",
+    )(parts, shrinks)
 
 
 def finish_kernel(mask_ref, parts_ref, up_ref, out_ref):
@@ -363,9 +381,8 @@
     held, _ = lax.optimization_barrier((jnp.concatenate([near, far], axis=0), partial))
     other = lax.ppermute(held, "rep", [(r, r ^ 1) for r in range(reps)])
     heads = arrange(place, spans)
-    parts = exchange(
-        project(place, heads, output_weight, held, other, shrinks), axis_index_groups=groups
-    )
+    parts = project(place, heads, output_weight, held, other, partial.shape[1] // 2)
+    parts = exchange(append(parts, shrinks), axis_index_groups=groups)
     return finish(parts, up_factors, chosen)
 
 

time: 64.7 us -> 63.4 us (0.980)
  Pallas kernels: 8.69 us -> 7.56 us
    pallas_call x1, Pallas kernels: 1.59 us -> 0.44 us  [project(): pl.pallas_call(project_kernel, out_shape=jax.ShapeDtypeStruct((dests, row...]
  transfers between devices with their start and end apart: 5 -> 5, of which waited for: 2 -> 2; matrix products, arithmetic and copies ran while one was open for 0% -> 0% of each run, Pallas kernels for 3% -> 4%
where the time goes in v11:
time: 63.4 us; the launch traced here: 62.6 us
  starting transfers between devices  25.3 us (40%)
  blocking collectives  23.6 us (37%)
  Pallas kernels  7.56 us (12%)
  waiting for transfers between devices  5.76 us (9%)
    all_to_all x1, blocking collectives, per_device(): parts = exchange(append(parts, shrinks), axis_index_groups=groups)  23.6 us
    all_to_all x1, starting transfers between devices, per_device(): spans = exchange(own).reshape(QUAD * rows, HEAD_SIZE)  7.8 us
    ppermute x1, starting transfers between devices, per_device(): lax.ppermute(far, 'tp', [(in_quad(q, m), in_quad(q, (m + 2) % QUAD)) for...  5.48 us
    ppermute x1, starting transfers between devices, per_device(): other = lax.ppermute(held, 'rep', [(r, r ^ 1) for r in range(reps)])  4.41 us
    ppermute x1, starting transfers between devices, per_device(): lax.ppermute(near, ('rep', 'tp'), [(r * devices + in_quad(q, m), r * devi...  4.35 us
    all_to_all x1, waiting for transfers between devices, per_device(): spans = exchange(own).reshape(QUAD * rows, HEAD_SIZE)  4.22 us
    pallas_call x1, Pallas kernels, start(): pl.pallas_call(start_kernel, out_shape=(jax.ShapeDtypeStruct((QUERY_HEADS...  4.08 us
    all_to_all x1, starting transfers between devices, per_device(): shrinks = exchange(partial, axis_index_groups=lines)  3.28 us
  transfers between devices with their start and end apart: 5, of which 2 were waited for; matrix products, arithmetic and copies ran while one was open for 0% of the time, Pallas kernels for 4%

profile of v11, /device:TPU:1, one launch (start us, length us, event | category | flops | bytes accessed | tf_op | source)
XLA Modules:
  0.0 62.6 jit_solution(13741551394593619399)
XLA Ops:
  0.0 0.0 copy-start.4
  0.0 0.0 copy-start.2
  0.0 0.0 copy-start.3
  0.0 4.1 %start.1 = (bf16[32,16,128]{2,1,0:T(8,128)(2,1)}, bf16[128,2048]{1,0:T(8,128)(2,1)}, bf16[64,2048]{1,0:T(8,128)(2,1)}) custom-call(s32[1]{0:T(128)} %bitcast.2.place_ref, s32[4]{0:T(128)} %len_ref.1, bf16[4,4096]{1,0:T(4,128)(2,1)} %q_hbm.1, bf16[4,256,512]{2,1,0:T(8,128)(2,1)} %k_hbm.1, bf16[4,256,512]{2,1,0:T(8,128)(2,1)} %v_hbm.1, ...), custom_call_target="tpu_custom_call" | custom-call | tf_op jit(solution)/shard_map/start/pallas_call | solution.py:109
  4.1 5.5 %collective-permute-start.1 = (bf16[64,2048]{1,0:T(8,128)(2,1)}, bf16[64,2048]{1,0:T(8,128)(2,1)S(1)}, u32[]{:S(2)}, u32[]{:S(2)}) collective-permute-start(bf16[64,2048]{1,0:T(8,128)(2,1)} %get-tuple-element.14), channel_id=1, source_target_pairs={{0,2},{1,3},{2,0},{3,1},{4,6},{5,7},{6,4},{7,5},{8,10},{9,11},{10,... | collective-permute-start | bytes 786440 | tf_op jit(solution)/shard_map/ppermute | solution.py:373
  9.6 7.8 %all-to-all-start = ((bf16[32,16,128]{2,1,0:T(8,128)(2,1)}), bf16[32,16,128]{2,1,0:T(8,128)(2,1)S(1)}, u32[]{:S(2)}, u32[]{:S(2)}) async-start(bf16[32,16,128]{2,1,0:T(8,128)(2,1)} %get-tuple-element.12), calls=%async_computation | async-start | bytes 262144 | tf_op jit(solution)/shard_map/all_to_all | solution.py:376
  17.4 4.3 %collective-permute-start = (bf16[128,2048]{1,0:T(8,128)(2,1)}, bf16[128,2048]{1,0:T(8,128)(2,1)S(1)}, u32[]{:S(2)}, u32[]{:S(2)}) collective-permute-start(bf16[128,2048]{1,0:T(8,128)(2,1)} %get-tuple-element.13), channel_id=1, source_target_pairs={{0,1},{1,2},{2,3},{3,0},{4,5},{5,6},{6,7},{7,4},{8,9},{9,10},{10,1... | collective-permute-start | bytes 1572872 | tf_op jit(solution)/shard_map/ppermute | solution.py:363
  21.7 0.0 copy-done.4
  21.8 0.1 copy.12.adapter_ref
  21.9 0.0 copy-done.2
  21.9 0.0 copy-done.3
  21.9 0.7 %prepare.1 = (bf16[128,1024]{1,0:T(8,128)(2,1)S(1)}, bf16[16,64,128]{2,1,0:T(8,128)(2,1)S(1)}) custom-call(s32[16]{0:T(128)S(1)} %copy-done.3, s32[128,1]{1,0:T(8,128)S(1)} %copy.12.adapter_ref, bf16[16,64,128]{2,1,0:T(8,128)(2,1)S(1)} %bitcast.6), custom_call_target="tpu_custom_call" | custom-call | tf_op jit(solution)/shard_map/prepare/pallas_call | solution.py:184
  22.6 4.2 %all-to-all-done = bf16[32,16,128]{2,1,0:T(8,128)(2,1)S(1)} async-done(((bf16[32,16,128]{2,1,0:T(8,128)(2,1)}), bf16[32,16,128]{2,1,0:T(8,128)(2,1)S(1)}, u32[]{:S(2)}, u32[]{:S(2)}) %all-to-all-start) | async-done | bytes 131104 | tf_op jit(solution)/shard_map/all_to_all | solution.py:376
  26.8 1.1 %shrink.1.after_hbm = bf16[4,64,128]{2,1,0:T(8,128)(2,1)} custom-call(s32[1]{0:T(128)} %bitcast.2.place_ref, bf16[512,128]{1,0:T(8,128)(2,1)S(1)} %bitcast.4, bf16[16,64,128]{2,1,0:T(8,128)(2,1)S(1)} %get-tuple-element.15.down_ref, bf16[128,1024]{1,0:T(8,128)(2,1)S(1)} %get-tuple-element.11.mask_ref), custom_call_target="tpu_custom_call" | custom-call | tf_op jit(solution)/shard_map/shrink/pallas_call | solution.py:160
  27.9 3.3 %all-to-all-start.1 = ((bf16[4,64,128]{2,1,0:T(8,128)(2,1)}), bf16[4,64,128]{2,1,0:T(8,128)(2,1)S(1)}, u32[]{:S(2)}, u32[]{:S(2)}) async-start(bf16[4,64,128]{2,1,0:T(8,128)(2,1)} %shrink.1.after_hbm), calls=%async_computation.1 | async-start | bytes 131072 | tf_op jit(solution)/shard_map/all_to_all | solution.py:379
  31.1 0.0 collective-permute-done.1.held_hbm
  31.2 0.0 collective-permute-done
  31.2 0.1 pad_maximum_fusion.held_ref
  31.3 0.0 copy-start
  31.3 4.4 %collective-permute-start.2 = (bf16[192,2048]{1,0:T(8,128)(2,1)S(1)}, bf16[192,2048]{1,0:T(8,128)(2,1)S(1)}, u32[]{:S(2)}, u32[]{:S(2)}) collective-permute-start(bf16[192,2048]{1,0:T(8,128)(2,1)S(1)} %pad_maximum_fusion.held_ref), channel_id=1, source_target_pairs={{0,32},{32,0},{64,96},{96,64},{128,160},{160,128},{192,224},{224,1... | collective-permute-start | bytes 2359304 | tf_op jit(solution)/shard_map/ppermute | solution.py:382
  35.7 0.4 arrange.1.heads_ref
  36.0 1.5 %collective-permute-done.2.other_ref = bf16[192,2048]{1,0:T(8,128)(2,1)S(1)} collective-permute-done((bf16[192,2048]{1,0:T(8,128)(2,1)S(1)}, bf16[192,2048]{1,0:T(8,128)(2,1)S(1)}, u32[]{:S(2)}, u32[]{:S(2)}) %collective-permute-start.2) | collective-permute-done | bytes 786464 | tf_op jit(solution)/shard_map/ppermute | solution.py:382
  37.6 0.0 copy-done
  37.6 0.4 project.1.parts_hbm
  38.0 0.0 copy-start.1
  38.0 0.0 all-to-all-done.1.shrink_ref
  38.1 23.6 %all_to_all.15.parts_ref = bf16[8,160,256]{2,1,0:T(8,128)(2,1)S(1)} all-to-all(bf16[8,160,256]{2,1,0:T(8,128)(2,1)S(1)} %append.1), channel_id=1, replica_groups={{0,4,8,12,16,20,24,28},{1,5,9,13,17,21,25,29},{2,6,10,14,18,22,26,30},{..., dimensions={0} | all-to-all | bytes 1310720 | tf_op jit(solution)/shard_map/all_to_all | solution.py:385
  61.7 0.0 copy-done.1
  61.7 0.9 %finish.1 = bf16[128,256]{1,0:T(8,128)(2,1)} custom-call(bf16[128,1024]{1,0:T(8,128)(2,1)S(1)} %get-tuple-element.11.mask_ref, bf16[8,160,256]{2,1,0:T(8,128)(2,1)S(1)} %all_to_all.15.parts_ref, bf16[16,64,256]{2,1,0:T(8,128)(2,1)S(1)} %copy-done.1), custom_call_target="tpu_custom_call" | custom-call | tf_op jit(solution)/shard_map/finish/pallas_call | solution.py:328
  (2 shorter events, 0.0 us)
Async XLA Ops:
  0.0 21.8 %copy-start.4 = (s32[128]{0:T(128)S(1)}, s32[128]{0:T(128)}, u32[]{:S(2)}) copy-start(s32[128]{0:T(128)} %param.13) | copy-start | bytes 1540
  0.0 21.9 %copy-start.2 = (bf16[16,128,64]{1,2,0:T(8,128)(2,1)S(1)}, bf16[16,128,64]{1,2,0:T(8,128)(2,1)}, u32[]{:S(2)}) copy-start(bf16[16,128,64]{1,2,0:T(8,128)(2,1)} %param.16) | copy-start | bytes 786436
  0.0 21.9 %copy-start.3 = (s32[16]{0:T(128)S(1)}, s32[16]{0:T(128)}, u32[]{:S(2)}) copy-start(s32[16]{0:T(128)} %block_ref.1) | copy-start | bytes 196
  4.1 27.1 %collective-permute-start.1 = (bf16[64,2048]{1,0:T(8,128)(2,1)}, bf16[64,2048]{1,0:T(8,128)(2,1)S(1)}, u32[]{:S(2)}, u32[]{:S(2)}) collective-permute-start(bf16[64,2048]{1,0:T(8,128)(2,1)} %get-tuple-element.14), channel_id=1, source_target_pairs={{0,2},{1,3},{2,0},{3,1},{4,6},{5,7},{6,4},{7,5},{8,10},{9,11},{10,... | collective-permute-start | bytes 786440 | tf_op jit(solution)/shard_map/ppermute | solution.py:373
  9.6 17.2 %all-to-all-start = ((bf16[32,16,128]{2,1,0:T(8,128)(2,1)}), bf16[32,16,128]{2,1,0:T(8,128)(2,1)S(1)}, u32[]{:S(2)}, u32[]{:S(2)}) async-start(bf16[32,16,128]{2,1,0:T(8,128)(2,1)} %get-tuple-element.12), calls=%async_computation | async-start | bytes 262144 | tf_op jit(solution)/shard_map/all_to_all | solution.py:376
  17.4 13.8 %collective-permute-start = (bf16[128,2048]{1,0:T(8,128)(2,1)}, bf16[128,2048]{1,0:T(8,128)(2,1)S(1)}, u32[]{:S(2)}, u32[]{:S(2)}) collective-permute-start(bf16[128,2048]{1,0:T(8,128)(2,1)} %get-tuple-element.13), channel_id=1, source_target_pairs={{0,1},{1,2},{2,3},{3,0},{4,5},{5,6},{6,7},{7,4},{8,9},{9,10},{10,1... | collective-permute-start | bytes 1572872 | tf_op jit(solution)/shard_map/ppermute | solution.py:363
  27.9 10.2 %all-to-all-start.1 = ((bf16[4,64,128]{2,1,0:T(8,128)(2,1)}), bf16[4,64,128]{2,1,0:T(8,128)(2,1)S(1)}, u32[]{:S(2)}, u32[]{:S(2)}) async-start(bf16[4,64,128]{2,1,0:T(8,128)(2,1)} %shrink.1.after_hbm), calls=%async_computation.1 | async-start | bytes 131072 | tf_op jit(solution)/shard_map/all_to_all | solution.py:379
  31.3 6.3 %copy-start = (bf16[128,8192]{1,0:T(8,128)(2,1)S(1)}, bf16[128,8192]{1,0:T(8,128)(2,1)}, u32[]{:S(2)}) copy-start(bf16[128,8192]{1,0:T(8,128)(2,1)} %weight_ref.1) | copy-start | bytes 6291460
  31.3 6.3 %collective-permute-start.2 = (bf16[192,2048]{1,0:T(8,128)(2,1)S(1)}, bf16[192,2048]{1,0:T(8,128)(2,1)S(1)}, u32[]{:S(2)}, u32[]{:S(2)}) collective-permute-start(bf16[192,2048]{1,0:T(8,128)(2,1)S(1)} %pad_maximum_fusion.held_ref), channel_id=1, source_target_pairs={{0,32},{32,0},{64,96},{96,64},{128,160},{160,128},{192,224},{224,1... | collective-permute-start | bytes 2359304 | tf_op jit(solution)/shard_map/ppermute | solution.py:382
  38.0 23.7 %copy-start.1 = (bf16[16,64,256]{2,1,0:T(8,128)(2,1)S(1)}, bf16[16,64,256]{2,1,0:T(8,128)(2,1)}, u32[]{:S(2)}) copy-start(bf16[16,64,256]{2,1,0:T(8,128)(2,1)} %up_ref.1) | copy-start | bytes 1572868

commit v12 on v11

--- a/solution.py
+++ b/solution.py
@@ -27,9 +27,9 @@
 
 
 def start_kernel(
-    place_ref, len_ref, q_hbm, k_hbm, v_hbm, w_hbm, heads_ref, near_ref, far_ref, *scratch
+    place_ref, len_ref, q_ref, k_hbm, v_hbm, w_hbm, heads_ref, near_ref, far_ref, *scratch
 ):
-    q_ref, k_ref, v_ref, q_sem, k_sem, v_sem, w_sem = scratch
+    k_ref, v_ref, k_sem, v_sem, w_sem = scratch
     rows, size = k_ref.shape[0], HEAD_SIZE
     k_copies = [pltpu.make_async_copy(k_hbm, k_ref, k_sem)]
     v_copies = [pltpu.make_async_copy(v_hbm, v_ref, v_sem)]
@@ -49,11 +49,9 @@
         w_copies.append(
             pltpu.make_async_copy(w_hbm.at[half, source], far_ref.at[:, columns], w_sem.at[1, q])
         )
-    q_copy = pltpu.make_async_copy(q_hbm, q_ref, q_sem)
-    for copy in [q_copy] + k_copies + v_copies:
+    for copy in k_copies + v_copies:
         copy.start()
 
-    q_copy.wait()
     q = q_ref[...].astype(F32)
     q_rows = jnp.concatenate(
         [q[:, h * size : (h + 1) * size] for h in range(QUERY_HEADS)], axis=0
@@ -113,9 +111,9 @@
             jax.ShapeDtypeStruct((depth, span), BF16),
             jax.ShapeDtypeStruct((depth // 2, span), BF16),
         ),
-        in_specs=[SMEM, SMEM, HBM, HBM, HBM, HBM],
+        in_specs=[SMEM, SMEM, VMEM, HBM, HBM, HBM],
         out_specs=(VMEM,) * 3,
-        scratch_shapes=[pltpu.VMEM(queries.shape, BF16), cache, cache, pltpu.SemaphoreType.DMA]
+        scratch_shapes=[cache, cache]
         + [pltpu.SemaphoreType.DMA] * 2
         + [pltpu.SemaphoreType.DMA((2, span // LINE))],
         compiler_params=WHOLE,

time: 63.4 us -> 63.7 us (level)
  no operation moved by 1% of the time
where the time goes in v12:
time: 63.7 us; the launch traced here: 63 us
  starting transfers between devices  25.3 us (40%)
  blocking collectives  23.6 us (37%)
  Pallas kernels  7.91 us (12%)
  waiting for transfers between devices  5.75 us (9%)
    all_to_all x1, blocking collectives, per_device(): parts = exchange(append(parts, shrinks), axis_index_groups=groups)  23.6 us
    all_to_all x1, starting transfers between devices, per_device(): spans = exchange(own).reshape(QUAD * rows, HEAD_SIZE)  7.8 us
    ppermute x1, starting transfers between devices, per_device(): lax.ppermute(far, 'tp', [(in_quad(q, m), in_quad(q, (m + 2) % QUAD)) for...  5.48 us
    pallas_call x1, Pallas kernels, start(): pl.pallas_call(start_kernel, out_shape=(jax.ShapeDtypeStruct((QUERY_HEADS...  4.42 us
    ppermute x1, starting transfers between devices, per_device(): other = lax.ppermute(held, 'rep', [(r, r ^ 1) for r in range(reps)])  4.41 us
    ppermute x1, starting transfers between devices, per_device(): lax.ppermute(near, ('rep', 'tp'), [(r * devices + in_quad(q, m), r * devi...  4.35 us
    all_to_all x1, waiting for transfers between devices, per_device(): spans = exchange(own).reshape(QUAD * rows, HEAD_SIZE)  4.21 us
    all_to_all x1, starting transfers between devices, per_device(): shrinks = exchange(partial, axis_index_groups=lines)  3.28 us
  transfers between devices with their start and end apart: 5, of which 2 were waited for; matrix products, arithmetic and copies ran while one was open for 0% of the time, Pallas kernels for 4%

profile of v12, /device:TPU:1, one launch (start us, length us, event | category | flops | bytes accessed | tf_op | source)
XLA Modules:
  0.0 63.0 jit_solution(12622211531621150034)
XLA Ops:
  0.0 0.0 copy-start.4
  0.0 0.0 copy-start.2
  0.0 0.0 copy-start.3
  0.0 4.4 %start.1 = (bf16[32,16,128]{2,1,0:T(8,128)(2,1)}, bf16[128,2048]{1,0:T(8,128)(2,1)}, bf16[64,2048]{1,0:T(8,128)(2,1)}) custom-call(s32[1]{0:T(128)} %bitcast.2.place_ref, s32[4]{0:T(128)} %len_ref.1, bf16[4,4096]{1,0:T(4,128)(2,1)} %q_ref.1, bf16[4,256,512]{2,1,0:T(8,128)(2,1)} %k_hbm.1, bf16[4,256,512]{2,1,0:T(8,128)(2,1)} %v_hbm.1, ...), custom_call_target="tpu_custom_call" | custom-call | tf_op jit(solution)/shard_map/start/pallas_call | solution.py:107
  4.4 5.5 %collective-permute-start.1 = (bf16[64,2048]{1,0:T(8,128)(2,1)}, bf16[64,2048]{1,0:T(8,128)(2,1)S(1)}, u32[]{:S(2)}, u32[]{:S(2)}) collective-permute-start(bf16[64,2048]{1,0:T(8,128)(2,1)} %get-tuple-element.14), channel_id=1, source_target_pairs={{0,2},{1,3},{2,0},{3,1},{4,6},{5,7},{6,4},{7,5},{8,10},{9,11},{10,... | collective-permute-start | bytes 786440 | tf_op jit(solution)/shard_map/ppermute | solution.py:371
  9.9 7.8 %all-to-all-start = ((bf16[32,16,128]{2,1,0:T(8,128)(2,1)}), bf16[32,16,128]{2,1,0:T(8,128)(2,1)S(1)}, u32[]{:S(2)}, u32[]{:S(2)}) async-start(bf16[32,16,128]{2,1,0:T(8,128)(2,1)} %get-tuple-element.12), calls=%async_computation | async-start | bytes 262144 | tf_op jit(solution)/shard_map/all_to_all | solution.py:374
  17.7 4.3 %collective-permute-start = (bf16[128,2048]{1,0:T(8,128)(2,1)}, bf16[128,2048]{1,0:T(8,128)(2,1)S(1)}, u32[]{:S(2)}, u32[]{:S(2)}) collective-permute-start(bf16[128,2048]{1,0:T(8,128)(2,1)} %get-tuple-element.13), channel_id=1, source_target_pairs={{0,1},{1,2},{2,3},{3,0},{4,5},{5,6},{6,7},{7,4},{8,9},{9,10},{10,1... | collective-permute-start | bytes 1572872 | tf_op jit(solution)/shard_map/ppermute | solution.py:361
  22.1 0.0 copy-done.4
  22.1 0.1 copy.12.adapter_ref
  22.2 0.0 copy-done.2
  22.2 0.0 copy-done.3
  22.2 0.7 %prepare.1 = (bf16[128,1024]{1,0:T(8,128)(2,1)S(1)}, bf16[16,64,128]{2,1,0:T(8,128)(2,1)S(1)}) custom-call(s32[16]{0:T(128)S(1)} %copy-done.3, s32[128,1]{1,0:T(8,128)S(1)} %copy.12.adapter_ref, bf16[16,64,128]{2,1,0:T(8,128)(2,1)S(1)} %bitcast.6), custom_call_target="tpu_custom_call" | custom-call | tf_op jit(solution)/shard_map/prepare/pallas_call | solution.py:182
  22.9 4.2 %all-to-all-done = bf16[32,16,128]{2,1,0:T(8,128)(2,1)S(1)} async-done(((bf16[32,16,128]{2,1,0:T(8,128)(2,1)}), bf16[32,16,128]{2,1,0:T(8,128)(2,1)S(1)}, u32[]{:S(2)}, u32[]{:S(2)}) %all-to-all-start) | async-done | bytes 131104 | tf_op jit(solution)/shard_map/all_to_all | solution.py:374
  27.1 1.1 %shrink.1.after_hbm = bf16[4,64,128]{2,1,0:T(8,128)(2,1)} custom-call(s32[1]{0:T(128)} %bitcast.2.place_ref, bf16[512,128]{1,0:T(8,128)(2,1)S(1)} %bitcast.4, bf16[16,64,128]{2,1,0:T(8,128)(2,1)S(1)} %get-tuple-element.15.down_ref, bf16[128,1024]{1,0:T(8,128)(2,1)S(1)} %get-tuple-element.11.mask_ref), custom_call_target="tpu_custom_call" | custom-call | tf_op jit(solution)/shard_map/shrink/pallas_call | solution.py:158
  28.2 3.3 %all-to-all-start.1 = ((bf16[4,64,128]{2,1,0:T(8,128)(2,1)}), bf16[4,64,128]{2,1,0:T(8,128)(2,1)S(1)}, u32[]{:S(2)}, u32[]{:S(2)}) async-start(bf16[4,64,128]{2,1,0:T(8,128)(2,1)} %shrink.1.after_hbm), calls=%async_computation.1 | async-start | bytes 131072 | tf_op jit(solution)/shard_map/all_to_all | solution.py:377
  31.5 0.0 collective-permute-done.1.held_hbm
  31.5 0.0 collective-permute-done
  31.5 0.1 pad_maximum_fusion.held_ref
  31.6 0.0 copy-start
  31.6 4.4 %collective-permute-start.2 = (bf16[192,2048]{1,0:T(8,128)(2,1)S(1)}, bf16[192,2048]{1,0:T(8,128)(2,1)S(1)}, u32[]{:S(2)}, u32[]{:S(2)}) collective-permute-start(bf16[192,2048]{1,0:T(8,128)(2,1)S(1)} %pad_maximum_fusion.held_ref), channel_id=1, source_target_pairs={{0,32},{32,0},{64,96},{96,64},{128,160},{160,128},{192,224},{224,1... | collective-permute-start | bytes 2359304 | tf_op jit(solution)/shard_map/ppermute | solution.py:380
  36.0 0.4 arrange.1.heads_ref
  36.4 1.5 %collective-permute-done.2.other_ref = bf16[192,2048]{1,0:T(8,128)(2,1)S(1)} collective-permute-done((bf16[192,2048]{1,0:T(8,128)(2,1)S(1)}, bf16[192,2048]{1,0:T(8,128)(2,1)S(1)}, u32[]{:S(2)}, u32[]{:S(2)}) %collective-permute-start.2) | collective-permute-done | bytes 786464 | tf_op jit(solution)/shard_map/ppermute | solution.py:380
  37.9 0.0 copy-done
  37.9 0.4 project.1.parts_hbm
  38.4 0.0 copy-start.1
  38.4 0.0 all-to-all-done.1.shrink_ref
  38.4 23.6 %all_to_all.15.parts_ref = bf16[8,160,256]{2,1,0:T(8,128)(2,1)S(1)} all-to-all(bf16[8,160,256]{2,1,0:T(8,128)(2,1)S(1)} %append.1), channel_id=1, replica_groups={{0,4,8,12,16,20,24,28},{1,5,9,13,17,21,25,29},{2,6,10,14,18,22,26,30},{..., dimensions={0} | all-to-all | bytes 1310720 | tf_op jit(solution)/shard_map/all_to_all | solution.py:383
  62.1 0.0 copy-done.1
  62.1 0.9 %finish.1 = bf16[128,256]{1,0:T(8,128)(2,1)} custom-call(bf16[128,1024]{1,0:T(8,128)(2,1)S(1)} %get-tuple-element.11.mask_ref, bf16[8,160,256]{2,1,0:T(8,128)(2,1)S(1)} %all_to_all.15.parts_ref, bf16[16,64,256]{2,1,0:T(8,128)(2,1)S(1)} %copy-done.1), custom_call_target="tpu_custom_call" | custom-call | tf_op jit(solution)/shard_map/finish/pallas_call | solution.py:326
  (2 shorter events, 0.0 us)
Async XLA Ops:
  0.0 22.1 %copy-start.4 = (s32[128]{0:T(128)S(1)}, s32[128]{0:T(128)}, u32[]{:S(2)}) copy-start(s32[128]{0:T(128)} %param.13) | copy-start | bytes 1540
  0.0 22.2 %copy-start.2 = (bf16[16,128,64]{1,2,0:T(8,128)(2,1)S(1)}, bf16[16,128,64]{1,2,0:T(8,128)(2,1)}, u32[]{:S(2)}) copy-start(bf16[16,128,64]{1,2,0:T(8,128)(2,1)} %param.16) | copy-start | bytes 786436
  0.0 22.2 %copy-start.3 = (s32[16]{0:T(128)S(1)}, s32[16]{0:T(128)}, u32[]{:S(2)}) copy-start(s32[16]{0:T(128)} %block_ref.1) | copy-start | bytes 196
  4.4 27.1 %collective-permute-start.1 = (bf16[64,2048]{1,0:T(8,128)(2,1)}, bf16[64,2048]{1,0:T(8,128)(2,1)S(1)}, u32[]{:S(2)}, u32[]{:S(2)}) collective-permute-start(bf16[64,2048]{1,0:T(8,128)(2,1)} %get-tuple-element.14), channel_id=1, source_target_pairs={{0,2},{1,3},{2,0},{3,1},{4,6},{5,7},{6,4},{7,5},{8,10},{9,11},{10,... | collective-permute-start | bytes 786440 | tf_op jit(solution)/shard_map/ppermute | solution.py:371
  9.9 17.2 %all-to-all-start = ((bf16[32,16,128]{2,1,0:T(8,128)(2,1)}), bf16[32,16,128]{2,1,0:T(8,128)(2,1)S(1)}, u32[]{:S(2)}, u32[]{:S(2)}) async-start(bf16[32,16,128]{2,1,0:T(8,128)(2,1)} %get-tuple-element.12), calls=%async_computation | async-start | bytes 262144 | tf_op jit(solution)/shard_map/all_to_all | solution.py:374
  17.7 13.8 %collective-permute-start = (bf16[128,2048]{1,0:T(8,128)(2,1)}, bf16[128,2048]{1,0:T(8,128)(2,1)S(1)}, u32[]{:S(2)}, u32[]{:S(2)}) collective-permute-start(bf16[128,2048]{1,0:T(8,128)(2,1)} %get-tuple-element.13), channel_id=1, source_target_pairs={{0,1},{1,2},{2,3},{3,0},{4,5},{5,6},{6,7},{7,4},{8,9},{9,10},{10,1... | collective-permute-start | bytes 1572872 | tf_op jit(solution)/shard_map/ppermute | solution.py:361
  28.2 10.2 %all-to-all-start.1 = ((bf16[4,64,128]{2,1,0:T(8,128)(2,1)}), bf16[4,64,128]{2,1,0:T(8,128)(2,1)S(1)}, u32[]{:S(2)}, u32[]{:S(2)}) async-start(bf16[4,64,128]{2,1,0:T(8,128)(2,1)} %shrink.1.after_hbm), calls=%async_computation.1 | async-start | bytes 131072 | tf_op jit(solution)/shard_map/all_to_all | solution.py:377
  31.6 6.3 %copy-start = (bf16[128,8192]{1,0:T(8,128)(2,1)S(1)}, bf16[128,8192]{1,0:T(8,128)(2,1)}, u32[]{:S(2)}) copy-start(bf16[128,8192]{1,0:T(8,128)(2,1)} %weight_ref.1) | copy-start | bytes 6291460
  31.6 6.3 %collective-permute-start.2 = (bf16[192,2048]{1,0:T(8,128)(2,1)S(1)}, bf16[192,2048]{1,0:T(8,128)(2,1)S(1)}, u32[]{:S(2)}, u32[]{:S(2)}) collective-permute-start(bf16[192,2048]{1,0:T(8,128)(2,1)S(1)} %pad_maximum_fusion.held_ref), channel_id=1, source_target_pairs={{0,32},{32,0},{64,96},{96,64},{128,160},{160,128},{192,224},{224,1... | collective-permute-start | bytes 2359304 | tf_op jit(solution)/shard_map/ppermute | solution.py:380
  38.4 23.7 %copy-start.1 = (bf16[16,64,256]{2,1,0:T(8,128)(2,1)S(1)}, bf16[16,64,256]{2,1,0:T(8,128)(2,1)}, u32[]{:S(2)}) copy-start(bf16[16,64,256]{2,1,0:T(8,128)(2,1)} %up_ref.1) | copy-start | bytes 1572868

commit v13 on v12

--- a/solution.py
+++ b/solution.py
@@ -161,6 +161,7 @@
         in_specs=[SMEM, VMEM, VMEM, VMEM],
         out_specs=VMEM,
         compiler_params=PARAMS,
+        cost_estimate=pl.CostEstimate(flops=10**9, bytes_accessed=2**20, transcendentals=0),
         name="shrink",
     )(place, spans, down, chosen)
 
@@ -191,23 +192,6 @@
         compiler_params=PARAMS,
         name="prepare",
     )(block_adapter, adapter_col, down)
-
-
-def pass_kernel(held_hbm, after_hbm, out_hbm):
-    del held_hbm, after_hbm, out_hbm
-
-
-def pass_on(held, after):
-    return pl.pallas_call(
-        pass_kernel,
-        out_shape=jax.ShapeDtypeStruct(held.shape, held.dtype),
-        in_specs=[HBM] * 2,
-        out_specs=HBM,
-        input_output_aliases={0: 0},
-        compiler_params=PARAMS,
-        cost_estimate=pl.CostEstimate(flops=10**10, bytes_accessed=2**18, transcendentals=0),
-        name="pass_on",
-    )(held, after)
 
 
 def arrange_kernel(place_ref, spans_ref, out_ref):
@@ -375,7 +359,6 @@
     chosen, down = prepare(adapter_col, block_adapter, jnp.swapaxes(down_factors, 1, 2))
     partial = shrink_parts(place, spans, down, chosen)
     shrinks = exchange(partial, axis_index_groups=lines)
-    far = pass_on(far, partial)
     held, _ = lax.optimization_barrier((jnp.concatenate([near, far], axis=0), partial))
     other = lax.ppermute(held, "rep", [(r, r ^ 1) for r in range(reps)])
     heads = arrange(place, spans)

time: 63.7 us -> 64 us (level)
  the two profiles are of different devices: /device:TPU:1 before, /device:TPU:3 now
where the time goes in v13:
time: 64 us; the launch traced here: 63.6 us
  starting transfers between devices  27 us (42%)
  blocking collectives  23.3 us (36%)
  Pallas kernels  7.93 us (12%)
  waiting for transfers between devices  5.03 us (8%)
    all_to_all x1, blocking collectives, per_device(): parts = exchange(append(parts, shrinks), axis_index_groups=groups)  23.3 us
    all_to_all x1, starting transfers between devices, per_device(): spans = exchange(own).reshape(QUAD * rows, HEAD_SIZE)  9.97 us
    ppermute x1, starting transfers between devices, per_device(): other = lax.ppermute(held, 'rep', [(r, r ^ 1) for r in range(reps)])  6.55 us
    all_to_all x1, starting transfers between devices, per_device(): shrinks = exchange(partial, axis_index_groups=lines)  4.9 us
    pallas_call x1, Pallas kernels, start(): pl.pallas_call(start_kernel, out_shape=(jax.ShapeDtypeStruct((QUERY_HEADS...  4.43 us
    ppermute x1, starting transfers between devices, per_device(): lax.ppermute(far, 'tp', [(in_quad(q, m), in_quad(q, (m + 2) % QUAD)) for...  3.7 us
    all_to_all x1, waiting for transfers between devices, per_device(): spans = exchange(own).reshape(QUAD * rows, HEAD_SIZE)  3.49 us
    ppermute x1, starting transfers between devices, per_device(): lax.ppermute(near, ('rep', 'tp'), [(r * devices + in_quad(q, m), r * devi...  1.92 us
  transfers between devices with their start and end apart: 5, of which 2 were waited for; matrix products, arithmetic and copies ran while one was open for 0% of the time, Pallas kernels for 4%

profile of v13, /device:TPU:3, one launch (start us, length us, event | category | flops | bytes accessed | tf_op | source)
XLA Modules:
  0.0 63.6 jit_solution(17228459778571738956)
XLA Ops:
  0.0 0.0 copy-start.4
  0.0 0.0 copy-start.2
  0.0 0.0 copy-start.3
  0.0 4.4 %start.1 = (bf16[32,16,128]{2,1,0:T(8,128)(2,1)}, bf16[128,2048]{1,0:T(8,128)(2,1)}, bf16[64,2048]{1,0:T(8,128)(2,1)}) custom-call(s32[1]{0:T(128)} %bitcast.2.place_ref, s32[4]{0:T(128)} %len_ref.1, bf16[4,4096]{1,0:T(4,128)(2,1)} %q_ref.1, bf16[4,256,512]{2,1,0:T(8,128)(2,1)} %k_hbm.1, bf16[4,256,512]{2,1,0:T(8,128)(2,1)} %v_hbm.1, ...), custom_call_target="tpu_custom_call" | custom-call | tf_op jit(solution)/shard_map/start/pallas_call | solution.py:107
  4.4 1.9 %collective-permute-start = (bf16[128,2048]{1,0:T(8,128)(2,1)}, bf16[128,2048]{1,0:T(8,128)(2,1)S(1)}, u32[]{:S(2)}, u32[]{:S(2)}) collective-permute-start(bf16[128,2048]{1,0:T(8,128)(2,1)} %get-tuple-element.13), channel_id=1, source_target_pairs={{0,1},{1,2},{2,3},{3,0},{4,5},{5,6},{6,7},{7,4},{8,9},{9,10},{10,1... | collective-permute-start | bytes 1572872 | tf_op jit(solution)/shard_map/ppermute | solution.py:345
  6.4 10.0 %all-to-all-start = ((bf16[32,16,128]{2,1,0:T(8,128)(2,1)}), bf16[32,16,128]{2,1,0:T(8,128)(2,1)S(1)}, u32[]{:S(2)}, u32[]{:S(2)}) async-start(bf16[32,16,128]{2,1,0:T(8,128)(2,1)} %get-tuple-element.12), calls=%async_computation | async-start | bytes 262144 | tf_op jit(solution)/shard_map/all_to_all | solution.py:358
  16.3 3.7 %collective-permute-start.1 = (bf16[64,2048]{1,0:T(8,128)(2,1)}, bf16[64,2048]{1,0:T(8,128)(2,1)S(1)}, u32[]{:S(2)}, u32[]{:S(2)}) collective-permute-start(bf16[64,2048]{1,0:T(8,128)(2,1)} %get-tuple-element.14), channel_id=1, source_target_pairs={{0,2},{1,3},{2,0},{3,1},{4,6},{5,7},{6,4},{7,5},{8,10},{9,11},{10,... | collective-permute-start | bytes 786440 | tf_op jit(solution)/shard_map/ppermute | solution.py:355
  20.1 0.0 copy-done.4
  20.1 0.1 copy.11.adapter_ref
  20.2 0.0 copy-done.2
  20.2 0.0 copy-done.3
  20.2 0.7 %prepare.1 = (bf16[128,1024]{1,0:T(8,128)(2,1)S(1)}, bf16[16,64,128]{2,1,0:T(8,128)(2,1)S(1)}) custom-call(s32[16]{0:T(128)S(1)} %copy-done.3, s32[128,1]{1,0:T(8,128)S(1)} %copy.11.adapter_ref, bf16[16,64,128]{2,1,0:T(8,128)(2,1)S(1)} %bitcast.4), custom_call_target="tpu_custom_call" | custom-call | tf_op jit(solution)/shard_map/prepare/pallas_call | solution.py:183
  20.9 3.5 %all-to-all-done = bf16[32,16,128]{2,1,0:T(8,128)(2,1)S(1)} async-done(((bf16[32,16,128]{2,1,0:T(8,128)(2,1)}), bf16[32,16,128]{2,1,0:T(8,128)(2,1)S(1)}, u32[]{:S(2)}, u32[]{:S(2)}) %all-to-all-start) | async-done | bytes 131104 | tf_op jit(solution)/shard_map/all_to_all | solution.py:358
  24.4 1.1 %shrink.1 = bf16[4,64,128]{2,1,0:T(8,128)(2,1)} custom-call(s32[1]{0:T(128)} %bitcast.2.place_ref, bf16[512,128]{1,0:T(8,128)(2,1)S(1)} %bitcast.5, bf16[16,64,128]{2,1,0:T(8,128)(2,1)S(1)} %get-tuple-element.15.down_ref, bf16[128,1024]{1,0:T(8,128)(2,1)S(1)} %get-tuple-element.11.mask_ref), custom_call_target="tpu_custom_call" | custom-call | flops 1000000000 | bytes 1048576 | tf_op jit(solution)/shard_map/shrink/pallas_call | solution.py:158
  25.4 4.9 %all-to-all-start.1 = ((bf16[4,64,128]{2,1,0:T(8,128)(2,1)}), bf16[4,64,128]{2,1,0:T(8,128)(2,1)S(1)}, u32[]{:S(2)}, u32[]{:S(2)}) async-start(bf16[4,64,128]{2,1,0:T(8,128)(2,1)} %shrink.1), calls=%async_computation.1 | async-start | bytes 131072 | tf_op jit(solution)/shard_map/all_to_all | solution.py:361
  30.3 0.0 collective-permute-done.1
  30.3 0.0 collective-permute-done
  30.3 0.1 pad_maximum_fusion.held_ref
  30.4 0.0 copy-start
  30.4 6.5 %collective-permute-start.2 = (bf16[192,2048]{1,0:T(8,128)(2,1)S(1)}, bf16[192,2048]{1,0:T(8,128)(2,1)S(1)}, u32[]{:S(2)}, u32[]{:S(2)}) collective-permute-start(bf16[192,2048]{1,0:T(8,128)(2,1)S(1)} %pad_maximum_fusion.held_ref), channel_id=1, source_target_pairs={{0,32},{32,0},{64,96},{96,64},{128,160},{160,128},{192,224},{224,1... | collective-permute-start | bytes 2359304 | tf_op jit(solution)/shard_map/ppermute | solution.py:363
  37.0 0.4 arrange.1.heads_ref
  37.3 1.5 %collective-permute-done.2.other_ref = bf16[192,2048]{1,0:T(8,128)(2,1)S(1)} collective-permute-done((bf16[192,2048]{1,0:T(8,128)(2,1)S(1)}, bf16[192,2048]{1,0:T(8,128)(2,1)S(1)}, u32[]{:S(2)}, u32[]{:S(2)}) %collective-permute-start.2) | collective-permute-done | bytes 786464 | tf_op jit(solution)/shard_map/ppermute | solution.py:363
  38.9 0.0 copy-done
  38.9 0.5 project.1.parts_hbm
  39.3 0.0 copy-start.1
  39.4 0.0 all-to-all-done.1.shrink_ref
  39.4 23.3 %all_to_all.15.parts_ref = bf16[8,160,256]{2,1,0:T(8,128)(2,1)S(1)} all-to-all(bf16[8,160,256]{2,1,0:T(8,128)(2,1)S(1)} %append.1), channel_id=1, replica_groups={{0,4,8,12,16,20,24,28},{1,5,9,13,17,21,25,29},{2,6,10,14,18,22,26,30},{..., dimensions={0} | all-to-all | bytes 1310720 | tf_op jit(solution)/shard_map/all_to_all | solution.py:366
  62.7 0.0 copy-done.1
  62.7 0.9 %finish.1 = bf16[128,256]{1,0:T(8,128)(2,1)} custom-call(bf16[128,1024]{1,0:T(8,128)(2,1)S(1)} %get-tuple-element.11.mask_ref, bf16[8,160,256]{2,1,0:T(8,128)(2,1)S(1)} %all_to_all.15.parts_ref, bf16[16,64,256]{2,1,0:T(8,128)(2,1)S(1)} %copy-done.1), custom_call_target="tpu_custom_call" | custom-call | tf_op jit(solution)/shard_map/finish/pallas_call | solution.py:310
  (1 shorter events, 0.0 us)
Async XLA Ops:
  0.0 20.1 %copy-start.4 = (s32[128]{0:T(128)S(1)}, s32[128]{0:T(128)}, u32[]{:S(2)}) copy-start(s32[128]{0:T(128)} %param.13) | copy-start | bytes 1540
  0.0 20.2 %copy-start.2 = (bf16[16,128,64]{1,2,0:T(8,128)(2,1)S(1)}, bf16[16,128,64]{1,2,0:T(8,128)(2,1)}, u32[]{:S(2)}) copy-start(bf16[16,128,64]{1,2,0:T(8,128)(2,1)} %param.16) | copy-start | bytes 786436
  0.0 20.2 %copy-start.3 = (s32[16]{0:T(128)S(1)}, s32[16]{0:T(128)}, u32[]{:S(2)}) copy-start(s32[16]{0:T(128)} %block_ref.1) | copy-start | bytes 196
  4.4 25.9 %collective-permute-start = (bf16[128,2048]{1,0:T(8,128)(2,1)}, bf16[128,2048]{1,0:T(8,128)(2,1)S(1)}, u32[]{:S(2)}, u32[]{:S(2)}) collective-permute-start(bf16[128,2048]{1,0:T(8,128)(2,1)} %get-tuple-element.13), channel_id=1, source_target_pairs={{0,1},{1,2},{2,3},{3,0},{4,5},{5,6},{6,7},{7,4},{8,9},{9,10},{10,1... | collective-permute-start | bytes 1572872 | tf_op jit(solution)/shard_map/ppermute | solution.py:345
  6.4 18.0 %all-to-all-start = ((bf16[32,16,128]{2,1,0:T(8,128)(2,1)}), bf16[32,16,128]{2,1,0:T(8,128)(2,1)S(1)}, u32[]{:S(2)}, u32[]{:S(2)}) async-start(bf16[32,16,128]{2,1,0:T(8,128)(2,1)} %get-tuple-element.12), calls=%async_computation | async-start | bytes 262144 | tf_op jit(solution)/shard_map/all_to_all | solution.py:358
  16.3 14.0 %collective-permute-start.1 = (bf16[64,2048]{1,0:T(8,128)(2,1)}, bf16[64,2048]{1,0:T(8,128)(2,1)S(1)}, u32[]{:S(2)}, u32[]{:S(2)}) collective-permute-start(bf16[64,2048]{1,0:T(8,128)(2,1)} %get-tuple-element.14), channel_id=1, source_target_pairs={{0,2},{1,3},{2,0},{3,1},{4,6},{5,7},{6,4},{7,5},{8,10},{9,11},{10,... | collective-permute-start | bytes 786440 | tf_op jit(solution)/shard_map/ppermute | solution.py:355
  25.4 13.9 %all-to-all-start.1 = ((bf16[4,64,128]{2,1,0:T(8,128)(2,1)}), bf16[4,64,128]{2,1,0:T(8,128)(2,1)S(1)}, u32[]{:S(2)}, u32[]{:S(2)}) async-start(bf16[4,64,128]{2,1,0:T(8,128)(2,1)} %shrink.1), calls=%async_computation.1 | async-start | bytes 131072 | tf_op jit(solution)/shard_map/all_to_all | solution.py:361
  30.4 8.5 %copy-start = (bf16[128,8192]{1,0:T(8,128)(2,1)S(1)}, bf16[128,8192]{1,0:T(8,128)(2,1)}, u32[]{:S(2)}) copy-start(bf16[128,8192]{1,0:T(8,128)(2,1)} %weight_ref.1) | copy-start | bytes 6291460
  30.4 8.4 %collective-permute-start.2 = (bf16[192,2048]{1,0:T(8,128)(2,1)S(1)}, bf16[192,2048]{1,0:T(8,128)(2,1)S(1)}, u32[]{:S(2)}, u32[]{:S(2)}) collective-permute-start(bf16[192,2048]{1,0:T(8,128)(2,1)S(1)} %pad_maximum_fusion.held_ref), channel_id=1, source_target_pairs={{0,32},{32,0},{64,96},{96,64},{128,160},{160,128},{192,224},{224,1... | collective-permute-start | bytes 2359304 | tf_op jit(solution)/shard_map/ppermute | solution.py:363
  39.3 23.3 %copy-start.1 = (bf16[16,64,256]{2,1,0:T(8,128)(2,1)S(1)}, bf16[16,64,256]{2,1,0:T(8,128)(2,1)}, u32[]{:S(2)}) copy-start(bf16[16,64,256]{2,1,0:T(8,128)(2,1)} %up_ref.1) | copy-start | bytes 1572868
